TPU v7x, 32 devices: a whole 2x2x4 slice. The times are simulated.
32 devices in a mesh: groups: 2 (over y), pair: 8 (over z, x), virt: 2 (over core).
Axes of the slice: x: 2, y: 2, z: 4, core: 2. Of those that a mesh axis runs over, the one named last changes fastest.
Arguments:
- amp_tiles: bfloat16 [16, 16, 128, 128], P(('groups', 'pair'), 'virt'), parts along dimension 0, may hold values from -6 to 6
- tile_coords: int32 [16, 16, 2], P(('groups', 'pair')), parts along dimension 0, may hold values from 0 to 11, as said below
- tile_mask: int32 [16, 16], P(('groups', 'pair')), parts along dimension 0, may hold values 0 or 1
- pair_orbs: int32 [16, 2], P(('groups', 'pair')), parts along dimension 0, may hold values from 0 to 7, as said below
- ladder_factor: bfloat16 [4, 1536, 1536], P(('groups', 'virt')), parts along dimension 0, may hold values from -0.25 to 0.25
- cycle_factor: bfloat16 [16, 1536, 128], P('groups'), parts along dimension 0, may hold values from -0.1875 to 0.1875
Outputs:
- residual: bfloat16 [16, 1536, 1536], P(('groups', 'pair'), 'virt'), parts along dimension 0
There are 2 independent parts, one for each index of `groups`. A program takes and returns all parts, laid end to end along the dimension named above; each array names one. Nothing has to cross between parts.
Inputs may be any that keep to these rules, and one draw needn't show every extreme that they name: `tile_coords`: row k of a pair holds the c tile and the d tile of slot k; the 16 slots of one pair name different tile pairs. `pair_orbs`: column 0 is i, column 1 is j; no two pairs are equal; pair p and pair p + 4 have the same j.
All inputs are finite; a program needn't handle non-finite values. No bound on the sum of `tile_mask` on one device may be relied on, other than what follows from the above.
Results may differ from a plain program's by a relative error of at most 0.0051.
Values may be sent and summed in bfloat16 or wider, within the bound.
No kernel may reach another device: no remote copies, remote signals or barrier semaphores. Data moves between devices by JAX's collectives and lax.ppermute only.
A program may use at most 128 MiB of HBM per device.

v0:
```python
import jax
import jax.numpy as jnp
from jax import lax
from jax.sharding import PartitionSpec as P


def tile_products(selected_tiles, coords, factor_now, row_block):
    full_width = factor_now.shape[0]
    tile_size = selected_tiles.shape[1]
    tile_count = full_width // tile_size
    blocks = factor_now.reshape(full_width, tile_count, tile_size)
    trailing_columns = jnp.take(blocks, coords[:, 1], axis=1)
    contraction_block = jnp.einsum(
        "ozg,tog->ozt", selected_tiles, trailing_columns, preferred_element_type=jnp.float32
    ).astype(jnp.bfloat16)
    row_total = row_block.shape[0]
    left_cols = jnp.take(
        row_block.reshape(row_total, tile_count, tile_size), coords[:, 0], axis=1
    ).reshape(row_total, -1)
    return (left_cols, contraction_block.reshape(-1, full_width))


def shards(amp_tiles, tile_coords, tile_mask, pair_orbs, ladder_factor, cycle_factor):
    core_count = lax.axis_size("virt")
    core_index = lax.axis_index("virt")
    local_count = amp_tiles.shape[1]
    tile_size = amp_tiles.shape[2]
    full_width = ladder_factor.shape[1]
    tile_count = full_width // tile_size
    half_rows = full_width // core_count
    occ_count = cycle_factor.shape[0]
    aux_count = cycle_factor.shape[2]
    first_slot = core_index * local_count
    own_coords = lax.dynamic_slice_in_dim(tile_coords[0], first_slot, local_count, 0)
    own_mask = lax.dynamic_slice_in_dim(tile_mask[0], first_slot, local_count, 0)
    resident_tiles = amp_tiles[0] * own_mask.astype(jnp.bfloat16)[:, None, None]
    left_orbital = pair_orbs[0, 0]
    right_orbital = pair_orbs[0, 1]
    cycle_rows = lax.dynamic_index_in_dim(cycle_factor, left_orbital, 0, keepdims=False)
    cycle_cols = jnp.take(
        cycle_rows.reshape(tile_count, tile_size, aux_count), own_coords[:, 0], axis=0
    )
    intermediate_terms = jnp.einsum(
        "kcq,kcd->kqd", cycle_cols, resident_tiles, preferred_element_type=jnp.float32
    )
    placed = (own_coords[:, 1][:, None] == jnp.arange(tile_count, dtype=jnp.int32)[None, :]).astype(
        jnp.float32
    )
    distribute_tiles = jnp.einsum("kn,kqd->qnd", placed, intermediate_terms).reshape(
        aux_count, full_width
    )
    chosen = (jnp.arange(occ_count, dtype=jnp.int32) == right_orbital).astype(jnp.float32)
    cycle_sums = lax.psum(chosen[:, None, None] * distribute_tiles[None], ("pair", "virt"))
    cycle_low = lax.dynamic_index_in_dim(cycle_sums, right_orbital, 0, keepdims=False).astype(
        jnp.bfloat16
    )
    leading_row_offset = core_index * half_rows
    cycle_term = jnp.dot(
        lax.dynamic_slice_in_dim(cycle_rows, leading_row_offset, half_rows, 0),
        cycle_low,
        preferred_element_type=jnp.float32,
    )
    selected_tiles = lax.all_gather(resident_tiles, "virt", axis=0, tiled=True)
    all_coords = tile_coords[0]
    products = tile_products(selected_tiles, all_coords, ladder_factor[0], ladder_factor[0])
    left_cols, contraction_block = products
    total = jnp.dot(left_cols, contraction_block, preferred_element_type=jnp.float32)
    ladder = lax.psum_scatter(total, "virt", scatter_dimension=0, tiled=True)
    return (ladder + cycle_term).astype(jnp.bfloat16)[None]


def solution(mesh):
    in_specs = (
        P(("groups", "pair"), "virt", None, None),
        P(("groups", "pair"), None, None),
        P(("groups", "pair"), None),
        P(("groups", "pair"), None),
        P(("groups", "virt"), None, None),
        P("groups", None, None),
    )
    out_specs = P(("groups", "pair"), "virt", None)
    return jax.shard_map(shards, mesh=mesh, in_specs=in_specs, out_specs=out_specs, check_vma=False)
```

profile of v0, /device:TPU:0, one launch (start us, length us, event | category | flops | bytes accessed | tf_op | source)
XLA Modules:
  0.0 227.5 jit_solution(11092970389107840639)
XLA Ops:
  6.5 0.0 copy-start
  6.5 0.0 reduce-scatter.2.cloned.1.call-start
  6.5 6.8 %copy.18 = bf16[1,1536,1536]{1,2,0:T(8,128)(2,1)} copy(bf16[1,1536,1536]{2,1,0:T(8,128)(2,1)} %param.12) | data formatting | bytes 9437184 | tf_op args[4]
  13.4 0.0 copy-start.1
  13.4 0.0 copy-start.3
  13.4 6.7 %copy.19 = bf16[1536,12,128]{2,0,1:T(8,128)(2,1)} copy(bf16[1536,12,128]{0,2,1:T(8,128)(2,1)} %bitcast.51) | data formatting | bytes 9437184 | tf_op jit(solution)/shard_map/reshape;squeeze | solution.py:18
  20.0 0.0 copy-done.1
  20.1 0.0 copy-done.3
  20.1 0.1 fusion.30
  20.2 1.0 bitcast_multiply_fusion
  21.2 2.4 %all_gather.3 = bf16[16,128,128]{2,1,0:T(8,128)(2,1)} all-gather(bf16[8,128,128]{2,1,0:T(8,128)(2,1)S(1)} %bitcast_multiply_fusion), channel_id=1, replica_groups=mesh['groups'=2,'pair'=8,'virt'=2] {'virt'}, dimensions={0}, use_global_device_ids=true | all-gather | bytes 786432 | tf_op jit(solution)/shard_map/all_gather | solution.py:63
  23.6 6.4 %gather_fusion.1 = bf16[16,1536,128]{2,1,0:T(8,128)(2,1)} fusion(bf16[1536,12,128]{2,0,1:T(8,128)(2,1)} %copy.19, s32[1024]{0:T(1024)S(1)} %get-tuple-element.17), kind=kCustom, calls=%fused_computation.clone | custom fusion | bytes 12582976 | tf_op jit(solution)/shard_map/jit(_take)/gather | solution.py:17
  30.0 6.3 %gather_fusion.2 = bf16[16,1536,128]{2,1,0:T(8,128)(2,1)} fusion(bf16[1536,12,128]{2,0,1:T(8,128)(2,1)} %copy.19, s32[1024]{0:T(1024)S(1)} %get-tuple-element.16), kind=kCustom, calls=%fused_computation.1.clone | custom fusion | bytes 12582976 | tf_op jit(solution)/shard_map/jit(_take)/gather | solution.py:12
  36.3 18.2 %convolution_bitcast_fusion = f32[1536,1536]{1,0:T(8,128)} fusion(bf16[16,1536,128]{2,1,0:T(8,128)(2,1)} %gather_fusion.1, pred[16]{0:T(512)(128)(4,1)S(1)} %get-tuple-element.12, bf16[16,128,128]{2,1,0:T(8,128)(2,1)} %all_gather.3, bf16[16,1536,128]{2,1,0:T(8,128)(2,1)} %gather_fusion.2, pred[16]{0:T(512)(128)(4,1)S(1)} %get-tuple-element.6), kind=kOutput, calls=%fused_computation.3 | convolution fusion | flops 10478419968 | bytes 22544416 | tf_op jit(solution)/shard_map/dot_general | solution.py:67
  54.5 0.0 copy-start.2
  54.5 0.0 reduce-scatter.2.cloned.1.call-update
  54.5 0.6 copy-done.2
  55.2 0.6 fusion.35
  58.8 0.1 fusion.28
  58.9 0.0 copy-done
  58.9 0.8 constant_dynamic-slice_fusion
  59.7 2.3 gather_fusion
  62.0 1.3 fusion.18
  63.3 1.4 convolution_bitcast_fusion.1
  64.7 2.5 %copy.23 = f32[128,12,128]{0,2,1:T(8,128)} copy(f32[128,12,128]{2,1,0:T(8,128)} %convolution_bitcast_fusion.1) | data formatting | bytes 1572864 | tf_op jit(solution)/shard_map/kn,kqd->qnd/transpose | solution.py:49
  67.2 2.4 %copy.24 = f32[128,1536]{1,0:T(8,128)} copy(f32[128,1536]{0,1:T(8,128)} %bitcast.52) | data formatting | bytes 1572864 | tf_op jit(solution)/shard_map/mul | solution.py:53
  69.6 0.6 compare_convert_fusion
  70.1 4.9 %broadcast_multiply_fusion = f32[8,128,1536]{2,1,0:T(8,128)} fusion(f32[128,1536]{1,0:T(8,128)} %copy.24, f32[8]{0:T(128)S(1)} %compare_convert_fusion), kind=kLoop, calls=%fused_computation.15 | loop fusion | flops 1572864 | bytes 7077920 | tf_op jit(solution)/shard_map/mul | solution.py:53
  75.6 140.4 %all-reduce.1 = bf16[8,128,1536]{2,1,0:T(8,128)(2,1)} all-reduce(f32[8,128,1536]{2,1,0:T(8,128)} %broadcast_multiply_fusion), channel_id=1, replica_groups=mesh['groups'=2,'pair'=8,'virt'=2] {'pair','virt'}, use_global_device_ids=true, to_apply=%region_1.3 | all-reduce | flops 1572864 | bytes 9437184 | tf_op jit(solution)/shard_map/psum | solution.py:53
  216.0 0.0 reduce-scatter.2.cloned.1.call-done
  216.0 4.6 %fusion.14 = bf16[1,768,1536]{2,1,0:T(8,128)(2,1)} fusion(f32[768,1536]{1,0:T(8,128)} %reduce-scatter.2.cloned.1.call-done, bf16[8,128,1536]{2,1,0:T(8,128)(2,1)} %all-reduce.1, s32[]{:T(128)S(6)} %select_n.44, bf16[8,1536,128]{2,1,0:T(8,128)(2,1)S(1)} %copy-done, s32[]{:T(128)S(6)} %select_n.39, s32[]{:T(128)S(6)} %select_n.41), kind=kOutput, calls=%fused_computation.16 | convolution fusion | flops 304349184 | bytes 7667724 | tf_op jit(solution)/shard_map/dot_general | solution.py:58
  (5 shorter events, 0.0 us)
Async XLA Ops:
  6.5 52.4 %copy-start = (bf16[8,1536,128]{2,1,0:T(8,128)(2,1)S(1)}, bf16[8,1536,128]{2,1,0:T(8,128)(2,1)}, u32[]{:S(2)}) copy-start(bf16[8,1536,128]{2,1,0:T(8,128)(2,1)} %param.13) | copy-start | bytes 9437188
  6.5 209.5 %reduce-scatter.2.cloned.1.call-start = ((), (), s32[]{:S(2)}) async-start(), calls=%async_computation.1 | async-start | bytes 14155776 | tf_op jit(solution)/shard_map/reduce_scatter | solution.py:68
  13.4 6.7 %copy-start.1 = (s32[1,16,2]{1,2,0:T(2,128)S(1)}, s32[1,16,2]{1,2,0:T(2,128)}, u32[]{:S(2)}) copy-start(s32[1,16,2]{1,2,0:T(2,128)} %param.9) | copy-start | bytes 388
  13.4 6.7 %copy-start.3 = (s32[1,16]{1,0:T(1,128)S(1)}, s32[1,16]{1,0:T(1,128)}, u32[]{:S(2)}) copy-start(s32[1,16]{1,0:T(1,128)} %param.10) | copy-start | bytes 196
  54.5 0.7 copy-start.2
Sparse Core Ops, SparseCore 0:
  54.7 20.4 reduce-scatter.1
where the time goes:
time: 230 us; the launch traced here: 228 us
  blocking collectives  143 us (62%)
  local copies, waits for them, and re-layouts  35.4 us (15%)
  matrix products  25.6 us (11%)
  between operations  17.1 us (7%)
  other arithmetic  6.64 us (3%)
    psum x1, blocking collectives, shards(): lax.psum(chosen[:, None, None] * distribute_tiles[None], ('pair', 'virt'))  140 us
    dot_general x1, matrix products, shards(): jnp.dot(left_cols, contraction_block, preferred_element_type=jnp.float32)  18.2 us
    unnamed x9, local copies, waits for them, and re-layouts  7.48 us
    another operation x1, local copies, waits for them, and re-layouts, tile_products(): row_block.reshape(row_total, tile_count, tile_size)  6.66 us
    gather x1, local copies, waits for them, and re-layouts, tile_products(): jnp.take(row_block.reshape(row_total, tile_count, tile_size), coords[:, 0...  6.37 us
    gather x1, local copies, waits for them, and re-layouts, tile_products(): trailing_columns = jnp.take(blocks, coords[:, 1], axis=1)  6.3 us
    mul x1, other arithmetic, shards(): chosen[:, None, None] * distribute_tiles[None]  4.92 us
    dot_general x1, matrix products, shards(): jnp.dot(lax.dynamic_slice_in_dim(cycle_rows, leading_row_offset, half_row...  4.63 us
  transfers between devices with their start and end apart: 1, of which 0 were waited for; matrix products, arithmetic and copies ran while one was open for 7% of the time, Pallas kernels for 0%

commit v1 on v0

v1 whole, which is shorter than its diff:
```python
import functools

import jax
import jax.numpy as jnp
from jax import lax
from jax.experimental import pallas as pl
from jax.experimental.pallas import tpu as pltpu
from jax.sharding import PartitionSpec as P

LANES = 128
SMEM = pl.BlockSpec(memory_space=pltpu.SMEM)
VMEM = pl.BlockSpec(memory_space=pltpu.VMEM)
ANY = pl.BlockSpec(memory_space=pl.ANY)
FIRST_FIRST = (((0,), (0,)), ((), ()))
LAST_LAST = (((1,), (1,)), ((), ()))


def params(mib):
    return pltpu.CompilerParams(vmem_limit_bytes=mib * 2**20)


def block(index, size):
    return pl.ds(pl.multiple_of(index * size, size), size)


def intermediate(coords, mask, orbs, place, own, other, cycle_factor, *, cores):
    slots = coords.shape[0]
    local, tile = own.shape[0], own.shape[1]
    width, aux = cycle_factor.shape[1:]
    share = aux // cores
    part = share // 2

    def body(coords, mask, orbs, place, own, other, factor, first, second, rows, total, sem):
        load = pltpu.make_async_copy(factor.at[orbs[0]], rows, sem)
        load.start()
        core = place[0]
        total[...] = jnp.zeros_like(total)
        load.wait()
        terms = []
        for s in range(slots):
            g = lax.rem(s + core * local, slots)
            held = own[s] if s < local else other[s - local]
            term = lax.dot_general(
                rows[block(coords[g, 0], tile), :], held, FIRST_FIRST,
                preferred_element_type=jnp.float32,
            )
            terms.append((g, term))
        for g, term in terms:
            total[:, block(coords[g, 1], tile)] += term * mask[g].astype(jnp.float32)
        first[...] = total[block(2 * core, part), :].astype(first.dtype)
        second[:, :width] = total[block(2 * core + 1, part), :].astype(second.dtype)
        label = jnp.zeros((part, LANES), jnp.float32) + orbs[1].astype(jnp.float32)
        second[:, width:] = label.astype(second.dtype)

    return pl.pallas_call(
        body,
        out_shape=[
            jax.ShapeDtypeStruct((part, width), jnp.bfloat16),
            jax.ShapeDtypeStruct((part, width + LANES), jnp.bfloat16),
        ],
        in_specs=[SMEM, SMEM, SMEM, SMEM, VMEM, VMEM, ANY],
        out_specs=[VMEM, VMEM],
        scratch_shapes=[
            pltpu.VMEM((width, aux), jnp.bfloat16),
            pltpu.VMEM((aux, width), jnp.float32),
            pltpu.SemaphoreType.DMA,
        ],
        compiler_params=params(16),
        name="intermediate",
    )(coords, mask, orbs, place, own, other, cycle_factor)


def same_orbital(mine, theirs, width):
    return (mine[:, width : width + 1] == theirs[:, width : width + 1]).astype(jnp.float32)


def sum_middle(first, first_far, second, second_near):
    width = first.shape[1]

    def body(first, first_far, second, *refs):
        near, (first_out, second_out) = refs[:-2], refs[-2:]
        first_out[...] = (first[...].astype(jnp.float32) + first_far[...].astype(jnp.float32)).astype(jnp.bfloat16)
        total = second[:, :width].astype(jnp.float32)
        for theirs in near:
            weight = same_orbital(second[...].astype(jnp.float32), theirs[...].astype(jnp.float32), width)
            total += weight * theirs[:, :width].astype(jnp.float32)
        second_out[...] = total.astype(jnp.bfloat16)

    return pl.pallas_call(
        body,
        out_shape=[jax.ShapeDtypeStruct(first.shape, jnp.bfloat16)] * 2,
        in_specs=[VMEM] * (3 + len(second_near)),
        out_specs=[VMEM, VMEM],
        compiler_params=params(16),
        name="sum_middle",
    )(first, first_far, second, *second_near)


def sum_last(second, second_near, first_sum, first_sum_near, second_sum, second_sum_far):
    part, width = first_sum.shape
    count = len(second_near)

    def body(*refs):
        second, near = refs[0], refs[1 : 1 + count]
        first, first_near = refs[1 + count], refs[2 + count : 2 + 2 * count]
        second_sum, second_far, out = refs[2 + 2 * count :]
        total = first[...].astype(jnp.float32)
        for theirs, value in zip(near, first_near):
            weight = same_orbital(second[...].astype(jnp.float32), theirs[...].astype(jnp.float32), width)
            total += weight * value[...].astype(jnp.float32)
        out[:part, :] = total.astype(jnp.bfloat16)
        out[part:, :] = (second_sum[...].astype(jnp.float32) + second_far[...].astype(jnp.float32)).astype(jnp.bfloat16)

    return pl.pallas_call(
        body,
        out_shape=jax.ShapeDtypeStruct((2 * part, width), jnp.bfloat16),
        in_specs=[VMEM] * (4 + 2 * count),
        out_specs=VMEM,
        compiler_params=params(16),
        name="sum_last",
    )(second, *second_near, first_sum, *first_sum_near, second_sum, second_sum_far)


def ladder(coords, mask, place, own, other, factor, *, far, out_dtype):
    slots = coords.shape[0]
    local, tile = own.shape[0], own.shape[1]
    width = factor.shape[0]
    half = width // 2
    tiles = width // tile
    span = 2 * tile

    def body(coords, mask, place, own, other, factor, out, left, wide, held, head, link, names, starts):
        core = place[0]
        rows = block(1 - core if far else core, half)
        held[:local] = own[...]
        held[local:] = other[...]

        def clear(n, carry):
            head[n] = -1
            return carry

        lax.fori_loop(0, tiles, clear, 0)

        def put(s, carry):
            g = lax.rem(s + core * local, slots)
            d = coords[g, 1]

            @pl.when(mask[g] != 0)
            def _():
                link[s] = head[d]
                head[d] = s

            return carry

        lax.fori_loop(0, slots, put, 0)

        def name(n, count):
            names[count] = n
            starts[count] = head[n]
            return count + (head[n] >= 0).astype(jnp.int32)

        found = lax.fori_loop(0, tiles, name, jnp.int32(0))

        def columns(s):
            return block(coords[lax.rem(s + core * local, slots), 0], tile)

        def two_slots(s):
            t = link[s]
            there = t >= 0
            t = jnp.maximum(t, 0)
            a = jnp.concatenate([factor[rows, columns(s)], factor[rows, columns(t)]], axis=1)
            b = jnp.concatenate([held[s], jnp.where(there, held[t], jnp.zeros_like(held[t]))], axis=0)
            return jnp.dot(a, b, preferred_element_type=jnp.float32), jnp.where(there, link[t], -1)

        def one_tile(w, carry):
            s = starts[w]
            t = link[s]
            more = jnp.where(t >= 0, link[jnp.maximum(t, 0)], -1)
            here = block(w, tile)

            @pl.when(more < 0)
            def _():
                left[:, here] = two_slots(s)[0].astype(left.dtype)

            @pl.when(more >= 0)
            def _():
                value, after = two_slots(s)
                wide[...] = value

                def add(s):
                    value, after = two_slots(s)
                    wide[...] += value
                    return after

                lax.while_loop(lambda s: s >= 0, add, after)
                left[:, here] = wide[...].astype(left.dtype)

            return carry

        lax.fori_loop(0, found, one_tile, 0)

        @pl.when(lax.rem(found, 2) == 1)
        def _():
            left[:, block(found, tile)] = jnp.zeros((half, tile), left.dtype)
            names[found] = 0

        steps = (found + 1) // 2
        for n in range(1, tiles // 2 + 1):

            @pl.when(steps == n)
            def _():
                def piece(j, carry):
                    here = block(j, half)
                    right = jnp.concatenate(
                        [factor[here, block(names[u], tile)] for u in range(2 * n)], axis=1
                    )
                    value = lax.dot_general(
                        left[:, : n * span], right, LAST_LAST, preferred_element_type=jnp.float32
                    )
                    out[:, here] = value.astype(out.dtype)
                    return carry

                lax.fori_loop(0, width // half, piece, 0)

        @pl.when(steps == 0)
        def _():
            out[...] = jnp.zeros(out.shape, out.dtype)

    return pl.pallas_call(
        body,
        out_shape=jax.ShapeDtypeStruct((half, width), out_dtype),
        in_specs=[SMEM, SMEM, SMEM, VMEM, VMEM, VMEM],
        out_specs=VMEM,
        scratch_shapes=[
            pltpu.VMEM((half, tiles * tile), jnp.bfloat16),
            pltpu.VMEM((half, tile), jnp.float32),
            pltpu.VMEM((slots, tile, tile), jnp.bfloat16),
            pltpu.SMEM((tiles,), jnp.int32),
            pltpu.SMEM((slots,), jnp.int32),
            pltpu.SMEM((tiles + 1,), jnp.int32),
            pltpu.SMEM((tiles + 1,), jnp.int32),
        ],
        compiler_params=params(32),
        cost_estimate=pl.CostEstimate(
            flops=2 * half * width * width, bytes_accessed=2 * width * width, transcendentals=0
        ),
        name="ladder_far" if far else "ladder_near",
    )(coords, mask, place, own, other, factor)


def finish(orbs, place, sums, other_sums, near, arrived, cycle_factor, *, pieces):
    half, width = near.shape
    aux = cycle_factor.shape[2]
    share = sums.shape[0]
    rows = half // pieces

    def body(orbs, place, sums, other_sums, near, arrived, cycle_factor, out, low, factor, sem):
        step = pl.program_id(0)

        @pl.when(step == 0)
        def _():
            load = pltpu.make_async_copy(cycle_factor.at[orbs[0], block(place[0], half)], factor, sem)
            load.start()
            low[block(place[0], share), :] = sums[...]
            low[block(1 - place[0], share), :] = other_sums[...]
            load.wait()

        term = jnp.dot(factor[block(step, rows), :], low[...], preferred_element_type=jnp.float32)
        out[...] = (near[...].astype(jnp.float32) + arrived[...].astype(jnp.float32) + term).astype(out.dtype)

    piece = pl.BlockSpec((rows, width), lambda step: (step, 0))
    return pl.pallas_call(
        body,
        out_shape=jax.ShapeDtypeStruct((half, width), jnp.bfloat16),
        grid=(pieces,),
        in_specs=[SMEM, SMEM, VMEM, VMEM, piece, piece, ANY],
        out_specs=piece,
        scratch_shapes=[
            pltpu.VMEM((aux, width), jnp.bfloat16),
            pltpu.VMEM((half, aux), jnp.bfloat16),
            pltpu.SemaphoreType.DMA,
        ],
        compiler_params=params(32),
        name="finish",
    )(orbs, place, sums, other_sums, near, arrived, cycle_factor)


def shards(amp_tiles, tile_coords, tile_mask, pair_orbs, ladder_factor, cycle_factor):
    cores, pairs = lax.axis_size("virt"), lax.axis_size("pair")
    assert cores == 2 and pairs % 2 == 0
    own = amp_tiles[0]
    coords, mask, orbs = tile_coords[0], tile_mask[0], pair_orbs[0]
    place = lax.axis_index("virt").astype(jnp.int32).reshape(1)
    swap = [(0, 1), (1, 0)]
    other = lax.ppermute(own, "virt", swap)
    first, second = intermediate(coords, mask, orbs, place, own, other, cycle_factor, cores=cores)

    classes = pairs // 2
    far = [(p, (p + classes) % pairs) for p in range(pairs)]

    def shifts(value):
        return [
            lax.ppermute(
                value, "pair", [(p, p // classes * classes + (p + k) % classes) for p in range(pairs)]
            )
            for k in range(1, classes)
        ]

    if classes <= 4:
        first_far = lax.ppermute(first, "pair", far)
        second_near = shifts(second)
        first_sum, second_sum = sum_middle(first, first_far, second, second_near)
        second_sum_far = lax.ppermute(second_sum, "pair", far)
        sums = sum_last(second, second_near, first_sum, shifts(first_sum), second_sum, second_sum_far)
    else:
        width = first.shape[1]
        occupied = jnp.arange(cycle_factor.shape[0], dtype=jnp.int32) == orbs[1]
        mine = jnp.concatenate([first, second[:, :width]], axis=0).astype(jnp.float32)
        total = lax.psum(jnp.where(occupied[:, None, None], mine[None], 0.0), "pair")
        sums = lax.dynamic_index_in_dim(total, orbs[1], 0, keepdims=False).astype(jnp.bfloat16)

    factor = ladder_factor[0]
    outgoing = ladder(coords, mask, place, own, other, factor, far=True, out_dtype=jnp.bfloat16)
    arrived = lax.ppermute(outgoing, "virt", swap)
    near = ladder(coords, mask, place, own, other, factor, far=False, out_dtype=jnp.float32)
    other_sums = lax.ppermute(sums, "virt", swap)
    return finish(orbs, place, sums, other_sums, near, arrived, cycle_factor, pieces=4)[None]


def solution(mesh):
    in_specs = (
        P(("groups", "pair"), "virt", None, None),
        P(("groups", "pair"), None, None),
        P(("groups", "pair"), None),
        P(("groups", "pair"), None),
        P(("groups", "virt"), None, None),
        P("groups", None, None),
    )
    out_specs = P(("groups", "pair"), "virt", None)
    return jax.shard_map(shards, mesh=mesh, in_specs=in_specs, out_specs=out_specs, check_vma=False)
```

time: 230 us -> 49.1 us (0.21)
  blocking collectives: 143 us -> 0 us
  local copies, waits for them, and re-layouts: 35.4 us -> 4.7 us
  matrix products: 25.6 us -> 0 us
  Pallas kernels: 0 us -> 18.9 us
  between operations: 17.1 us -> 0.23 us
  starting transfers between devices: 0.01 us -> 13.9 us
  waiting for transfers between devices: 0.02 us -> 10.5 us
  other arithmetic: 6.64 us -> 0 us
    psum x1 -> x0, blocking collectives: 140 us -> none  [shards(): lax.psum(chosen[:, None, None] * distribute_tiles[None], ('pair', 'virt'))]
    dot_general x4 -> x0, matrix products: 25.6 us -> none  [the longest x1 18.2 us: shards(): jnp.dot(left_cols, contraction_block, preferred_element_type=jnp.float32)]
    pallas_call x0 -> x6, Pallas kernels: none -> 18.9 us  [the longest x2 13.8 us: ladder(): pl.pallas_call(body, out_shape=jax.ShapeDtypeStruct((half, width), out_dt...]
    gather x3 -> x0, local copies, waits for them, and re-layouts: 14.9 us -> none  [the longest x1 6.37 us: tile_products(): jnp.take(row_block.reshape(row_total, tile_count, tile_size), coords[:, 0...]
    ppermute x0 -> x11, starting transfers between devices: none -> 13.9 us  [the longest x6 9.25 us: shifts(): lax.ppermute(value, 'pair', [(p, p // classes * classes + (p + k) % class...]
    ppermute x0 -> x11, waiting for transfers between devices: none -> 10.5 us  [the longest x6 5.1 us: shifts(): lax.ppermute(value, 'pair', [(p, p // classes * classes + (p + k) % class...]
    another operation x1 -> x0, local copies, waits for them, and re-layouts: 6.66 us -> none  [tile_products(): row_block.reshape(row_total, tile_count, tile_size)]
    mul x2 -> x0, other arithmetic: 5.95 us -> none  [the longest x1 4.92 us: shards(): chosen[:, None, None] * distribute_tiles[None]]
  transfers between devices with their start and end apart: 1 -> 11, of which waited for: 0 -> 8; matrix products, arithmetic and copies ran while one was open for 7% -> 2% of each run, Pallas kernels for 0% -> 18%
where the time goes in v1:
time: 49.1 us; the launch traced here: 48.3 us
  Pallas kernels  18.9 us (38%)
  starting transfers between devices  13.9 us (28%)
  waiting for transfers between devices  10.5 us (21%)
  local copies, waits for them, and re-layouts  4.7 us (10%)
    pallas_call x2, Pallas kernels, ladder(): pl.pallas_call(body, out_shape=jax.ShapeDtypeStruct((half, width), out_dt...  13.8 us
    ppermute x6, starting transfers between devices, shifts(): lax.ppermute(value, 'pair', [(p, p // classes * classes + (p + k) % class...  9.25 us
    ppermute x6, waiting for transfers between devices, shifts(): lax.ppermute(value, 'pair', [(p, p // classes * classes + (p + k) % class...  5.1 us
    unnamed x10, local copies, waits for them, and re-layouts  3.95 us
    ppermute x1, waiting for transfers between devices, shards(): first_far = lax.ppermute(first, 'pair', far)  3.89 us
    pallas_call x1, Pallas kernels, finish(): pl.pallas_call(body, out_shape=jax.ShapeDtypeStruct((half, width), jnp.bf...  3.47 us
    ppermute x1, starting transfers between devices, shards(): second_sum_far = lax.ppermute(second_sum, 'pair', far)  2.01 us
    ppermute x1, starting transfers between devices, shards(): first_far = lax.ppermute(first, 'pair', far)  1.68 us
  transfers between devices with their start and end apart: 11, of which 8 were waited for; matrix products, arithmetic and copies ran while one was open for 2% of the time, Pallas kernels for 18%

profile of v1, /device:TPU:0, one launch (start us, length us, event | category | flops | bytes accessed | tf_op | source)
XLA Modules:
  0.0 48.3 jit_solution(10304658252769071872)
XLA Ops:
  0.0 0.5 collective-permute-start
  0.5 0.8 %copy.7.coords = s32[16,2]{1,0:T(8,128)S(1)} copy(s32[16,2]{0,1:T(2,128)} %bitcast.18) | data formatting | bytes 256 | tf_op jit(solution)/shard_map/squeeze | solution.py:292
  1.2 0.6 %collective-permute-done.other = bf16[8,128,128]{2,1,0:T(8,128)(2,1)S(1)} collective-permute-done((bf16[8,128,128]{2,1,0:T(8,128)(2,1)}, bf16[8,128,128]{2,1,0:T(8,128)(2,1)S(1)}, u32[]{:S(2)}, u32[]{:S(2)}) %collective-permute-start) | collective-permute-done | bytes 262176 | tf_op jit(solution)/shard_map/ppermute | solution.py:295
  1.8 0.0 copy-start.1
  1.8 0.9 %copy-done.1 = bf16[1,8,128,128]{3,2,1,0:T(8,128)(2,1)S(1)} copy-done((bf16[1,8,128,128]{3,2,1,0:T(8,128)(2,1)S(1)}, bf16[1,8,128,128]{3,2,1,0:T(8,128)(2,1)}, u32[]{:S(2)}) %copy-start.1) | copy-done | bytes 262168
  2.8 0.0 copy-start.3
  2.8 0.7 %copy-done.3 = s32[1,16]{1,0:T(1,128)S(1)} copy-done((s32[1,16]{1,0:T(1,128)S(1)}, s32[1,16]{1,0:T(1,128)}, u32[]{:S(2)}) %copy-start.3) | copy-done | bytes 88
  3.4 0.0 copy-start.4
  3.4 2.3 %copy-done.4 = bf16[1,1536,1536]{2,1,0:T(8,128)(2,1)S(1)} copy-done((bf16[1,1536,1536]{2,1,0:T(8,128)(2,1)S(1)}, bf16[1,1536,1536]{2,1,0:T(8,128)(2,1)}, u32[]{:S(2)}) %copy-start.4) | copy-done | bytes 4718616
  5.8 0.0 copy-start
  5.8 0.0 copy-start.2
  5.8 6.8 %ladder_far.1 = bf16[768,1536]{1,0:T(8,128)(2,1)S(1)} custom-call(s32[16,2]{1,0:T(8,128)S(1)} %copy.7.coords, s32[16]{0:T(128)S(1)} %bitcast.13, s32[1]{0:T(128)} %bitcast.1.place, bf16[8,128,128]{2,1,0:T(8,128)(2,1)S(1)} %bitcast.8, bf16[8,128,128]{2,1,0:T(8,128)(2,1)S(1)} %collective-permute-done.other, bf16[1536,1536]{1,0:T(8,128)(2,1)S(1)} %bitcast.16), custom_call_target="tpu_custom_call" | custom-call | flops 3623878656 | bytes 4718592 | tf_op jit(solution)/shard_map/ladder_far/pallas_call | solution.py:229
  12.6 0.4 collective-permute-start.10
  13.0 0.0 copy-done
  13.0 0.0 copy-done.2
  13.0 1.3 %intermediate.1 = (bf16[32,1536]{1,0:T(8,128)(2,1)S(1)}, bf16[32,1664]{1,0:T(8,128)(2,1)S(1)}) custom-call(s32[16,2]{1,0:T(8,128)S(1)} %copy.7.coords, s32[16]{0:T(128)S(1)} %bitcast.14, s32[2]{0:T(128)S(1)} %bitcast.11, s32[1]{0:T(128)} %bitcast.1.place, bf16[8,128,128]{2,1,0:T(8,128)(2,1)S(1)} %bitcast.9, ...), custom_call_target="tpu_custom_call" | custom-call | tf_op jit(solution)/shard_map/intermediate/pallas_call | solution.py:55
  14.4 3.4 %collective-permute-start.3 = (bf16[32,1664]{1,0:T(8,128)(2,1)S(1)}, bf16[32,1664]{1,0:T(8,128)(2,1)S(1)}, u32[]{:S(2)}, u32[]{:S(2)}) collective-permute-start(bf16[32,1664]{1,0:T(8,128)(2,1)S(1)} %get-tuple-element.9.second.refs_0_), channel_id=1, source_target_pairs={{0,6},{2,0},{4,2},{6,4},{8,14},{10,8},{12,10},{14,12},{1,7},{3,1},... | collective-permute-start | bytes 319496 | tf_op jit(solution)/shard_map/ppermute | solution.py:303
  17.8 0.0 collective-permute-start.2
  17.8 1.9 %collective-permute-start.1 = (bf16[32,1664]{1,0:T(8,128)(2,1)S(1)}, bf16[32,1664]{1,0:T(8,128)(2,1)S(1)}, u32[]{:S(2)}, u32[]{:S(2)}) collective-permute-start(bf16[32,1664]{1,0:T(8,128)(2,1)S(1)} %get-tuple-element.9.second.refs_0_), channel_id=1, source_target_pairs={{0,2},{2,4},{4,6},{6,0},{8,10},{10,12},{12,14},{14,8},{1,3},{3,5},... | collective-permute-start | bytes 319496 | tf_op jit(solution)/shard_map/ppermute | solution.py:303
  19.8 1.7 %collective-permute-start.4 = (bf16[32,1536]{1,0:T(8,128)(2,1)S(1)}, bf16[32,1536]{1,0:T(8,128)(2,1)S(1)}, u32[]{:S(2)}, u32[]{:S(2)}) collective-permute-start(bf16[32,1536]{1,0:T(8,128)(2,1)S(1)} %get-tuple-element.10.first), channel_id=1, source_target_pairs={{0,8},{2,10},{4,12},{6,14},{8,0},{10,2},{12,4},{14,6},{1,9},{3,11}... | collective-permute-start | bytes 294920 | tf_op jit(solution)/shard_map/ppermute | solution.py:310
  21.5 3.9 %collective-permute-done.4.first_far = bf16[32,1536]{1,0:T(8,128)(2,1)S(1)} collective-permute-done((bf16[32,1536]{1,0:T(8,128)(2,1)S(1)}, bf16[32,1536]{1,0:T(8,128)(2,1)S(1)}, u32[]{:S(2)}, u32[]{:S(2)}) %collective-permute-start.4) | collective-permute-done | bytes 98336 | tf_op jit(solution)/shard_map/ppermute | solution.py:310
  25.4 0.0 collective-permute-done.3.refs_2_.refs_3_
  25.4 0.3 collective-permute-done.2.refs_1_.refs_2_
  25.6 0.8 %collective-permute-done.1.refs_0_.refs_1_ = bf16[32,1664]{1,0:T(8,128)(2,1)S(1)} collective-permute-done((bf16[32,1664]{1,0:T(8,128)(2,1)S(1)}, bf16[32,1664]{1,0:T(8,128)(2,1)S(1)}, u32[]{:S(2)}, u32[]{:S(2)}) %collective-permute-start.1) | collective-permute-done | bytes 106528 | tf_op jit(solution)/shard_map/ppermute | solution.py:303
  26.4 0.1 sum_middle.1
  26.6 2.0 %collective-permute-start.8 = (bf16[32,1536]{1,0:T(8,128)(2,1)S(1)}, bf16[32,1536]{1,0:T(8,128)(2,1)S(1)}, u32[]{:S(2)}, u32[]{:S(2)}) collective-permute-start(bf16[32,1536]{1,0:T(8,128)(2,1)S(1)} %get-tuple-element.12.refs_8_), channel_id=1, source_target_pairs={{0,8},{2,10},{4,12},{6,14},{8,0},{10,2},{12,4},{14,6},{1,9},{3,11}... | collective-permute-start | bytes 294920 | tf_op jit(solution)/shard_map/ppermute | solution.py:313
  28.6 3.3 %collective-permute-start.7 = (bf16[32,1536]{1,0:T(8,128)(2,1)S(1)}, bf16[32,1536]{1,0:T(8,128)(2,1)S(1)}, u32[]{:S(2)}, u32[]{:S(2)}) collective-permute-start(bf16[32,1536]{1,0:T(8,128)(2,1)S(1)} %get-tuple-element.11.refs_4_), channel_id=1, source_target_pairs={{0,6},{2,0},{4,2},{6,4},{8,14},{10,8},{12,10},{14,12},{1,7},{3,1},... | collective-permute-start | bytes 294920 | tf_op jit(solution)/shard_map/ppermute | solution.py:303
  31.8 0.0 collective-permute-start.6
  31.9 0.6 %collective-permute-start.5 = (bf16[32,1536]{1,0:T(8,128)(2,1)S(1)}, bf16[32,1536]{1,0:T(8,128)(2,1)S(1)}, u32[]{:S(2)}, u32[]{:S(2)}) collective-permute-start(bf16[32,1536]{1,0:T(8,128)(2,1)S(1)} %get-tuple-element.11.refs_4_), channel_id=1, source_target_pairs={{0,2},{2,4},{4,6},{6,0},{8,10},{10,12},{12,14},{14,8},{1,3},{3,5},... | collective-permute-start | bytes 294920 | tf_op jit(solution)/shard_map/ppermute | solution.py:303
  32.4 0.9 %collective-permute-done.8.refs_9_ = bf16[32,1536]{1,0:T(8,128)(2,1)S(1)} collective-permute-done((bf16[32,1536]{1,0:T(8,128)(2,1)S(1)}, bf16[32,1536]{1,0:T(8,128)(2,1)S(1)}, u32[]{:S(2)}, u32[]{:S(2)}) %collective-permute-start.8) | collective-permute-done | bytes 98336 | tf_op jit(solution)/shard_map/ppermute | solution.py:313
  33.3 0.8 %collective-permute-done.7.refs_7_ = bf16[32,1536]{1,0:T(8,128)(2,1)S(1)} collective-permute-done((bf16[32,1536]{1,0:T(8,128)(2,1)S(1)}, bf16[32,1536]{1,0:T(8,128)(2,1)S(1)}, u32[]{:S(2)}, u32[]{:S(2)}) %collective-permute-start.7) | collective-permute-done | bytes 98336 | tf_op jit(solution)/shard_map/ppermute | solution.py:303
  34.1 2.4 %collective-permute-done.6.refs_6_ = bf16[32,1536]{1,0:T(8,128)(2,1)S(1)} collective-permute-done((bf16[32,1536]{1,0:T(8,128)(2,1)S(1)}, bf16[32,1536]{1,0:T(8,128)(2,1)S(1)}, u32[]{:S(2)}, u32[]{:S(2)}) %collective-permute-start.6) | collective-permute-done | bytes 98336 | tf_op jit(solution)/shard_map/ppermute | solution.py:303
  36.5 0.9 %collective-permute-done.5.refs_5_ = bf16[32,1536]{1,0:T(8,128)(2,1)S(1)} collective-permute-done((bf16[32,1536]{1,0:T(8,128)(2,1)S(1)}, bf16[32,1536]{1,0:T(8,128)(2,1)S(1)}, u32[]{:S(2)}, u32[]{:S(2)}) %collective-permute-start.5) | collective-permute-done | bytes 98336 | tf_op jit(solution)/shard_map/ppermute | solution.py:303
  37.4 0.1 sum_last.1.sums
  37.5 0.1 collective-permute-start.9
  37.6 7.0 %ladder_near.1.near = f32[768,1536]{1,0:T(8,128)S(1)} custom-call(s32[16,2]{1,0:T(8,128)S(1)} %copy.7.coords, s32[16]{0:T(128)S(1)} %bitcast.15, s32[1]{0:T(128)} %bitcast.1.place, bf16[8,128,128]{2,1,0:T(8,128)(2,1)S(1)} %bitcast.10, bf16[8,128,128]{2,1,0:T(8,128)(2,1)S(1)} %collective-permute-done.other, bf16[1536,1536]{1,0:T(8,128)(2,1)S(1)} %bitcast.17), custom_call_target="tpu_custom_call" | custom-call | flops 3623878656 | bytes 4718592 | tf_op jit(solution)/shard_map/ladder_near/pallas_call | solution.py:229
  44.6 0.0 collective-permute-done.9.other_sums
  44.6 0.0 collective-permute-done.10.arrived
  44.6 3.5 %finish.1 = bf16[768,1536]{1,0:T(8,128)(2,1)} custom-call(s32[2]{0:T(128)S(1)} %bitcast.12, s32[1]{0:T(128)} %bitcast.1.place, bf16[64,1536]{1,0:T(8,128)(2,1)S(1)} %sum_last.1.sums, bf16[64,1536]{1,0:T(8,128)(2,1)S(1)} %collective-permute-done.9.other_sums, f32[768,1536]{1,0:T(8,128)S(1)} %ladder_near.1.near, ...), custom_call_target="tpu_custom_call" | custom-call | tf_op jit(solution)/shard_map/finish/pallas_call | solution.py:272
Async XLA Ops:
  0.0 1.8 %collective-permute-start = (bf16[8,128,128]{2,1,0:T(8,128)(2,1)}, bf16[8,128,128]{2,1,0:T(8,128)(2,1)S(1)}, u32[]{:S(2)}, u32[]{:S(2)}) collective-permute-start(bf16[8,128,128]{2,1,0:T(8,128)(2,1)} %bitcast.7), channel_id=1, source_target_pairs={{0,1},{1,0},{2,3},{3,2},{4,5},{5,4},{6,7},{7,6},{8,9},{9,8},{10,11... | collective-permute-start | bytes 786440 | tf_op jit(solution)/shard_map/ppermute | solution.py:295
  1.8 0.9 %copy-start.1 = (bf16[1,8,128,128]{3,2,1,0:T(8,128)(2,1)S(1)}, bf16[1,8,128,128]{3,2,1,0:T(8,128)(2,1)}, u32[]{:S(2)}) copy-start(bf16[1,8,128,128]{3,2,1,0:T(8,128)(2,1)} %param.6) | copy-start | bytes 786436
  2.8 0.7 %copy-start.3 = (s32[1,16]{1,0:T(1,128)S(1)}, s32[1,16]{1,0:T(1,128)}, u32[]{:S(2)}) copy-start(s32[1,16]{1,0:T(1,128)} %param.8) | copy-start | bytes 196
  3.4 2.3 %copy-start.4 = (bf16[1,1536,1536]{2,1,0:T(8,128)(2,1)S(1)}, bf16[1,1536,1536]{2,1,0:T(8,128)(2,1)}, u32[]{:S(2)}) copy-start(bf16[1,1536,1536]{2,1,0:T(8,128)(2,1)} %param.10) | copy-start | bytes 14155780
  5.8 7.3 %copy-start = (bf16[8,1536,128]{2,1,0:T(8,128)(2,1)S(1)}, bf16[8,1536,128]{2,1,0:T(8,128)(2,1)}, u32[]{:S(2)}) copy-start(bf16[8,1536,128]{2,1,0:T(8,128)(2,1)} %cycle_factor.1) | copy-start | bytes 9437188
  5.8 7.3 %copy-start.2 = (s32[1,2]{1,0:T(1,128)S(1)}, s32[1,2]{1,0:T(1,128)}, u32[]{:S(2)}) copy-start(s32[1,2]{1,0:T(1,128)} %param.9) | copy-start | bytes 28
  12.6 32.0 %collective-permute-start.10 = (bf16[768,1536]{1,0:T(8,128)(2,1)S(1)}, bf16[768,1536]{1,0:T(8,128)(2,1)S(1)}, u32[]{:S(2)}, u32[]{:S(2)}) collective-permute-start(bf16[768,1536]{1,0:T(8,128)(2,1)S(1)} %ladder_far.1), channel_id=1, source_target_pairs={{0,1},{1,0},{2,3},{3,2},{4,5},{5,4},{6,7},{7,6},{8,9},{9,8},{10,11... | collective-permute-start | bytes 7077896 | tf_op jit(solution)/shard_map/ppermute | solution.py:324
  14.4 11.0 %collective-permute-start.3 = (bf16[32,1664]{1,0:T(8,128)(2,1)S(1)}, bf16[32,1664]{1,0:T(8,128)(2,1)S(1)}, u32[]{:S(2)}, u32[]{:S(2)}) collective-permute-start(bf16[32,1664]{1,0:T(8,128)(2,1)S(1)} %get-tuple-element.9.second.refs_0_), channel_id=1, source_target_pairs={{0,6},{2,0},{4,2},{6,4},{8,14},{10,8},{12,10},{14,12},{1,7},{3,1},... | collective-permute-start | bytes 319496 | tf_op jit(solution)/shard_map/ppermute | solution.py:303
  17.8 7.8 %collective-permute-start.2 = (bf16[32,1664]{1,0:T(8,128)(2,1)S(1)}, bf16[32,1664]{1,0:T(8,128)(2,1)S(1)}, u32[]{:S(2)}, u32[]{:S(2)}) collective-permute-start(bf16[32,1664]{1,0:T(8,128)(2,1)S(1)} %get-tuple-element.9.second.refs_0_), channel_id=1, source_target_pairs={{0,4},{2,6},{4,0},{6,2},{8,12},{10,14},{12,8},{14,10},{1,5},{3,7},... | collective-permute-start | bytes 319496 | tf_op jit(solution)/shard_map/ppermute | solution.py:303
  17.8 8.6 %collective-permute-start.1 = (bf16[32,1664]{1,0:T(8,128)(2,1)S(1)}, bf16[32,1664]{1,0:T(8,128)(2,1)S(1)}, u32[]{:S(2)}, u32[]{:S(2)}) collective-permute-start(bf16[32,1664]{1,0:T(8,128)(2,1)S(1)} %get-tuple-element.9.second.refs_0_), channel_id=1, source_target_pairs={{0,2},{2,4},{4,6},{6,0},{8,10},{10,12},{12,14},{14,8},{1,3},{3,5},... | collective-permute-start | bytes 319496 | tf_op jit(solution)/shard_map/ppermute | solution.py:303
  19.8 5.6 %collective-permute-start.4 = (bf16[32,1536]{1,0:T(8,128)(2,1)S(1)}, bf16[32,1536]{1,0:T(8,128)(2,1)S(1)}, u32[]{:S(2)}, u32[]{:S(2)}) collective-permute-start(bf16[32,1536]{1,0:T(8,128)(2,1)S(1)} %get-tuple-element.10.first), channel_id=1, source_target_pairs={{0,8},{2,10},{4,12},{6,14},{8,0},{10,2},{12,4},{14,6},{1,9},{3,11}... | collective-permute-start | bytes 294920 | tf_op jit(solution)/shard_map/ppermute | solution.py:310
  26.6 6.7 %collective-permute-start.8 = (bf16[32,1536]{1,0:T(8,128)(2,1)S(1)}, bf16[32,1536]{1,0:T(8,128)(2,1)S(1)}, u32[]{:S(2)}, u32[]{:S(2)}) collective-permute-start(bf16[32,1536]{1,0:T(8,128)(2,1)S(1)} %get-tuple-element.12.refs_8_), channel_id=1, source_target_pairs={{0,8},{2,10},{4,12},{6,14},{8,0},{10,2},{12,4},{14,6},{1,9},{3,11}... | collective-permute-start | bytes 294920 | tf_op jit(solution)/shard_map/ppermute | solution.py:313
  28.6 5.5 %collective-permute-start.7 = (bf16[32,1536]{1,0:T(8,128)(2,1)S(1)}, bf16[32,1536]{1,0:T(8,128)(2,1)S(1)}, u32[]{:S(2)}, u32[]{:S(2)}) collective-permute-start(bf16[32,1536]{1,0:T(8,128)(2,1)S(1)} %get-tuple-element.11.refs_4_), channel_id=1, source_target_pairs={{0,6},{2,0},{4,2},{6,4},{8,14},{10,8},{12,10},{14,12},{1,7},{3,1},... | collective-permute-start | bytes 294920 | tf_op jit(solution)/shard_map/ppermute | solution.py:303
  31.8 4.6 %collective-permute-start.6 = (bf16[32,1536]{1,0:T(8,128)(2,1)S(1)}, bf16[32,1536]{1,0:T(8,128)(2,1)S(1)}, u32[]{:S(2)}, u32[]{:S(2)}) collective-permute-start(bf16[32,1536]{1,0:T(8,128)(2,1)S(1)} %get-tuple-element.11.refs_4_), channel_id=1, source_target_pairs={{0,4},{2,6},{4,0},{6,2},{8,12},{10,14},{12,8},{14,10},{1,5},{3,7},... | collective-permute-start | bytes 294920 | tf_op jit(solution)/shard_map/ppermute | solution.py:303
  31.9 5.5 %collective-permute-start.5 = (bf16[32,1536]{1,0:T(8,128)(2,1)S(1)}, bf16[32,1536]{1,0:T(8,128)(2,1)S(1)}, u32[]{:S(2)}, u32[]{:S(2)}) collective-permute-start(bf16[32,1536]{1,0:T(8,128)(2,1)S(1)} %get-tuple-element.11.refs_4_), channel_id=1, source_target_pairs={{0,2},{2,4},{4,6},{6,0},{8,10},{10,12},{12,14},{14,8},{1,3},{3,5},... | collective-permute-start | bytes 294920 | tf_op jit(solution)/shard_map/ppermute | solution.py:303
  37.5 7.1 %collective-permute-start.9 = (bf16[64,1536]{1,0:T(8,128)(2,1)S(1)}, bf16[64,1536]{1,0:T(8,128)(2,1)S(1)}, u32[]{:S(2)}, u32[]{:S(2)}) collective-permute-start(bf16[64,1536]{1,0:T(8,128)(2,1)S(1)} %sum_last.1.sums), channel_id=1, source_target_pairs={{0,1},{1,0},{2,3},{3,2},{4,5},{5,4},{6,7},{7,6},{8,9},{9,8},{10,11... | collective-permute-start | bytes 589832 | tf_op jit(solution)/shard_map/ppermute | solution.py:326

commit v2 on v0

v2 whole, which is shorter than its diff:
```python
import functools

import jax
import jax.numpy as jnp
from jax import lax
from jax.experimental import pallas as pl
from jax.experimental.pallas import tpu as pltpu
from jax.sharding import PartitionSpec as P

LANES = 128
SMEM = pl.BlockSpec(memory_space=pltpu.SMEM)
VMEM = pl.BlockSpec(memory_space=pltpu.VMEM)
HBM = pl.BlockSpec(memory_space=pltpu.HBM)
FIRST_FIRST = (((0,), (0,)), ((), ()))
LAST_LAST = (((1,), (1,)), ((), ()))
AFTER, COLUMN, ROW, KEPT, START, NAME, FACTS = range(7)
USED, CORE, ORBITAL = range(3)


def params(mib):
    return pltpu.CompilerParams(vmem_limit_bytes=mib * 2**20)


def block(index, size):
    return pl.ds(pl.multiple_of(index * size, size), size)


def in_hbm(array):
    return pltpu.with_memory_space_constraint(array, pltpu.HBM)


def in_smem(array):
    return pltpu.with_memory_space_constraint(array, pltpu.SMEM)


def add_terms(total, table, rows, tiles, slots):
    size = tiles.shape[1]
    terms = [
        lax.dot_general(
            rows[block(table[COLUMN, s], size), :], tiles[k], FIRST_FIRST, preferred_element_type=jnp.float32
        )
        for k, s in enumerate(slots)
    ]
    for s, term in zip(slots, terms):
        total[:, block(table[ROW, s], size)] += term * table[KEPT, s].astype(jnp.float32)


def prepare(coords, mask, orbs, place, own, cycle_factor):
    slots = coords.shape[1]
    local, tile = own.shape[0], own.shape[1]
    width, aux = cycle_factor.shape[1:]
    tiles = width // tile
    places = max(slots, -(-tiles // 4) * 4) + 1

    def body(coords, mask, orbs, place, own, factor, table, held, rows, total, s_coords, s_mask, s_orbs, head, sems):
        loads = [
            pltpu.make_async_copy(source, target, sems.at[n])
            for n, (source, target) in enumerate([(orbs, s_orbs), (coords, s_coords), (mask, s_mask), (own, held)])
        ]
        for load in loads:
            load.start()
        core = place[0]
        total[...] = jnp.zeros_like(total)
        loads[0].wait()
        load_rows = pltpu.make_async_copy(factor.at[s_orbs[0, 0]], rows, sems.at[4])
        load_rows.start()
        table[FACTS, CORE] = core
        table[FACTS, ORBITAL] = s_orbs[0, 1]

        def clear(n, carry):
            head[n] = slots
            table[START, n] = slots
            table[NAME, n] = 0
            return carry

        lax.fori_loop(0, places, clear, 0, unroll=True)
        table[AFTER, slots] = slots
        table[COLUMN, slots] = 0
        loads[1].wait()
        loads[2].wait()

        def put(s, carry):
            g = lax.rem(s + core * local, slots)
            d = s_coords[1, g]
            kept = s_mask[0, g]
            table[COLUMN, s] = s_coords[0, g]
            table[ROW, s] = d
            table[KEPT, s] = kept
            before = head[d]
            table[AFTER, s] = before
            head[d] = jnp.where(kept != 0, s, before)
            return carry

        lax.fori_loop(0, slots, put, 0, unroll=True)

        def name(n, count):
            first = head[n]
            table[NAME, count] = n
            table[START, count] = first
            return count + (first < slots).astype(jnp.int32)

        used = lax.fori_loop(0, tiles, name, jnp.int32(0), unroll=True)
        table[FACTS, USED] = used
        table[START, used] = slots
        table[NAME, used] = 0
        loads[3].wait()
        load_rows.wait()
        add_terms(total, table, rows, held, range(local))

    return pl.pallas_call(
        body,
        out_shape=[
            pltpu.SMEM((7, places), jnp.int32),
            jax.ShapeDtypeStruct(own.shape, own.dtype),
            jax.ShapeDtypeStruct((width, aux), jnp.bfloat16),
            jax.ShapeDtypeStruct((aux, width), jnp.float32),
        ],
        in_specs=[HBM, HBM, HBM, SMEM, HBM, HBM],
        out_specs=[SMEM, VMEM, VMEM, VMEM],
        scratch_shapes=[
            pltpu.SMEM(coords.shape, jnp.int32),
            pltpu.SMEM(mask.shape, jnp.int32),
            pltpu.SMEM(orbs.shape, jnp.int32),
            pltpu.SMEM((places,), jnp.int32),
            pltpu.SemaphoreType.DMA((5,)),
        ],
        compiler_params=params(16),
        name="prepare",
    )(in_hbm(coords), in_hbm(mask), in_hbm(orbs), place, in_hbm(own), in_hbm(cycle_factor))


def intermediate(table, own, other, rows, start, *, cores):
    local, tile = own.shape[0], own.shape[1]
    aux, width = start.shape
    share = aux // cores

    def body(table, own, other, rows, start, out, held, total):
        total[...] = start[...]
        add_terms(total, table, rows, other, range(local, 2 * local))
        out[:, :width] = total[block(table[FACTS, CORE], share), :].astype(out.dtype)
        label = jnp.zeros((share, LANES), jnp.float32) + table[FACTS, ORBITAL].astype(jnp.float32)
        out[:, width:] = label.astype(out.dtype)
        held[:local] = own[...]
        held[local : 2 * local] = other[...]
        held[2 * local] = jnp.zeros((tile, tile), held.dtype)

    return pl.pallas_call(
        body,
        out_shape=[
            jax.ShapeDtypeStruct((share, width + LANES), jnp.bfloat16),
            jax.ShapeDtypeStruct((2 * local + 1, tile, tile), jnp.bfloat16),
        ],
        in_specs=[SMEM, VMEM, VMEM, VMEM, VMEM],
        out_specs=[VMEM, VMEM],
        scratch_shapes=[pltpu.VMEM((aux, width), jnp.float32)],
        compiler_params=params(16),
        name="intermediate",
    )(in_smem(table), own, other, rows, start)


def add_arrivals(table, mine, arrivals, *, plain, labelled):
    share, full = mine.shape
    width = full - LANES

    def body(table, mine, *refs):
        arrivals, out = refs[:-1], refs[-1]
        total = mine[:, :width].astype(jnp.float32)
        label = mine[:, width : width + 1].astype(jnp.float32)
        as_is = table[FACTS, CORE] == plain
        for k, theirs in enumerate(arrivals):
            same = (label == theirs[:, width : width + 1].astype(jnp.float32)).astype(jnp.float32)
            weight = jnp.where(as_is, float(k == len(arrivals) - 1), same)
            total += jnp.where(weight > 0.5, theirs[:, :width].astype(jnp.float32), 0.0)
        out[:, :width] = total.astype(out.dtype)
        if labelled:
            out[:, width:] = mine[:, width:]

    return pl.pallas_call(
        body,
        out_shape=jax.ShapeDtypeStruct((share, full if labelled else width), mine.dtype),
        in_specs=[SMEM, VMEM] + [VMEM] * len(arrivals),
        out_specs=VMEM,
        compiler_params=params(16),
        name="sum_middle" if labelled else "sum_last",
    )(in_smem(table), mine, *arrivals)


def ladder(table, held, factor, *, far, out_dtype):
    empty, tile = held.shape[0] - 1, held.shape[1]
    width = factor.shape[0]
    half = width // 2
    tiles = width // tile
    span = 2 * tile
    group = 4
    room = -(-tiles // group) * group

    def body(table, held, factor, out, left, wide):
        core = table[FACTS, CORE]
        rows = block(1 - core if far else core, half)
        found = table[FACTS, USED]

        def two_slots(s):
            t = table[AFTER, s]
            a = jnp.concatenate(
                [factor[rows, block(table[COLUMN, s], tile)], factor[rows, block(table[COLUMN, t], tile)]], axis=1
            )
            b = jnp.concatenate([held[s], held[t]], axis=0)
            return jnp.dot(a, b, preferred_element_type=jnp.float32), table[AFTER, t]

        def some_tiles(m, carry):
            for k in range(group):
                w = m * group + k
                left[:, block(w, tile)] = two_slots(table[START, w])[0].astype(left.dtype)
            return carry

        lax.fori_loop(0, (found + group - 1) // group, some_tiles, 0)

        def long_tile(w, carry):
            s = table[START, w]

            @pl.when(table[AFTER, table[AFTER, s]] != empty)
            def _():
                value, after = two_slots(s)
                wide[...] = value

                def add(s):
                    value, after = two_slots(s)
                    wide[...] += value
                    return after

                lax.while_loop(lambda s: s != empty, add, after)
                left[:, block(w, tile)] = wide[...].astype(left.dtype)

            return carry

        lax.fori_loop(0, found, long_tile, 0)

        steps = (found + 1) // 2
        for n in range(1, tiles // 2 + 1):

            @pl.when(steps == n)
            def _():
                def piece(j, carry):
                    here = block(j, half)
                    right = jnp.concatenate(
                        [factor[here, block(table[NAME, u], tile)] for u in range(2 * n)], axis=1
                    )
                    value = lax.dot_general(
                        left[:, : n * span], right, LAST_LAST, preferred_element_type=jnp.float32
                    )
                    out[:, here] = value.astype(out.dtype)
                    return carry

                lax.fori_loop(0, width // half, piece, 0)

        @pl.when(steps == 0)
        def _():
            out[...] = jnp.zeros(out.shape, out.dtype)

    return pl.pallas_call(
        body,
        out_shape=jax.ShapeDtypeStruct((half, width), out_dtype),
        in_specs=[SMEM, VMEM, VMEM],
        out_specs=VMEM,
        scratch_shapes=[
            pltpu.VMEM((half, room * tile), jnp.bfloat16),
            pltpu.VMEM((half, tile), jnp.float32),
        ],
        compiler_params=params(32),
        cost_estimate=pl.CostEstimate(
            flops=2 * half * width * width, bytes_accessed=2 * width * width, transcendentals=0
        ),
        name="ladder_far" if far else "ladder_near",
    )(in_smem(table), held, factor)


def finish(table, sums, other_sums, near, arrived, cycle_rows, *, pieces):
    half, width = near.shape
    aux = cycle_rows.shape[1]
    share = sums.shape[0]
    rows = half // pieces

    def body(table, sums, other_sums, near, arrived, factor, out, low, done, sems):
        core = table[FACTS, CORE]
        low[block(core, share), :] = sums[...]
        low[block(1 - core, share), :] = other_sums[...]
        stores = []
        for n in range(pieces):
            here = slice(n * rows, (n + 1) * rows)
            term = jnp.dot(
                factor[pl.ds(pl.multiple_of(core * half + n * rows, rows), rows), :], low[...],
                preferred_element_type=jnp.float32,
            )
            done[here, :] = (near[here, :].astype(jnp.float32) + arrived[here, :].astype(jnp.float32) + term).astype(done.dtype)
            store = pltpu.make_async_copy(done.at[here, :], out.at[here, :], sems.at[n])
            store.start()
            stores.append(store)
        for store in stores:
            store.wait()

    return pl.pallas_call(
        body,
        out_shape=jax.ShapeDtypeStruct((half, width), jnp.bfloat16),
        in_specs=[SMEM, VMEM, VMEM, VMEM, VMEM, VMEM],
        out_specs=HBM,
        scratch_shapes=[
            pltpu.VMEM((aux, width), jnp.bfloat16),
            pltpu.VMEM((half, width), jnp.bfloat16),
            pltpu.SemaphoreType.DMA((pieces,)),
        ],
        compiler_params=params(32),
        name="finish",
    )(in_smem(table), sums, other_sums, near, arrived, cycle_rows)


def shards(amp_tiles, tile_coords, tile_mask, pair_orbs, ladder_factor, cycle_factor):
    cores, pairs = lax.axis_size("virt"), lax.axis_size("pair")
    assert cores == 2 and pairs % 2 == 0
    own = amp_tiles[0]
    place = lax.axis_index("virt").astype(jnp.int32).reshape(1)
    swap = [(0, 1), (1, 0)]
    other = lax.ppermute(own, "virt", swap)
    table, own, cycle_rows, start = prepare(tile_coords[0].T, tile_mask, pair_orbs, place, own, cycle_factor)
    message, held = intermediate(table, own, other, cycle_rows, start, cores=cores)
    factor = ladder_factor[0]
    outgoing = ladder(table, held, factor, far=True, out_dtype=jnp.bfloat16)

    classes = pairs // 2
    even = classes & (classes - 1) == 0

    def within(p, k):
        return p // classes * classes + (p % classes ^ k if even else (p % classes + k) % classes)

    def permute(value, k, far_core):
        routes = []
        for p in range(pairs):
            for core in range(cores):
                if core != far_core:
                    routes.append((p * cores + core, within(p, k) * cores + core))
                elif k == classes - 1:
                    routes.append((p * cores + core, (p + classes) % pairs * cores + core))
        return lax.ppermute(value, ("pair", "virt"), routes)

    if 2 <= classes <= 4:
        arrivals = [permute(message, k, 0) for k in range(1, classes)]
        arrivals, outgoing = lax.optimization_barrier((arrivals, outgoing))
        arrived = lax.ppermute(outgoing, "virt", swap)
        middle = add_arrivals(table, message, arrivals, plain=0, labelled=True)
        middle, held = lax.optimization_barrier((middle, held))
        near = ladder(table, held, factor, far=False, out_dtype=jnp.float32)
        arrivals = [permute(middle, k, 1) for k in range(1, classes)]
        arrivals, near = lax.optimization_barrier((arrivals, near))
        sums = add_arrivals(table, middle, arrivals, plain=1, labelled=False)
    else:
        arrived = lax.ppermute(outgoing, "virt", swap)
        near = ladder(table, held, factor, far=False, out_dtype=jnp.float32)
        width = factor.shape[0]
        right = pair_orbs[0, 1]
        occupied = jnp.arange(cycle_factor.shape[0], dtype=jnp.int32) == right
        mine = message[:, :width].astype(jnp.float32)
        total = lax.psum(jnp.where(occupied[:, None, None], mine[None], 0.0), "pair")
        sums = lax.dynamic_index_in_dim(total, right, 0, keepdims=False).astype(jnp.bfloat16)

    other_sums = lax.ppermute(sums, "virt", swap)
    return finish(table, sums, other_sums, near, arrived, cycle_rows, pieces=4)[None]


def solution(mesh):
    in_specs = (
        P(("groups", "pair"), "virt", None, None),
        P(("groups", "pair"), None, None),
        P(("groups", "pair"), None),
        P(("groups", "pair"), None),
        P(("groups", "virt"), None, None),
        P("groups", None, None),
    )
    out_specs = P(("groups", "pair"), "virt", None)
    return jax.shard_map(shards, mesh=mesh, in_specs=in_specs, out_specs=out_specs, check_vma=False)
```

time: 230 us -> 35.3 us (0.15)
  blocking collectives: 143 us -> 0 us
  local copies, waits for them, and re-layouts: 35.4 us -> 0.01 us
  matrix products: 25.6 us -> 0 us
  Pallas kernels: 0 us -> 17.4 us
  between operations: 17.1 us -> 0.31 us
  starting transfers between devices: 0.01 us -> 15.9 us
  other arithmetic: 6.64 us -> 0 us
    psum x1 -> x0, blocking collectives: 140 us -> none  [shards(): lax.psum(chosen[:, None, None] * distribute_tiles[None], ('pair', 'virt'))]
    dot_general x4 -> x0, matrix products: 25.6 us -> none  [the longest x1 18.2 us: shards(): jnp.dot(left_cols, contraction_block, preferred_element_type=jnp.float32)]
    pallas_call x0 -> x7, Pallas kernels: none -> 17.4 us  [the longest x2 12.6 us: ladder(): pl.pallas_call(body, out_shape=jax.ShapeDtypeStruct((half, width), out_dt...]
    ppermute x0 -> x9, starting transfers between devices: none -> 15.9 us  [the longest x6 12.3 us: permute(): return lax.ppermute(value, ('pair', 'virt'), routes)]
    gather x3 -> x0, local copies, waits for them, and re-layouts: 14.9 us -> none  [the longest x1 6.37 us: tile_products(): jnp.take(row_block.reshape(row_total, tile_count, tile_size), coords[:, 0...]
    unnamed x9 -> x2, local copies, waits for them, and re-layouts: 7.48 us -> 0.01 us
    another operation x1 -> x0, local copies, waits for them, and re-layouts: 6.66 us -> none  [tile_products(): row_block.reshape(row_total, tile_count, tile_size)]
    mul x2 -> x0, other arithmetic: 5.95 us -> none  [the longest x1 4.92 us: shards(): chosen[:, None, None] * distribute_tiles[None]]
  transfers between devices with their start and end apart: 1 -> 9, of which waited for: 0 -> 1; matrix products, arithmetic and copies ran while one was open for 7% -> 0% of each run, Pallas kernels for 0% -> 44%
where the time goes in v2:
time: 35.3 us; the launch traced here: 35.1 us
  Pallas kernels  17.4 us (49%)
  starting transfers between devices  15.9 us (45%)
  waiting for transfers between devices  1.45 us (4%)
    pallas_call x2, Pallas kernels, ladder(): pl.pallas_call(body, out_shape=jax.ShapeDtypeStruct((half, width), out_dt...  12.6 us
    ppermute x6, starting transfers between devices, permute(): return lax.ppermute(value, ('pair', 'virt'), routes)  12.3 us
    ppermute x1, starting transfers between devices, shards(): arrived = lax.ppermute(outgoing, 'virt', swap)  2.99 us
    pallas_call x1, Pallas kernels, prepare(): pl.pallas_call(body, out_shape=[pltpu.SMEM((7, places), jnp.int32), jax.S...  2.28 us
    pallas_call x1, Pallas kernels, finish(): pl.pallas_call(body, out_shape=jax.ShapeDtypeStruct((half, width), jnp.bf...  1.76 us
    ppermute x1, waiting for transfers between devices, shards(): other_sums = lax.ppermute(sums, 'virt', swap)  1.43 us
  transfers between devices with their start and end apart: 9, of which 1 were waited for; matrix products, arithmetic and copies ran while one was open for 0% of the time, Pallas kernels for 44%

profile of v2, /device:TPU:0, one launch (start us, length us, event | category | flops | bytes accessed | tf_op | source)
XLA Modules:
  0.0 35.1 jit_solution(11356324101757969541)
XLA Ops:
  0.0 0.5 %collective-permute-start = (bf16[8,128,128]{2,1,0:T(8,128)(2,1)}, bf16[8,128,128]{2,1,0:T(8,128)(2,1)S(1)}, u32[]{:S(2)}, u32[]{:S(2)}) collective-permute-start(bf16[8,128,128]{2,1,0:T(8,128)(2,1)} %bitcast.9), channel_id=1, source_target_pairs={{0,1},{1,0},{2,3},{3,2},{4,5},{5,4},{6,7},{7,6},{8,9},{9,8},{10,11... | collective-permute-start | bytes 786440 | tf_op jit(solution)/shard_map/ppermute | solution.py:322
  0.5 0.0 copy-start
  0.5 2.3 %prepare.1 = (s32[7,17]{1,0:T(8,128)S(4)}, bf16[8,128,128]{2,1,0:T(8,128)(2,1)S(1)}, bf16[1536,128]{1,0:T(8,128)(2,1)S(1)}, f32[128,1536]{1,0:T(8,128)S(1)}) custom-call(s32[2,16]{1,0:T(2,128)} %bitcast.11, s32[1,16]{1,0:T(1,128)} %mask.1, s32[1,2]{1,0:T(1,128)} %orbs.1, s32[1]{0:T(128)} %bitcast.2.place, bf16[8,128,128]{2,1,0:T(8,128)(2,1)} %bitcast.10, ...), custom_call_target="tpu_custom_call" | custom-call | tf_op jit(solution)/shard_map/prepare/pallas_call | solution.py:110
  2.7 0.0 collective-permute-done.other
  2.8 0.3 intermediate.1
  3.1 3.7 %collective-permute-start.3 = (bf16[64,1664]{1,0:T(8,128)(2,1)S(1)}, bf16[64,1664]{1,0:T(8,128)(2,1)S(1)}, u32[]{:S(2)}, u32[]{:S(2)}) collective-permute-start(bf16[64,1664]{1,0:T(8,128)(2,1)S(1)} %get-tuple-element.25.mine), channel_id=1, source_target_pairs={{0,8},{1,7},{2,10},{3,5},{4,12},{5,3},{6,14},{7,1},{8,0},{9,15},{1... | collective-permute-start | bytes 638984 | tf_op jit(solution)/shard_map/ppermute | solution.py:342
  6.7 0.7 %collective-permute-start.2 = (bf16[64,1664]{1,0:T(8,128)(2,1)S(1)}, bf16[64,1664]{1,0:T(8,128)(2,1)S(1)}, u32[]{:S(2)}, u32[]{:S(2)}) collective-permute-start(bf16[64,1664]{1,0:T(8,128)(2,1)S(1)} %get-tuple-element.25.mine), channel_id=1, source_target_pairs={{1,5},{3,7},{5,1},{7,3},{9,13},{11,15},{13,9},{15,11},{17,21},{19,... | collective-permute-start | bytes 638984 | tf_op jit(solution)/shard_map/ppermute | solution.py:342
  7.4 0.7 %collective-permute-start.1 = (bf16[64,1664]{1,0:T(8,128)(2,1)S(1)}, bf16[64,1664]{1,0:T(8,128)(2,1)S(1)}, u32[]{:S(2)}, u32[]{:S(2)}) collective-permute-start(bf16[64,1664]{1,0:T(8,128)(2,1)S(1)} %get-tuple-element.25.mine), channel_id=1, source_target_pairs={{1,3},{3,1},{5,7},{7,5},{9,11},{11,9},{13,15},{15,13},{17,19},{19,... | collective-permute-start | bytes 638984 | tf_op jit(solution)/shard_map/ppermute | solution.py:342
  8.1 0.0 copy-done
  8.1 6.2 %ladder_far.1 = bf16[768,1536]{1,0:T(8,128)(2,1)S(1)} custom-call(s32[7,17]{1,0:T(8,128)S(4)} %get-tuple-element.21.table, bf16[17,128,128]{2,1,0:T(8,128)(2,1)S(1)} %get-tuple-element.31.held, bf16[1536,1536]{1,0:T(8,128)(2,1)S(1)} %bitcast.7), custom_call_target="tpu_custom_call" | custom-call | flops 3623878656 | bytes 4718592 | tf_op jit(solution)/shard_map/ladder_far/pallas_call | solution.py:260
  14.4 0.0 collective-permute-done.3.refs_2_
  14.4 0.0 collective-permute-done.2.refs_1_
  14.4 0.0 collective-permute-done.1.refs_0_
  14.4 3.0 %collective-permute-start.8 = (bf16[768,1536]{1,0:T(8,128)(2,1)S(1)}, bf16[768,1536]{1,0:T(8,128)(2,1)S(1)}, u32[]{:S(2)}, u32[]{:S(2)}) collective-permute-start(bf16[768,1536]{1,0:T(8,128)(2,1)S(1)} %ladder_far.1), channel_id=1, source_target_pairs={{0,1},{1,0},{2,3},{3,2},{4,5},{5,4},{6,7},{7,6},{8,9},{9,8},{10,11... | collective-permute-start | bytes 7077896 | tf_op jit(solution)/shard_map/ppermute | solution.py:347
  17.4 0.2 sum_middle.1.mine
  17.6 1.4 %collective-permute-start.6 = (bf16[64,1664]{1,0:T(8,128)(2,1)S(1)}, bf16[64,1664]{1,0:T(8,128)(2,1)S(1)}, u32[]{:S(2)}, u32[]{:S(2)}) collective-permute-start(bf16[64,1664]{1,0:T(8,128)(2,1)S(1)} %sum_middle.1.mine), channel_id=1, source_target_pairs={{0,6},{1,9},{2,4},{3,11},{4,2},{5,13},{6,0},{7,15},{8,14},{9,1},{1... | collective-permute-start | bytes 638984 | tf_op jit(solution)/shard_map/ppermute | solution.py:342
  19.0 2.3 %collective-permute-start.5 = (bf16[64,1664]{1,0:T(8,128)(2,1)S(1)}, bf16[64,1664]{1,0:T(8,128)(2,1)S(1)}, u32[]{:S(2)}, u32[]{:S(2)}) collective-permute-start(bf16[64,1664]{1,0:T(8,128)(2,1)S(1)} %sum_middle.1.mine), channel_id=1, source_target_pairs={{0,4},{2,6},{4,0},{6,2},{8,12},{10,14},{12,8},{14,10},{16,20},{18,... | collective-permute-start | bytes 638984 | tf_op jit(solution)/shard_map/ppermute | solution.py:342
  21.3 3.7 %collective-permute-start.4 = (bf16[64,1664]{1,0:T(8,128)(2,1)S(1)}, bf16[64,1664]{1,0:T(8,128)(2,1)S(1)}, u32[]{:S(2)}, u32[]{:S(2)}) collective-permute-start(bf16[64,1664]{1,0:T(8,128)(2,1)S(1)} %sum_middle.1.mine), channel_id=1, source_target_pairs={{0,2},{2,0},{4,6},{6,4},{8,10},{10,8},{12,14},{14,12},{16,18},{18,... | collective-permute-start | bytes 638984 | tf_op jit(solution)/shard_map/ppermute | solution.py:342
  25.0 6.4 %ladder_near.1.near = f32[768,1536]{1,0:T(8,128)S(1)} custom-call(s32[7,17]{1,0:T(8,128)S(4)} %get-tuple-element.21.table, bf16[17,128,128]{2,1,0:T(8,128)(2,1)S(1)} %get-tuple-element.31.held, bf16[1536,1536]{1,0:T(8,128)(2,1)S(1)} %bitcast.8), custom_call_target="tpu_custom_call" | custom-call | flops 3623878656 | bytes 4718592 | tf_op jit(solution)/shard_map/ladder_near/pallas_call | solution.py:260
  31.4 0.0 collective-permute-done.6.refs_2_
  31.4 0.0 collective-permute-done.5.refs_1_
  31.4 0.0 collective-permute-done.4.refs_0_
  31.4 0.2 sum_last.1.sums
  31.6 0.1 collective-permute-start.7
  31.7 1.4 %collective-permute-done.7.other_sums = bf16[64,1536]{1,0:T(8,128)(2,1)S(1)} collective-permute-done((bf16[64,1536]{1,0:T(8,128)(2,1)S(1)}, bf16[64,1536]{1,0:T(8,128)(2,1)S(1)}, u32[]{:S(2)}, u32[]{:S(2)}) %collective-permute-start.7) | collective-permute-done | bytes 196640 | tf_op jit(solution)/shard_map/ppermute | solution.py:364
  33.1 0.0 collective-permute-done.8.arrived
  33.1 1.8 %finish.1 = bf16[768,1536]{1,0:T(8,128)(2,1)} custom-call(s32[7,17]{1,0:T(8,128)S(4)} %get-tuple-element.21.table, bf16[64,1536]{1,0:T(8,128)(2,1)S(1)} %sum_last.1.sums, bf16[64,1536]{1,0:T(8,128)(2,1)S(1)} %collective-permute-done.7.other_sums, f32[768,1536]{1,0:T(8,128)S(1)} %ladder_near.1.near, bf16[768,1536]{1,0:T(8,128)(2,1)S(1)} %collective-permute-done.8.arrived, ...), custom_call_target="tpu_custom_call" | custom-call | tf_op jit(solution)/shard_map/finish/pallas_call | solution.py:301
Async XLA Ops:
  0.0 2.7 %collective-permute-start = (bf16[8,128,128]{2,1,0:T(8,128)(2,1)}, bf16[8,128,128]{2,1,0:T(8,128)(2,1)S(1)}, u32[]{:S(2)}, u32[]{:S(2)}) collective-permute-start(bf16[8,128,128]{2,1,0:T(8,128)(2,1)} %bitcast.9), channel_id=1, source_target_pairs={{0,1},{1,0},{2,3},{3,2},{4,5},{5,4},{6,7},{7,6},{8,9},{9,8},{10,11... | collective-permute-start | bytes 786440 | tf_op jit(solution)/shard_map/ppermute | solution.py:322
  0.5 7.6 %copy-start = (bf16[1,1536,1536]{2,1,0:T(8,128)(2,1)S(1)}, bf16[1,1536,1536]{2,1,0:T(8,128)(2,1)}, u32[]{:S(2)}) copy-start(bf16[1,1536,1536]{2,1,0:T(8,128)(2,1)} %param.10) | copy-start | bytes 14155780
  3.1 11.3 %collective-permute-start.3 = (bf16[64,1664]{1,0:T(8,128)(2,1)S(1)}, bf16[64,1664]{1,0:T(8,128)(2,1)S(1)}, u32[]{:S(2)}, u32[]{:S(2)}) collective-permute-start(bf16[64,1664]{1,0:T(8,128)(2,1)S(1)} %get-tuple-element.25.mine), channel_id=1, source_target_pairs={{0,8},{1,7},{2,10},{3,5},{4,12},{5,3},{6,14},{7,1},{8,0},{9,15},{1... | collective-permute-start | bytes 638984 | tf_op jit(solution)/shard_map/ppermute | solution.py:342
  6.7 7.6 %collective-permute-start.2 = (bf16[64,1664]{1,0:T(8,128)(2,1)S(1)}, bf16[64,1664]{1,0:T(8,128)(2,1)S(1)}, u32[]{:S(2)}, u32[]{:S(2)}) collective-permute-start(bf16[64,1664]{1,0:T(8,128)(2,1)S(1)} %get-tuple-element.25.mine), channel_id=1, source_target_pairs={{1,5},{3,7},{5,1},{7,3},{9,13},{11,15},{13,9},{15,11},{17,21},{19,... | collective-permute-start | bytes 638984 | tf_op jit(solution)/shard_map/ppermute | solution.py:342
  7.4 7.0 %collective-permute-start.1 = (bf16[64,1664]{1,0:T(8,128)(2,1)S(1)}, bf16[64,1664]{1,0:T(8,128)(2,1)S(1)}, u32[]{:S(2)}, u32[]{:S(2)}) collective-permute-start(bf16[64,1664]{1,0:T(8,128)(2,1)S(1)} %get-tuple-element.25.mine), channel_id=1, source_target_pairs={{1,3},{3,1},{5,7},{7,5},{9,11},{11,9},{13,15},{15,13},{17,19},{19,... | collective-permute-start | bytes 638984 | tf_op jit(solution)/shard_map/ppermute | solution.py:342
  14.4 18.8 %collective-permute-start.8 = (bf16[768,1536]{1,0:T(8,128)(2,1)S(1)}, bf16[768,1536]{1,0:T(8,128)(2,1)S(1)}, u32[]{:S(2)}, u32[]{:S(2)}) collective-permute-start(bf16[768,1536]{1,0:T(8,128)(2,1)S(1)} %ladder_far.1), channel_id=1, source_target_pairs={{0,1},{1,0},{2,3},{3,2},{4,5},{5,4},{6,7},{7,6},{8,9},{9,8},{10,11... | collective-permute-start | bytes 7077896 | tf_op jit(solution)/shard_map/ppermute | solution.py:347
  17.6 13.8 %collective-permute-start.6 = (bf16[64,1664]{1,0:T(8,128)(2,1)S(1)}, bf16[64,1664]{1,0:T(8,128)(2,1)S(1)}, u32[]{:S(2)}, u32[]{:S(2)}) collective-permute-start(bf16[64,1664]{1,0:T(8,128)(2,1)S(1)} %sum_middle.1.mine), channel_id=1, source_target_pairs={{0,6},{1,9},{2,4},{3,11},{4,2},{5,13},{6,0},{7,15},{8,14},{9,1},{1... | collective-permute-start | bytes 638984 | tf_op jit(solution)/shard_map/ppermute | solution.py:342
  19.0 12.4 %collective-permute-start.5 = (bf16[64,1664]{1,0:T(8,128)(2,1)S(1)}, bf16[64,1664]{1,0:T(8,128)(2,1)S(1)}, u32[]{:S(2)}, u32[]{:S(2)}) collective-permute-start(bf16[64,1664]{1,0:T(8,128)(2,1)S(1)} %sum_middle.1.mine), channel_id=1, source_target_pairs={{0,4},{2,6},{4,0},{6,2},{8,12},{10,14},{12,8},{14,10},{16,20},{18,... | collective-permute-start | bytes 638984 | tf_op jit(solution)/shard_map/ppermute | solution.py:342
  21.3 10.1 %collective-permute-start.4 = (bf16[64,1664]{1,0:T(8,128)(2,1)S(1)}, bf16[64,1664]{1,0:T(8,128)(2,1)S(1)}, u32[]{:S(2)}, u32[]{:S(2)}) collective-permute-start(bf16[64,1664]{1,0:T(8,128)(2,1)S(1)} %sum_middle.1.mine), channel_id=1, source_target_pairs={{0,2},{2,0},{4,6},{6,4},{8,10},{10,8},{12,14},{14,12},{16,18},{18,... | collective-permute-start | bytes 638984 | tf_op jit(solution)/shard_map/ppermute | solution.py:342
  31.6 1.5 %collective-permute-start.7 = (bf16[64,1536]{1,0:T(8,128)(2,1)S(1)}, bf16[64,1536]{1,0:T(8,128)(2,1)S(1)}, u32[]{:S(2)}, u32[]{:S(2)}) collective-permute-start(bf16[64,1536]{1,0:T(8,128)(2,1)S(1)} %sum_last.1.sums), channel_id=1, source_target_pairs={{0,1},{1,0},{2,3},{3,2},{4,5},{5,4},{6,7},{7,6},{8,9},{9,8},{10,11... | collective-permute-start | bytes 589832 | tf_op jit(solution)/shard_map/ppermute | solution.py:364

commit v3 on v2

--- a/solution.py
+++ b/solution.py
@@ -158,129 +158,185 @@
     )(in_smem(table), own, other, rows, start)
 
 
-def add_arrivals(table, mine, arrivals, *, plain, labelled):
-    share, full = mine.shape
+def step(table, next_orbs, mine, arrival, *, plain):
+    share, full = arrival.shape
     width = full - LANES
 
-    def body(table, mine, *refs):
-        arrivals, out = refs[:-1], refs[-1]
-        total = mine[:, :width].astype(jnp.float32)
-        label = mine[:, width : width + 1].astype(jnp.float32)
-        as_is = table[FACTS, CORE] == plain
-        for k, theirs in enumerate(arrivals):
-            same = (label == theirs[:, width : width + 1].astype(jnp.float32)).astype(jnp.float32)
-            weight = jnp.where(as_is, float(k == len(arrivals) - 1), same)
-            total += jnp.where(weight > 0.5, theirs[:, :width].astype(jnp.float32), 0.0)
-        out[:, :width] = total.astype(out.dtype)
-        if labelled:
-            out[:, width:] = mine[:, width:]
-
-    return pl.pallas_call(
-        body,
-        out_shape=jax.ShapeDtypeStruct((share, full if labelled else width), mine.dtype),
-        in_specs=[SMEM, VMEM] + [VMEM] * len(arrivals),
+    def body(table, next_orbs, mine, arrival, kept, out):
+        value = mine[:, :width].astype(jnp.float32)
+        extra = arrival[:, :width].astype(jnp.float32)
+        own = jnp.zeros((share, LANES), jnp.float32) + table[FACTS, ORBITAL].astype(jnp.float32)
+        out[:, width:] = own.astype(out.dtype)
+
+        @pl.when(table[FACTS, CORE] == plain)
+        def _():
+            total = value + extra
+            kept[...] = total
+            out[:, :width] = total.astype(out.dtype)
+
+        @pl.when(table[FACTS, CORE] != plain)
+        def _():
+            label = own[:, :1]
+            theirs = arrival[:, width : width + 1].astype(jnp.float32)
+            behind = next_orbs[0:1, 1:2].astype(jnp.float32)
+            kept[...] = value + jnp.where(theirs == label, extra, 0.0)
+            out[:, :width] = (
+                jnp.where(label == behind, value, 0.0) + jnp.where(theirs == behind, extra, 0.0)
+            ).astype(out.dtype)
+
+    return pl.pallas_call(
+        body,
+        out_shape=[
+            jax.ShapeDtypeStruct((share, width), jnp.float32),
+            jax.ShapeDtypeStruct((share, full), arrival.dtype),
+        ],
+        in_specs=[SMEM, VMEM, VMEM, VMEM],
+        out_specs=[VMEM, VMEM],
+        compiler_params=params(16),
+        name="step",
+    )(in_smem(table), next_orbs, mine, arrival)
+
+
+def last_step(mine, arrival):
+    width = mine.shape[1]
+
+    def body(mine, arrival, out):
+        out[...] = (mine[...] + arrival[:, :width].astype(jnp.float32)).astype(out.dtype)
+
+    return pl.pallas_call(
+        body,
+        out_shape=jax.ShapeDtypeStruct(mine.shape, arrival.dtype),
+        in_specs=[VMEM, VMEM],
         out_specs=VMEM,
         compiler_params=params(16),
-        name="sum_middle" if labelled else "sum_last",
-    )(in_smem(table), mine, *arrivals)
-
-
-def ladder(table, held, factor, *, far, out_dtype):
+        name="last_step",
+    )(mine, arrival)
+
+
+def build_half(table, held, factor, left, wide, *, far):
     empty, tile = held.shape[0] - 1, held.shape[1]
+    half, group = left.shape[0], 4
+    core = table[FACTS, CORE]
+    found = table[FACTS, USED]
+    rows = block(1 - core if far else core, half)
+
+    def two_slots(s):
+        t = table[AFTER, s]
+        a = jnp.concatenate(
+            [factor[rows, block(table[COLUMN, s], tile)], factor[rows, block(table[COLUMN, t], tile)]], axis=1
+        )
+        b = jnp.concatenate([held[s], held[t]], axis=0)
+        return jnp.dot(a, b, preferred_element_type=jnp.float32), table[AFTER, t]
+
+    def some_tiles(m, carry):
+        for k in range(group):
+            w = m * group + k
+            left[:, block(w, tile)] = two_slots(table[START, w])[0].astype(left.dtype)
+        return carry
+
+    lax.fori_loop(0, (found + group - 1) // group, some_tiles, 0)
+
+    def long_tile(w, carry):
+        s = table[START, w]
+
+        @pl.when(table[AFTER, table[AFTER, s]] != empty)
+        def _():
+            value, after = two_slots(s)
+            wide[...] = value
+
+            def add(s):
+                value, after = two_slots(s)
+                wide[...] += value
+                return after
+
+            lax.while_loop(lambda s: s != empty, add, after)
+            left[:, block(w, tile)] = wide[...].astype(left.dtype)
+
+        return carry
+
+    lax.fori_loop(0, found, long_tile, 0)
+
+
+def multiply(table, left, factor, tile, first_side, out):
+    half = left.shape[0]
+    steps = (table[FACTS, USED] + 1) // 2
+    for n in range(factor.shape[0] // tile // 2 + 1):
+
+        @pl.when(steps == n)
+        def _():
+            def unit(k, carry):
+                if n == 0:
+                    out[k] = jnp.zeros((half, half), out.dtype)
+                    return carry
+                here = block(first_side + k, half)
+                right = jnp.concatenate(
+                    [factor[here, block(table[NAME, w], tile)] for w in range(2 * n)], axis=1
+                )
+                out[k] = lax.dot_general(
+                    left[:, : 2 * n * tile], right, LAST_LAST, preferred_element_type=jnp.float32
+                ).astype(out.dtype)
+                return carry
+
+            lax.fori_loop(0, out.shape[0], unit, 0)
+
+
+def ladder_first(table, held, factor):
+    tile = held.shape[1]
     width = factor.shape[0]
     half = width // 2
-    tiles = width // tile
-    span = 2 * tile
-    group = 4
-    room = -(-tiles // group) * group
-
-    def body(table, held, factor, out, left, wide):
-        core = table[FACTS, CORE]
-        rows = block(1 - core if far else core, half)
-        found = table[FACTS, USED]
-
-        def two_slots(s):
-            t = table[AFTER, s]
-            a = jnp.concatenate(
-                [factor[rows, block(table[COLUMN, s], tile)], factor[rows, block(table[COLUMN, t], tile)]], axis=1
-            )
-            b = jnp.concatenate([held[s], held[t]], axis=0)
-            return jnp.dot(a, b, preferred_element_type=jnp.float32), table[AFTER, t]
-
-        def some_tiles(m, carry):
-            for k in range(group):
-                w = m * group + k
-                left[:, block(w, tile)] = two_slots(table[START, w])[0].astype(left.dtype)
-            return carry
-
-        lax.fori_loop(0, (found + group - 1) // group, some_tiles, 0)
-
-        def long_tile(w, carry):
-            s = table[START, w]
-
-            @pl.when(table[AFTER, table[AFTER, s]] != empty)
-            def _():
-                value, after = two_slots(s)
-                wide[...] = value
-
-                def add(s):
-                    value, after = two_slots(s)
-                    wide[...] += value
-                    return after
-
-                lax.while_loop(lambda s: s != empty, add, after)
-                left[:, block(w, tile)] = wide[...].astype(left.dtype)
-
-            return carry
-
-        lax.fori_loop(0, found, long_tile, 0)
-
-        steps = (found + 1) // 2
-        for n in range(1, tiles // 2 + 1):
-
-            @pl.when(steps == n)
-            def _():
-                def piece(j, carry):
-                    here = block(j, half)
-                    right = jnp.concatenate(
-                        [factor[here, block(table[NAME, u], tile)] for u in range(2 * n)], axis=1
-                    )
-                    value = lax.dot_general(
-                        left[:, : n * span], right, LAST_LAST, preferred_element_type=jnp.float32
-                    )
-                    out[:, here] = value.astype(out.dtype)
-                    return carry
-
-                lax.fori_loop(0, width // half, piece, 0)
-
-        @pl.when(steps == 0)
-        def _():
-            out[...] = jnp.zeros(out.shape, out.dtype)
-
-    return pl.pallas_call(
-        body,
-        out_shape=jax.ShapeDtypeStruct((half, width), out_dtype),
-        in_specs=[SMEM, VMEM, VMEM],
-        out_specs=VMEM,
-        scratch_shapes=[
-            pltpu.VMEM((half, room * tile), jnp.bfloat16),
-            pltpu.VMEM((half, tile), jnp.float32),
-        ],
+    room = -(-(width // tile) // 4) * 4 * tile
+
+    def body(table, held, factor, left, far_a, wide):
+        build_half(table, held, factor, left, wide, far=True)
+        multiply(table, left, factor, tile, 0, far_a)
+
+    return ladder_call(
+        body, [(half, room), (1, half, half)], (half, tile), in_smem(table), held, factor, flops=10**10
+    )
+
+
+def ladder_second(table, held, factor, left_far):
+    tile = held.shape[1]
+    half, room = left_far.shape
+
+    def body(table, held, factor, left_far, left, far_b, wide):
+        multiply(table, left_far, factor, tile, 1, far_b)
+        build_half(table, held, factor, left, wide, far=False)
+
+    return ladder_call(
+        body, [(half, room), (1, half, half)], (half, tile), in_smem(table), held, factor, left_far, flops=10**10
+    )
+
+
+def ladder_third(table, factor, left, tile):
+    half = left.shape[0]
+
+    def body(table, factor, left, near, wide):
+        multiply(table, left, factor, tile, 0, near)
+
+    return ladder_call(body, [(2, half, half)], (half, tile), in_smem(table), factor, left, flops=4 * 10**10)[0]
+
+
+def ladder_call(body, shapes, wide, *operands, flops):
+    return pl.pallas_call(
+        body,
+        out_shape=[jax.ShapeDtypeStruct(shape, jnp.bfloat16) for shape in shapes],
+        in_specs=[SMEM] + [VMEM] * (len(operands) - 1),
+        out_specs=[VMEM] * len(shapes),
+        scratch_shapes=[pltpu.VMEM(wide, jnp.float32)],
         compiler_params=params(32),
-        cost_estimate=pl.CostEstimate(
-            flops=2 * half * width * width, bytes_accessed=2 * width * width, transcendentals=0
-        ),
-        name="ladder_far" if far else "ladder_near",
-    )(in_smem(table), held, factor)
+        cost_estimate=pl.CostEstimate(flops=flops, bytes_accessed=1, transcendentals=0),
+        name="ladder",
+    )(*operands)
 
 
 def finish(table, sums, other_sums, near, arrived, cycle_rows, *, pieces):
-    half, width = near.shape
+    half, width = near.shape[1], 2 * near.shape[2]
     aux = cycle_rows.shape[1]
     share = sums.shape[0]
     rows = half // pieces
 
-    def body(table, sums, other_sums, near, arrived, factor, out, low, done, sems):
+    def body(table, sums, other_sums, near, far_a, far_b, factor, out, low, done, sems):
         core = table[FACTS, CORE]
         low[block(core, share), :] = sums[...]
         low[block(1 - core, share), :] = other_sums[...]
@@ -291,7 +347,10 @@
                 factor[pl.ds(pl.multiple_of(core * half + n * rows, rows), rows), :], low[...],
                 preferred_element_type=jnp.float32,
             )
-            done[here, :] = (near[here, :].astype(jnp.float32) + arrived[here, :].astype(jnp.float32) + term).astype(done.dtype)
+            for k, arrived in enumerate([far_a, far_b]):
+                side = slice(k * half, (k + 1) * half)
+                total = near[k, here, :].astype(jnp.float32) + arrived[0, here, :].astype(jnp.float32) + term[:, side]
+                done[here, side] = total.astype(done.dtype)
             store = pltpu.make_async_copy(done.at[here, :], out.at[here, :], sems.at[n])
             store.start()
             stores.append(store)
@@ -301,7 +360,7 @@
     return pl.pallas_call(
         body,
         out_shape=jax.ShapeDtypeStruct((half, width), jnp.bfloat16),
-        in_specs=[SMEM, VMEM, VMEM, VMEM, VMEM, VMEM],
+        in_specs=[SMEM] + [VMEM] * 6,
         out_specs=HBM,
         scratch_shapes=[
             pltpu.VMEM((aux, width), jnp.bfloat16),
@@ -310,7 +369,7 @@
         ],
         compiler_params=params(32),
         name="finish",
-    )(in_smem(table), sums, other_sums, near, arrived, cycle_rows)
+    )(in_smem(table), sums, other_sums, near, *arrived, cycle_rows)
 
 
 def shards(amp_tiles, tile_coords, tile_mask, pair_orbs, ladder_factor, cycle_factor):
@@ -320,40 +379,39 @@
     place = lax.axis_index("virt").astype(jnp.int32).reshape(1)
     swap = [(0, 1), (1, 0)]
     other = lax.ppermute(own, "virt", swap)
+    square = pairs == 8
+    if square:
+        next_orbs = lax.ppermute(pair_orbs, "pair", [(p, p ^ 2) for p in range(pairs)])
     table, own, cycle_rows, start = prepare(tile_coords[0].T, tile_mask, pair_orbs, place, own, cycle_factor)
     message, held = intermediate(table, own, other, cycle_rows, start, cores=cores)
     factor = ladder_factor[0]
-    outgoing = ladder(table, held, factor, far=True, out_dtype=jnp.bfloat16)
-
-    classes = pairs // 2
-    even = classes & (classes - 1) == 0
-
-    def within(p, k):
-        return p // classes * classes + (p % classes ^ k if even else (p % classes + k) % classes)
-
-    def permute(value, k, far_core):
-        routes = []
-        for p in range(pairs):
-            for core in range(cores):
-                if core != far_core:
-                    routes.append((p * cores + core, within(p, k) * cores + core))
-                elif k == classes - 1:
-                    routes.append((p * cores + core, (p + classes) % pairs * cores + core))
+
+    def exchange(value, first_core, second_core):
+        partners = (first_core, second_core)
+        routes = [(p * 2 + c, (p ^ partners[c]) * 2 + c) for p in range(pairs) for c in range(2)]
         return lax.ppermute(value, ("pair", "virt"), routes)
 
-    if 2 <= classes <= 4:
-        arrivals = [permute(message, k, 0) for k in range(1, classes)]
-        arrivals, outgoing = lax.optimization_barrier((arrivals, outgoing))
-        arrived = lax.ppermute(outgoing, "virt", swap)
-        middle = add_arrivals(table, message, arrivals, plain=0, labelled=True)
-        middle, held = lax.optimization_barrier((middle, held))
-        near = ladder(table, held, factor, far=False, out_dtype=jnp.float32)
-        arrivals = [permute(middle, k, 1) for k in range(1, classes)]
-        arrivals, near = lax.optimization_barrier((arrivals, near))
-        sums = add_arrivals(table, middle, arrivals, plain=1, labelled=False)
+    if square:
+        arrival = exchange(message, 4, 1)
+        left, far_a = ladder_first(table, held, factor)
+        arrival, left = lax.optimization_barrier((arrival, left))
+        kept, message = step(table, next_orbs, message, arrival, plain=0)
+        message, left = lax.optimization_barrier((message, left))
+        arrival = exchange(message, 1, 2)
+        left, far_b = ladder_second(table, held, factor, left)
+        arrival, left = lax.optimization_barrier((arrival, left))
+        kept, message = step(table, next_orbs, kept, arrival, plain=1)
+        message, left, far_a, far_b = lax.optimization_barrier((message, left, far_a, far_b))
+        arrival = exchange(message, 2, 4)
+        arrived = [lax.ppermute(far, "virt", swap) for far in (far_a, far_b)]
+        near = ladder_third(table, factor, left, held.shape[1])
+        arrival, near = lax.optimization_barrier((arrival, near))
+        sums = last_step(kept, arrival)
     else:
-        arrived = lax.ppermute(outgoing, "virt", swap)
-        near = ladder(table, held, factor, far=False, out_dtype=jnp.float32)
+        left, far_a = ladder_first(table, held, factor)
+        left, far_b = ladder_second(table, held, factor, left)
+        near = ladder_third(table, factor, left, held.shape[1])
+        arrived = [lax.ppermute(far, "virt", swap) for far in (far_a, far_b)]
         width = factor.shape[0]
         right = pair_orbs[0, 1]
         occupied = jnp.arange(cycle_factor.shape[0], dtype=jnp.int32) == right

time: 35.3 us -> 30.6 us (0.87)
  starting transfers between devices: 15.9 us -> 8.34 us
  waiting for transfers between devices: 1.45 us -> 5.97 us
  Pallas kernels: 17.4 us -> 15.8 us
    ppermute x7 -> x6, starting transfers between devices: 15.3 us -> 7.82 us  [the longest x3 4.68 us: exchange(): return lax.ppermute(value, ('pair', 'virt'), routes)]
    ppermute x7 -> x6, waiting for transfers between devices: 0.02 us -> 4.54 us  [the longest x3 4.53 us: exchange(): return lax.ppermute(value, ('pair', 'virt'), routes)]
    pallas_call x4 -> x6, Pallas kernels: 13.1 us -> 11.5 us  [the longest x3 11.1 us: ladder_call(): pl.pallas_call(body, out_shape=[jax.ShapeDtypeStruct(shape, jnp.bfloat16)...]
  transfers between devices with their start and end apart: 9 -> 8, of which waited for: 1 -> 3; matrix products, arithmetic and copies ran while one was open for 0% -> 0% of each run, Pallas kernels for 44% -> 45%
where the time goes in v3:
time: 30.6 us; the launch traced here: 30.4 us
  Pallas kernels  15.8 us (52%)
  starting transfers between devices  8.34 us (27%)
  waiting for transfers between devices  5.97 us (20%)
    pallas_call x3, Pallas kernels, ladder_call(): pl.pallas_call(body, out_shape=[jax.ShapeDtypeStruct(shape, jnp.bfloat16)...  11.1 us
    ppermute x3, starting transfers between devices, exchange(): return lax.ppermute(value, ('pair', 'virt'), routes)  4.68 us
    ppermute x3, waiting for transfers between devices, exchange(): return lax.ppermute(value, ('pair', 'virt'), routes)  4.53 us
    ppermute x1, starting transfers between devices, shards(): lax.ppermute(pair_orbs, 'pair', [(p, p ^ 2) for p in range(pairs)])  2.57 us
    pallas_call x1, Pallas kernels, prepare(): pl.pallas_call(body, out_shape=[pltpu.SMEM((7, places), jnp.int32), jax.S...  2.28 us
    pallas_call x1, Pallas kernels, finish(): pl.pallas_call(body, out_shape=jax.ShapeDtypeStruct((half, width), jnp.bf...  1.78 us
    ppermute x1, waiting for transfers between devices, shards(): other_sums = lax.ppermute(sums, 'virt', swap)  1.43 us
  transfers between devices with their start and end apart: 8, of which 3 were waited for; matrix products, arithmetic and copies ran while one was open for 0% of the time, Pallas kernels for 45%

profile of v3, /device:TPU:0, one launch (start us, length us, event | category | flops | bytes accessed | tf_op | source)
XLA Modules:
  0.0 30.4 jit_solution(11806358647813732075)
XLA Ops:
  0.0 0.5 %collective-permute-start.1 = (bf16[8,128,128]{2,1,0:T(8,128)(2,1)}, bf16[8,128,128]{2,1,0:T(8,128)(2,1)S(1)}, u32[]{:S(2)}, u32[]{:S(2)}) collective-permute-start(bf16[8,128,128]{2,1,0:T(8,128)(2,1)} %bitcast.10), channel_id=1, source_target_pairs={{0,1},{1,0},{2,3},{3,2},{4,5},{5,4},{6,7},{7,6},{8,9},{9,8},{10,11... | collective-permute-start | bytes 786440 | tf_op jit(solution)/shard_map/ppermute | solution.py:381
  0.5 2.6 %collective-permute-start = (s32[1,2]{1,0:T(1,128)}, s32[1,2]{1,0:T(1,128)S(1)}, u32[]{:S(2)}, u32[]{:S(2)}) collective-permute-start(s32[1,2]{1,0:T(1,128)} %orbs.1), channel_id=1, source_target_pairs={{0,4},{2,6},{4,0},{6,2},{8,12},{10,14},{12,8},{14,10},{1,5},{3,7},... | collective-permute-start | bytes 32 | tf_op jit(solution)/shard_map/ppermute | solution.py:384
  3.0 0.0 copy-start
  3.0 2.3 %prepare.1 = (s32[7,17]{1,0:T(8,128)S(4)}, bf16[8,128,128]{2,1,0:T(8,128)(2,1)S(1)}, bf16[1536,128]{1,0:T(8,128)(2,1)S(1)}, f32[128,1536]{1,0:T(8,128)S(1)}) custom-call(s32[2,16]{1,0:T(2,128)} %bitcast.12, s32[1,16]{1,0:T(1,128)} %mask.1, s32[1,2]{1,0:T(1,128)} %orbs.1, s32[1]{0:T(128)} %bitcast.2.place, bf16[8,128,128]{2,1,0:T(8,128)(2,1)} %bitcast.11, ...), custom_call_target="tpu_custom_call" | custom-call | tf_op jit(solution)/shard_map/prepare/pallas_call | solution.py:110
  5.3 0.0 collective-permute-done.1.other
  5.3 0.3 %intermediate.1 = (bf16[64,1664]{1,0:T(8,128)(2,1)S(1)}, bf16[17,128,128]{2,1,0:T(8,128)(2,1)S(1)}) custom-call(s32[7,17]{1,0:T(8,128)S(4)} %get-tuple-element.31.table, bf16[8,128,128]{2,1,0:T(8,128)(2,1)S(1)} %get-tuple-element.32.own, bf16[8,128,128]{2,1,0:T(8,128)(2,1)S(1)} %collective-permute-done.1.other, ...), custom_call_target="tpu_custom_call" | custom-call | tf_op jit(solution)/shard_map/intermediate/pallas_call | solution.py:147
  5.7 2.6 %collective-permute-start.2 = (bf16[64,1664]{1,0:T(8,128)(2,1)S(1)}, bf16[64,1664]{1,0:T(8,128)(2,1)S(1)}, u32[]{:S(2)}, u32[]{:S(2)}) collective-permute-start(bf16[64,1664]{1,0:T(8,128)(2,1)S(1)} %get-tuple-element.35.mine), channel_id=1, source_target_pairs={{0,8},{1,3},{2,10},{3,1},{4,12},{5,7},{6,14},{7,5},{8,0},{9,11},{1... | collective-permute-start | bytes 638984 | tf_op jit(solution)/shard_map/ppermute | solution.py:392
  8.3 0.0 copy-done
  8.3 4.0 %ladder.3 = (bf16[768,1536]{1,0:T(8,128)(2,1)S(1)}, bf16[1,768,768]{2,1,0:T(8,128)(2,1)S(1)}) custom-call(s32[7,17]{1,0:T(8,128)S(4)} %get-tuple-element.31.table, bf16[17,128,128]{2,1,0:T(8,128)(2,1)S(1)} %get-tuple-element.36.held, bf16[1536,1536]{1,0:T(8,128)(2,1)S(1)} %bitcast.7), custom_call_target="tpu_custom_call" | custom-call | flops 10000000000 | bytes 1 | tf_op jit(solution)/shard_map/ladder/pallas_call | solution.py:321
  12.3 2.0 %collective-permute-done.2.arrival = bf16[64,1664]{1,0:T(8,128)(2,1)S(1)} collective-permute-done((bf16[64,1664]{1,0:T(8,128)(2,1)S(1)}, bf16[64,1664]{1,0:T(8,128)(2,1)S(1)}, u32[]{:S(2)}, u32[]{:S(2)}) %collective-permute-start.2) | collective-permute-done | bytes 213024 | tf_op jit(solution)/shard_map/ppermute | solution.py:392
  14.3 0.0 collective-permute-done.next_orbs
  14.3 0.1 step.2
  14.5 2.0 %collective-permute-start.3 = (bf16[64,1664]{1,0:T(8,128)(2,1)S(1)}, bf16[64,1664]{1,0:T(8,128)(2,1)S(1)}, u32[]{:S(2)}, u32[]{:S(2)}) collective-permute-start(bf16[64,1664]{1,0:T(8,128)(2,1)S(1)} %get-tuple-element.42), channel_id=1, source_target_pairs={{0,2},{1,5},{2,0},{3,7},{4,6},{5,1},{6,4},{7,3},{8,10},{9,13},{10,... | collective-permute-start | bytes 638984 | tf_op jit(solution)/shard_map/ppermute | solution.py:392
  16.4 4.2 %ladder.4 = (bf16[768,1536]{1,0:T(8,128)(2,1)S(1)}, bf16[1,768,768]{2,1,0:T(8,128)(2,1)S(1)}) custom-call(s32[7,17]{1,0:T(8,128)S(4)} %get-tuple-element.31.table, bf16[17,128,128]{2,1,0:T(8,128)(2,1)S(1)} %get-tuple-element.36.held, bf16[1536,1536]{1,0:T(8,128)(2,1)S(1)} %bitcast.8, bf16[768,1536]{1,0:T(8,128)(2,1)S(1)} %get-tuple-element.43.left_far), custom_call_target="tpu_custom_call" | custom-call | flops 10000000000 | bytes 1 | tf_op jit(solution)/shard_map/ladder/pallas_call | solution.py:321
  20.6 0.0 collective-permute-done.3.arrival
  20.6 0.2 step.3
  20.9 0.1 collective-permute-start.4
  21.0 0.1 collective-permute-start.6
  21.0 0.5 %collective-permute-start.7 = (bf16[1,768,768]{2,1,0:T(8,128)(2,1)S(1)}, bf16[1,768,768]{2,1,0:T(8,128)(2,1)S(1)}, u32[]{:S(2)}, u32[]{:S(2)}) collective-permute-start(bf16[1,768,768]{2,1,0:T(8,128)(2,1)S(1)} %get-tuple-element.56), channel_id=1, source_target_pairs={{0,1},{1,0},{2,3},{3,2},{4,5},{5,4},{6,7},{7,6},{8,9},{9,8},{10,11... | collective-permute-start | bytes 3538952 | tf_op jit(solution)/shard_map/ppermute | solution.py:406
  21.5 2.9 %ladder.5.near = bf16[2,768,768]{2,1,0:T(8,128)(2,1)S(1)} custom-call(s32[7,17]{1,0:T(8,128)S(4)} %get-tuple-element.31.table, bf16[1536,1536]{1,0:T(8,128)(2,1)S(1)} %bitcast.9, bf16[768,1536]{1,0:T(8,128)(2,1)S(1)} %get-tuple-element.52.left), custom_call_target="tpu_custom_call" | custom-call | flops 40000000000 | bytes 1 | tf_op jit(solution)/shard_map/ladder/pallas_call | solution.py:321
  24.4 2.5 %collective-permute-done.4.arrival = bf16[64,1664]{1,0:T(8,128)(2,1)S(1)} collective-permute-done((bf16[64,1664]{1,0:T(8,128)(2,1)S(1)}, bf16[64,1664]{1,0:T(8,128)(2,1)S(1)}, u32[]{:S(2)}, u32[]{:S(2)}) %collective-permute-start.4) | collective-permute-done | bytes 213024 | tf_op jit(solution)/shard_map/ppermute | solution.py:392
  27.0 0.1 collective-permute-start.5
  27.1 1.4 %collective-permute-done.5.other_sums = bf16[64,1536]{1,0:T(8,128)(2,1)S(1)} collective-permute-done((bf16[64,1536]{1,0:T(8,128)(2,1)S(1)}, bf16[64,1536]{1,0:T(8,128)(2,1)S(1)}, u32[]{:S(2)}, u32[]{:S(2)}) %collective-permute-start.5) | collective-permute-done | bytes 196640 | tf_op jit(solution)/shard_map/ppermute | solution.py:422
  28.5 0.0 collective-permute-done.6.far_a
  28.5 0.0 collective-permute-done.7.far_b
  28.5 1.8 %finish.1 = bf16[768,1536]{1,0:T(8,128)(2,1)} custom-call(s32[7,17]{1,0:T(8,128)S(4)} %get-tuple-element.31.table, bf16[64,1536]{1,0:T(8,128)(2,1)S(1)} %last_step.1.sums, bf16[64,1536]{1,0:T(8,128)(2,1)S(1)} %collective-permute-done.5.other_sums, bf16[2,768,768]{2,1,0:T(8,128)(2,1)S(1)} %ladder.5.near, ...), custom_call_target="tpu_custom_call" | custom-call | tf_op jit(solution)/shard_map/finish/pallas_call | solution.py:360
  (1 shorter events, 0.0 us)
Async XLA Ops:
  0.0 5.3 %collective-permute-start.1 = (bf16[8,128,128]{2,1,0:T(8,128)(2,1)}, bf16[8,128,128]{2,1,0:T(8,128)(2,1)S(1)}, u32[]{:S(2)}, u32[]{:S(2)}) collective-permute-start(bf16[8,128,128]{2,1,0:T(8,128)(2,1)} %bitcast.10), channel_id=1, source_target_pairs={{0,1},{1,0},{2,3},{3,2},{4,5},{5,4},{6,7},{7,6},{8,9},{9,8},{10,11... | collective-permute-start | bytes 786440 | tf_op jit(solution)/shard_map/ppermute | solution.py:381
  0.5 13.9 %collective-permute-start = (s32[1,2]{1,0:T(1,128)}, s32[1,2]{1,0:T(1,128)S(1)}, u32[]{:S(2)}, u32[]{:S(2)}) collective-permute-start(s32[1,2]{1,0:T(1,128)} %orbs.1), channel_id=1, source_target_pairs={{0,4},{2,6},{4,0},{6,2},{8,12},{10,14},{12,8},{14,10},{1,5},{3,7},... | collective-permute-start | bytes 32 | tf_op jit(solution)/shard_map/ppermute | solution.py:384
  3.0 5.3 %copy-start = (bf16[1,1536,1536]{2,1,0:T(8,128)(2,1)S(1)}, bf16[1,1536,1536]{2,1,0:T(8,128)(2,1)}, u32[]{:S(2)}) copy-start(bf16[1,1536,1536]{2,1,0:T(8,128)(2,1)} %param.10) | copy-start | bytes 14155780
  5.7 8.7 %collective-permute-start.2 = (bf16[64,1664]{1,0:T(8,128)(2,1)S(1)}, bf16[64,1664]{1,0:T(8,128)(2,1)S(1)}, u32[]{:S(2)}, u32[]{:S(2)}) collective-permute-start(bf16[64,1664]{1,0:T(8,128)(2,1)S(1)} %get-tuple-element.35.mine), channel_id=1, source_target_pairs={{0,8},{1,3},{2,10},{3,1},{4,12},{5,7},{6,14},{7,5},{8,0},{9,11},{1... | collective-permute-start | bytes 638984 | tf_op jit(solution)/shard_map/ppermute | solution.py:392
  14.5 6.2 %collective-permute-start.3 = (bf16[64,1664]{1,0:T(8,128)(2,1)S(1)}, bf16[64,1664]{1,0:T(8,128)(2,1)S(1)}, u32[]{:S(2)}, u32[]{:S(2)}) collective-permute-start(bf16[64,1664]{1,0:T(8,128)(2,1)S(1)} %get-tuple-element.42), channel_id=1, source_target_pairs={{0,2},{1,5},{2,0},{3,7},{4,6},{5,1},{6,4},{7,3},{8,10},{9,13},{10,... | collective-permute-start | bytes 638984 | tf_op jit(solution)/shard_map/ppermute | solution.py:392
  20.9 6.1 %collective-permute-start.4 = (bf16[64,1664]{1,0:T(8,128)(2,1)S(1)}, bf16[64,1664]{1,0:T(8,128)(2,1)S(1)}, u32[]{:S(2)}, u32[]{:S(2)}) collective-permute-start(bf16[64,1664]{1,0:T(8,128)(2,1)S(1)} %get-tuple-element.51), channel_id=1, source_target_pairs={{0,4},{1,9},{2,6},{3,11},{4,0},{5,13},{6,2},{7,15},{8,12},{9,1},{1... | collective-permute-start | bytes 638984 | tf_op jit(solution)/shard_map/ppermute | solution.py:392
  21.0 7.5 %collective-permute-start.6 = (bf16[1,768,768]{2,1,0:T(8,128)(2,1)S(1)}, bf16[1,768,768]{2,1,0:T(8,128)(2,1)S(1)}, u32[]{:S(2)}, u32[]{:S(2)}) collective-permute-start(bf16[1,768,768]{2,1,0:T(8,128)(2,1)S(1)} %get-tuple-element.55), channel_id=1, source_target_pairs={{0,1},{1,0},{2,3},{3,2},{4,5},{5,4},{6,7},{7,6},{8,9},{9,8},{10,11... | collective-permute-start | bytes 3538952 | tf_op jit(solution)/shard_map/ppermute | solution.py:406
  21.0 7.5 %collective-permute-start.7 = (bf16[1,768,768]{2,1,0:T(8,128)(2,1)S(1)}, bf16[1,768,768]{2,1,0:T(8,128)(2,1)S(1)}, u32[]{:S(2)}, u32[]{:S(2)}) collective-permute-start(bf16[1,768,768]{2,1,0:T(8,128)(2,1)S(1)} %get-tuple-element.56), channel_id=1, source_target_pairs={{0,1},{1,0},{2,3},{3,2},{4,5},{5,4},{6,7},{7,6},{8,9},{9,8},{10,11... | collective-permute-start | bytes 3538952 | tf_op jit(solution)/shard_map/ppermute | solution.py:406
  27.0 1.5 %collective-permute-start.5 = (bf16[64,1536]{1,0:T(8,128)(2,1)S(1)}, bf16[64,1536]{1,0:T(8,128)(2,1)S(1)}, u32[]{:S(2)}, u32[]{:S(2)}) collective-permute-start(bf16[64,1536]{1,0:T(8,128)(2,1)S(1)} %last_step.1.sums), channel_id=1, source_target_pairs={{0,1},{1,0},{2,3},{3,2},{4,5},{5,4},{6,7},{7,6},{8,9},{9,8},{10,11... | collective-permute-start | bytes 589832 | tf_op jit(solution)/shard_map/ppermute | solution.py:422

commit v4 on v3

v4 whole, which is shorter than its diff:
```python
import functools

import jax
import jax.numpy as jnp
from jax import lax
from jax.experimental import pallas as pl
from jax.experimental.pallas import tpu as pltpu
from jax.sharding import PartitionSpec as P

LANES = 128
SMEM = pl.BlockSpec(memory_space=pltpu.SMEM)
VMEM = pl.BlockSpec(memory_space=pltpu.VMEM)
HBM = pl.BlockSpec(memory_space=pltpu.HBM)
FIRST_FIRST = (((0,), (0,)), ((), ()))
LAST_LAST = (((1,), (1,)), ((), ()))
COLUMN, ROW, KEPT, SORTED, NAME, BEGIN, FACTS = range(7)
USED, CORE, ORBITAL = range(3)


def params(mib):
    return pltpu.CompilerParams(vmem_limit_bytes=mib * 2**20)


def block(index, size):
    return pl.ds(pl.multiple_of(index * size, size), size)


def in_hbm(array):
    return pltpu.with_memory_space_constraint(array, pltpu.HBM)


def in_smem(array):
    return pltpu.with_memory_space_constraint(array, pltpu.SMEM)


def add_terms(total, table, rows, tiles, slots):
    size = tiles.shape[1]
    terms = [
        lax.dot_general(
            rows[block(table[COLUMN, s], size), :], tiles[k], FIRST_FIRST, preferred_element_type=jnp.float32
        )
        for k, s in enumerate(slots)
    ]
    for s, term in zip(slots, terms):
        total[:, block(table[ROW, s], size)] += term * table[KEPT, s].astype(jnp.float32)


def prepare(coords, mask, orbs, place, own, cycle_factor):
    slots = coords.shape[1]
    local, tile = own.shape[0], own.shape[1]
    width, aux = cycle_factor.shape[1:]
    tiles = width // tile
    places = max(slots + 1, tiles + 3)

    def body(coords, mask, orbs, place, own, factor, table, held, rows, total, s_coords, s_mask, s_orbs, count, sems):
        loads = [
            pltpu.make_async_copy(source, target, sems.at[n])
            for n, (source, target) in enumerate([(orbs, s_orbs), (coords, s_coords), (mask, s_mask), (own, held)])
        ]
        for load in loads:
            load.start()
        core = place[0]
        total[...] = jnp.zeros_like(total)
        loads[0].wait()
        load_rows = pltpu.make_async_copy(factor.at[s_orbs[0, 0]], rows, sems.at[4])
        load_rows.start()
        table[FACTS, CORE] = core
        table[FACTS, ORBITAL] = s_orbs[0, 1]

        for n in range(tiles):
            count[n] = 0
        loads[1].wait()
        loads[2].wait()
        for s in range(slots):
            g = lax.rem(s + core * local, slots)
            d, kept = s_coords[1, g], s_mask[0, g]
            table[COLUMN, s] = s_coords[0, g]
            table[ROW, s] = d
            table[KEPT, s] = kept
            table[SORTED, s] = slots
            count[d] += (kept != 0).astype(jnp.int32)
        table[COLUMN, slots] = 0
        begin, used = jnp.int32(0), jnp.int32(0)
        for n in range(tiles):
            here = count[n]
            table[NAME, used] = n
            table[BEGIN, used] = begin
            count[n] = begin
            begin += here
            used += (here > 0).astype(jnp.int32)
        table[FACTS, USED] = used
        for n in range(3):
            table[NAME, used + n] = 0
            table[BEGIN, used + n] = begin
        for s in range(slots):
            d = table[ROW, s]
            at = count[d]
            kept = table[KEPT, s] != 0
            table[SORTED, jnp.where(kept, at, slots)] = s
            count[d] = at + kept.astype(jnp.int32)
        loads[3].wait()
        load_rows.wait()
        add_terms(total, table, rows, held, range(local))

    return pl.pallas_call(
        body,
        out_shape=[
            pltpu.SMEM((7, places), jnp.int32),
            jax.ShapeDtypeStruct(own.shape, own.dtype),
            jax.ShapeDtypeStruct((width, aux), jnp.bfloat16),
            jax.ShapeDtypeStruct((aux, width), jnp.float32),
        ],
        in_specs=[HBM, HBM, HBM, SMEM, HBM, HBM],
        out_specs=[SMEM, VMEM, VMEM, VMEM],
        scratch_shapes=[
            pltpu.SMEM(coords.shape, jnp.int32),
            pltpu.SMEM(mask.shape, jnp.int32),
            pltpu.SMEM(orbs.shape, jnp.int32),
            pltpu.SMEM((tiles,), jnp.int32),
            pltpu.SemaphoreType.DMA((5,)),
        ],
        compiler_params=params(16),
        name="prepare",
    )(in_hbm(coords), in_hbm(mask), in_hbm(orbs), place, in_hbm(own), in_hbm(cycle_factor))


def intermediate(table, own, other, rows, start, *, cores):
    local, tile = own.shape[0], own.shape[1]
    aux, width = start.shape
    share = aux // cores

    def body(table, own, other, rows, start, out, held, total):
        total[...] = start[...]
        add_terms(total, table, rows, other, range(local, 2 * local))
        out[:, :width] = total[block(table[FACTS, CORE], share), :].astype(out.dtype)
        label = jnp.zeros((share, LANES), jnp.float32) + table[FACTS, ORBITAL].astype(jnp.float32)
        out[:, width:] = label.astype(out.dtype)
        held[:local] = own[...]
        held[local : 2 * local] = other[...]
        held[2 * local] = jnp.zeros((tile, tile), held.dtype)

    return pl.pallas_call(
        body,
        out_shape=[
            jax.ShapeDtypeStruct((share, width + LANES), jnp.bfloat16),
            jax.ShapeDtypeStruct((2 * local + 1, tile, tile), jnp.bfloat16),
        ],
        in_specs=[SMEM, VMEM, VMEM, VMEM, VMEM],
        out_specs=[VMEM, VMEM],
        scratch_shapes=[pltpu.VMEM((aux, width), jnp.float32)],
        compiler_params=params(16),
        name="intermediate",
    )(in_smem(table), own, other, rows, start)


def step(table, next_orbs, mine, arrival, *, plain):
    share, full = arrival.shape
    width = full - LANES

    def body(table, next_orbs, mine, arrival, kept, out):
        value = mine[:, :width].astype(jnp.float32)
        extra = arrival[:, :width].astype(jnp.float32)
        own = jnp.zeros((share, LANES), jnp.float32) + table[FACTS, ORBITAL].astype(jnp.float32)
        out[:, width:] = own.astype(out.dtype)

        @pl.when(table[FACTS, CORE] == plain)
        def _():
            total = value + extra
            kept[...] = total
            out[:, :width] = total.astype(out.dtype)

        @pl.when(table[FACTS, CORE] != plain)
        def _():
            label = own[:, :1]
            theirs = arrival[:, width : width + 1].astype(jnp.float32)
            behind = next_orbs[0:1, 1:2].astype(jnp.float32)
            kept[...] = value + jnp.where(theirs == label, extra, 0.0)
            out[:, :width] = (
                jnp.where(label == behind, value, 0.0) + jnp.where(theirs == behind, extra, 0.0)
            ).astype(out.dtype)

    return pl.pallas_call(
        body,
        out_shape=[
            jax.ShapeDtypeStruct((share, width), jnp.float32),
            jax.ShapeDtypeStruct((share, full), arrival.dtype),
        ],
        in_specs=[SMEM, VMEM, VMEM, VMEM],
        out_specs=[VMEM, VMEM],
        compiler_params=params(16),
        name="step",
    )(in_smem(table), next_orbs, mine, arrival)


def last_step(mine, arrival):
    width = mine.shape[1]

    def body(mine, arrival, out):
        out[...] = (mine[...] + arrival[:, :width].astype(jnp.float32)).astype(out.dtype)

    return pl.pallas_call(
        body,
        out_shape=jax.ShapeDtypeStruct(mine.shape, arrival.dtype),
        in_specs=[VMEM, VMEM],
        out_specs=VMEM,
        compiler_params=params(16),
        name="last_step",
    )(mine, arrival)


def ladder_build(table, held, factor):
    empty, tile = held.shape[0] - 1, held.shape[1]
    width = factor.shape[0]
    pairs = -(-(width // tile) // 2)

    def body(table, held, factor, left, wide):
        def two_tiles(m, carry):
            first, second, end = [table[BEGIN, 2 * m + k] for k in range(3)]
            here = block(m, 2 * tile)

            def product(at, count):
                columns, weights = [], []
                for k in range(count):
                    s = jnp.where(at + k < end, table[SORTED, jnp.minimum(at + k, empty)], empty)
                    columns.append(factor[:, block(table[COLUMN, s], tile)])
                    value, none = held[s], jnp.zeros((tile, tile), held.dtype)
                    early = at + k < second
                    weights.append(
                        jnp.concatenate([jnp.where(early, value, none), jnp.where(early, none, value)], axis=1)
                    )
                return jnp.dot(
                    jnp.concatenate(columns, axis=1), jnp.concatenate(weights, axis=0),
                    preferred_element_type=jnp.float32,
                )

            rounds = (end - first + 1) // 2
            for n in range(1, 4):

                @pl.when(rounds == n)
                def _():
                    left[:, here] = product(first, 2 * n).astype(left.dtype)

            @pl.when(rounds > 3)
            def _():
                wide[...] = product(first, 2)

                def add(t, carry):
                    wide[...] += product(first + 2 * t, 2)
                    return carry

                lax.fori_loop(1, rounds, add, 0)
                left[:, here] = wide[...].astype(left.dtype)

            return carry

        lax.fori_loop(0, (table[FACTS, USED] + 1) // 2, two_tiles, 0)

    wide = pltpu.VMEM((width, 2 * tile), jnp.float32)
    return ladder_call(body, (width, 2 * pairs * tile), [wide], in_smem(table), held, factor, flops=10**10)


def ladder_multiply(table, left, factor, tile, *, far, flops):
    half = left.shape[0] // 2

    def body(table, left, factor, out):
        core = table[FACTS, CORE]
        rows = block(1 - core if far else core, half)
        steps = (table[FACTS, USED] + 1) // 2
        for n in range(factor.shape[0] // tile // 2 + 1):

            @pl.when(steps == n)
            def _():
                def unit(k, carry):
                    if n == 0:
                        out[k] = jnp.zeros((half, half), out.dtype)
                        return carry
                    here = block(k, half)
                    right = jnp.concatenate(
                        [factor[here, block(table[NAME, w], tile)] for w in range(2 * n)], axis=1
                    )
                    out[k] = lax.dot_general(
                        left[rows, : 2 * n * tile], right, LAST_LAST, preferred_element_type=jnp.float32
                    ).astype(out.dtype)
                    return carry

                lax.fori_loop(0, 2, unit, 0)

    return ladder_call(body, (2, half, half), [], in_smem(table), left, factor, flops=flops)


def ladder_call(body, shape, scratch, *operands, flops):
    return pl.pallas_call(
        body,
        out_shape=jax.ShapeDtypeStruct(shape, jnp.bfloat16),
        in_specs=[SMEM] + [VMEM] * (len(operands) - 1),
        out_specs=VMEM,
        scratch_shapes=scratch,
        compiler_params=params(32),
        cost_estimate=pl.CostEstimate(flops=flops, bytes_accessed=1, transcendentals=0),
        name="ladder",
    )(*operands)


def finish(table, sums, other_sums, near, arrived, cycle_rows, *, pieces):
    half, width = near.shape[1], 2 * near.shape[2]
    aux = cycle_rows.shape[1]
    share = sums.shape[0]
    rows = half // pieces

    def body(table, sums, other_sums, near, arrived, factor, out, low, done, sems):
        core = table[FACTS, CORE]
        low[block(core, share), :] = sums[...]
        low[block(1 - core, share), :] = other_sums[...]
        stores = []
        for n in range(pieces):
            here = slice(n * rows, (n + 1) * rows)
            term = jnp.dot(
                factor[pl.ds(pl.multiple_of(core * half + n * rows, rows), rows), :], low[...],
                preferred_element_type=jnp.float32,
            )
            for k in range(2):
                side = slice(k * half, (k + 1) * half)
                total = near[k, here, :].astype(jnp.float32) + arrived[k, here, :].astype(jnp.float32) + term[:, side]
                done[here, side] = total.astype(done.dtype)
            store = pltpu.make_async_copy(done.at[here, :], out.at[here, :], sems.at[n])
            store.start()
            stores.append(store)
        for store in stores:
            store.wait()

    return pl.pallas_call(
        body,
        out_shape=jax.ShapeDtypeStruct((half, width), jnp.bfloat16),
        in_specs=[SMEM] + [VMEM] * 5,
        out_specs=HBM,
        scratch_shapes=[
            pltpu.VMEM((aux, width), jnp.bfloat16),
            pltpu.VMEM((half, width), jnp.bfloat16),
            pltpu.SemaphoreType.DMA((pieces,)),
        ],
        compiler_params=params(32),
        name="finish",
    )(in_smem(table), sums, other_sums, near, arrived, cycle_rows)


def shards(amp_tiles, tile_coords, tile_mask, pair_orbs, ladder_factor, cycle_factor):
    cores, pairs = lax.axis_size("virt"), lax.axis_size("pair")
    assert cores == 2 and pairs % 2 == 0
    own = amp_tiles[0]
    place = lax.axis_index("virt").astype(jnp.int32).reshape(1)
    swap = [(0, 1), (1, 0)]
    other = lax.ppermute(own, "virt", swap)
    square = pairs == 8
    table, own, cycle_rows, start = prepare(tile_coords[0].T, tile_mask, pair_orbs, place, own, cycle_factor)
    message, held = intermediate(table, own, other, cycle_rows, start, cores=cores)
    factor = ladder_factor[0]
    tile = held.shape[1]

    def exchange(value, first_core, second_core):
        partners = (first_core, second_core)
        routes = [(p * 2 + c, (p ^ partners[c]) * 2 + c) for p in range(pairs) for c in range(2)]
        return lax.ppermute(value, ("pair", "virt"), routes)

    if square:
        arrival = exchange(message, 4, 2)
        message, pair_orbs, held, factor = lax.optimization_barrier((message, pair_orbs, held, factor))
        next_orbs = lax.ppermute(pair_orbs, "pair", [(p, p ^ 1) for p in range(pairs)])
        left = ladder_build(table, held, factor)
        arrival, left = lax.optimization_barrier((arrival, left))
        kept, message = step(table, next_orbs, message, arrival, plain=0)
        message, left = lax.optimization_barrier((message, left))
        arrival = exchange(message, 2, 1)
        far = ladder_multiply(table, left, factor, tile, far=True, flops=10**10)
        arrival, far = lax.optimization_barrier((arrival, far))
        kept, message = step(table, next_orbs, kept, arrival, plain=1)
        message, left, far = lax.optimization_barrier((message, left, far))
        arrival = exchange(message, 1, 4)
        arrived = lax.ppermute(far, "virt", swap)
        near = ladder_multiply(table, left, factor, tile, far=False, flops=4 * 10**10)
        arrival, near = lax.optimization_barrier((arrival, near))
        sums = last_step(kept, arrival)
    else:
        left = ladder_build(table, held, factor)
        far = ladder_multiply(table, left, factor, tile, far=True, flops=10**10)
        near = ladder_multiply(table, left, factor, tile, far=False, flops=10**10)
        arrived = lax.ppermute(far, "virt", swap)
        width = factor.shape[0]
        right = pair_orbs[0, 1]
        occupied = jnp.arange(cycle_factor.shape[0], dtype=jnp.int32) == right
        mine = message[:, :width].astype(jnp.float32)
        total = lax.psum(jnp.where(occupied[:, None, None], mine[None], 0.0), "pair")
        sums = lax.dynamic_index_in_dim(total, right, 0, keepdims=False).astype(jnp.bfloat16)

    other_sums = lax.ppermute(sums, "virt", swap)
    return finish(table, sums, other_sums, near, arrived, cycle_rows, pieces=4)[None]


def solution(mesh):
    in_specs = (
        P(("groups", "pair"), "virt", None, None),
        P(("groups", "pair"), None, None),
        P(("groups", "pair"), None),
        P(("groups", "pair"), None),
        P(("groups", "virt"), None, None),
        P("groups", None, None),
    )
    out_specs = P(("groups", "pair"), "virt", None)
    return jax.shard_map(shards, mesh=mesh, in_specs=in_specs, out_specs=out_specs, check_vma=False)
```

time: 30.6 us -> 28.6 us (0.935)
  Pallas kernels: 15.8 us -> 13.1 us
  starting transfers between devices: 8.34 us -> 10.3 us
  waiting for transfers between devices: 5.97 us -> 4.82 us
    ppermute x3, starting transfers between devices: 4.68 us -> 7.99 us  [exchange(): return lax.ppermute(value, ('pair', 'virt'), routes)]
    pallas_call x3, Pallas kernels: 11.1 us -> 7.97 us  [ladder_call(): pl.pallas_call(body, out_shape=jax.ShapeDtypeStruct(shape, jnp.bfloat16),...]
    ppermute x3 -> x2, starting transfers between devices: 3.14 us -> 1.49 us  [the longest x1 1.49 us: shards(): lax.ppermute(pair_orbs, 'pair', [(p, p ^ 1) for p in range(pairs)])]
    ppermute x3, waiting for transfers between devices: 4.53 us -> 3.63 us  [exchange(): return lax.ppermute(value, ('pair', 'virt'), routes)]
    pallas_call x1, Pallas kernels: 2.28 us -> 2.64 us  [prepare(): pl.pallas_call(body, out_shape=[pltpu.SMEM((7, places), jnp.int32), jax.S...]
  transfers between devices with their start and end apart: 8 -> 7, of which waited for: 3 -> 4; matrix products, arithmetic and copies ran while one was open for 0% -> 0% of each run, Pallas kernels for 45% -> 37%
where the time goes in v4:
time: 28.6 us; the launch traced here: 28.4 us
  Pallas kernels  13.1 us (46%)
  starting transfers between devices  10.3 us (36%)
  waiting for transfers between devices  4.82 us (17%)
    ppermute x3, starting transfers between devices, exchange(): return lax.ppermute(value, ('pair', 'virt'), routes)  7.99 us
    pallas_call x3, Pallas kernels, ladder_call(): pl.pallas_call(body, out_shape=jax.ShapeDtypeStruct(shape, jnp.bfloat16),...  7.97 us
    ppermute x3, waiting for transfers between devices, exchange(): return lax.ppermute(value, ('pair', 'virt'), routes)  3.63 us
    pallas_call x1, Pallas kernels, prepare(): pl.pallas_call(body, out_shape=[pltpu.SMEM((7, places), jnp.int32), jax.S...  2.64 us
    pallas_call x1, Pallas kernels, finish(): pl.pallas_call(body, out_shape=jax.ShapeDtypeStruct((half, width), jnp.bf...  1.77 us
    ppermute x1, starting transfers between devices, shards(): lax.ppermute(pair_orbs, 'pair', [(p, p ^ 1) for p in range(pairs)])  1.49 us
    ppermute x1, waiting for transfers between devices, shards(): other_sums = lax.ppermute(sums, 'virt', swap)  1.18 us
  transfers between devices with their start and end apart: 7, of which 4 were waited for; matrix products, arithmetic and copies ran while one was open for 0% of the time, Pallas kernels for 37%

profile of v4, /device:TPU:0, one launch (start us, length us, event | category | flops | bytes accessed | tf_op | source)
XLA Modules:
  0.0 28.4 jit_solution(6100864248177657024)
XLA Ops:
  0.0 0.5 %collective-permute-start = (bf16[8,128,128]{2,1,0:T(8,128)(2,1)}, bf16[8,128,128]{2,1,0:T(8,128)(2,1)S(1)}, u32[]{:S(2)}, u32[]{:S(2)}) collective-permute-start(bf16[8,128,128]{2,1,0:T(8,128)(2,1)} %bitcast.10), channel_id=1, source_target_pairs={{0,1},{1,0},{2,3},{3,2},{4,5},{5,4},{6,7},{7,6},{8,9},{9,8},{10,11... | collective-permute-start | bytes 786440 | tf_op jit(solution)/shard_map/ppermute | solution.py:352
  0.5 0.0 copy-start.1
  0.5 0.0 copy-start
  0.5 2.6 %prepare.1 = (s32[7,17]{1,0:T(8,128)S(4)}, bf16[8,128,128]{2,1,0:T(8,128)(2,1)S(1)}, bf16[1536,128]{1,0:T(8,128)(2,1)S(1)}, f32[128,1536]{1,0:T(8,128)S(1)}) custom-call(s32[2,16]{1,0:T(2,128)} %bitcast.12, s32[1,16]{1,0:T(1,128)} %mask.1, s32[1,2]{1,0:T(1,128)} %orbs.1, s32[1]{0:T(128)} %bitcast.2.place, bf16[8,128,128]{2,1,0:T(8,128)(2,1)} %bitcast.11, ...), custom_call_target="tpu_custom_call" | custom-call | tf_op jit(solution)/shard_map/prepare/pallas_call | solution.py:105
  3.1 0.0 collective-permute-done.other
  3.1 0.3 %intermediate.1 = (bf16[64,1664]{1,0:T(8,128)(2,1)S(1)}, bf16[17,128,128]{2,1,0:T(8,128)(2,1)S(1)}) custom-call(s32[7,17]{1,0:T(8,128)S(4)} %get-tuple-element.30.table, bf16[8,128,128]{2,1,0:T(8,128)(2,1)S(1)} %get-tuple-element.31.own, bf16[8,128,128]{2,1,0:T(8,128)(2,1)S(1)} %collective-permute-done.other, ...), custom_call_target="tpu_custom_call" | custom-call | tf_op jit(solution)/shard_map/intermediate/pallas_call | solution.py:142
  3.5 3.7 %collective-permute-start.2 = (bf16[64,1664]{1,0:T(8,128)(2,1)S(1)}, bf16[64,1664]{1,0:T(8,128)(2,1)S(1)}, u32[]{:S(2)}, u32[]{:S(2)}) collective-permute-start(bf16[64,1664]{1,0:T(8,128)(2,1)S(1)} %get-tuple-element.37.mine), channel_id=1, source_target_pairs={{0,8},{1,5},{2,10},{3,7},{4,12},{5,1},{6,14},{7,3},{8,0},{9,13},{1... | collective-permute-start | bytes 638984 | tf_op jit(solution)/shard_map/ppermute | solution.py:362
  7.1 0.0 copy-done.1
  7.1 1.5 %collective-permute-start.1 = (s32[1,2]{1,0:T(1,128)S(1)}, s32[1,2]{1,0:T(1,128)S(1)}, u32[]{:S(2)}, u32[]{:S(2)}) collective-permute-start(s32[1,2]{1,0:T(1,128)S(1)} %copy-done.1), channel_id=1, source_target_pairs={{0,2},{2,0},{4,6},{6,4},{8,10},{10,8},{12,14},{14,12},{1,3},{3,1},... | collective-permute-start | bytes 32 | tf_op jit(solution)/shard_map/ppermute | solution.py:367
  8.6 0.0 copy-done
  8.6 2.3 %ladder.3.left = bf16[1536,1536]{1,0:T(8,128)(2,1)S(1)} custom-call(s32[7,17]{1,0:T(8,128)S(4)} %get-tuple-element.30.table, bf16[17,128,128]{2,1,0:T(8,128)(2,1)S(1)} %get-tuple-element.38.held, bf16[1536,1536]{1,0:T(8,128)(2,1)S(1)} %bitcast.7), custom_call_target="tpu_custom_call" | custom-call | flops 10000000000 | bytes 1 | tf_op jit(solution)/shard_map/ladder/pallas_call | solution.py:292
  10.9 1.2 %collective-permute-done.2.arrival = bf16[64,1664]{1,0:T(8,128)(2,1)S(1)} collective-permute-done((bf16[64,1664]{1,0:T(8,128)(2,1)S(1)}, bf16[64,1664]{1,0:T(8,128)(2,1)S(1)}, u32[]{:S(2)}, u32[]{:S(2)}) %collective-permute-start.2) | collective-permute-done | bytes 213024 | tf_op jit(solution)/shard_map/ppermute | solution.py:362
  12.1 0.0 collective-permute-done.1.next_orbs
  12.1 0.1 step.2
  12.2 2.8 %collective-permute-start.3 = (bf16[64,1664]{1,0:T(8,128)(2,1)S(1)}, bf16[64,1664]{1,0:T(8,128)(2,1)S(1)}, u32[]{:S(2)}, u32[]{:S(2)}) collective-permute-start(bf16[64,1664]{1,0:T(8,128)(2,1)S(1)} %get-tuple-element.44), channel_id=1, source_target_pairs={{0,4},{1,3},{2,6},{3,1},{4,0},{5,7},{6,2},{7,5},{8,12},{9,11},{10,... | collective-permute-start | bytes 638984 | tf_op jit(solution)/shard_map/ppermute | solution.py:362
  15.0 2.9 %ladder.4 = bf16[2,768,768]{2,1,0:T(8,128)(2,1)S(1)} custom-call(s32[7,17]{1,0:T(8,128)S(4)} %get-tuple-element.30.table, bf16[1536,1536]{1,0:T(8,128)(2,1)S(1)} %ladder.3.left, bf16[1536,1536]{1,0:T(8,128)(2,1)S(1)} %bitcast.8), custom_call_target="tpu_custom_call" | custom-call | flops 10000000000 | bytes 1 | tf_op jit(solution)/shard_map/ladder/pallas_call | solution.py:292
  17.8 1.0 %collective-permute-done.3.arrival = bf16[64,1664]{1,0:T(8,128)(2,1)S(1)} collective-permute-done((bf16[64,1664]{1,0:T(8,128)(2,1)S(1)}, bf16[64,1664]{1,0:T(8,128)(2,1)S(1)}, u32[]{:S(2)}, u32[]{:S(2)}) %collective-permute-start.3) | collective-permute-done | bytes 213024 | tf_op jit(solution)/shard_map/ppermute | solution.py:362
  18.8 0.2 step.3
  19.0 1.6 %collective-permute-start.4 = (bf16[64,1664]{1,0:T(8,128)(2,1)S(1)}, bf16[64,1664]{1,0:T(8,128)(2,1)S(1)}, u32[]{:S(2)}, u32[]{:S(2)}) collective-permute-start(bf16[64,1664]{1,0:T(8,128)(2,1)S(1)} %get-tuple-element.50), channel_id=1, source_target_pairs={{0,2},{1,9},{2,0},{3,11},{4,6},{5,13},{6,4},{7,15},{8,10},{9,1},{1... | collective-permute-start | bytes 638984 | tf_op jit(solution)/shard_map/ppermute | solution.py:362
  20.6 0.0 collective-permute-start.6
  20.6 2.9 %ladder.5.near = bf16[2,768,768]{2,1,0:T(8,128)(2,1)S(1)} custom-call(s32[7,17]{1,0:T(8,128)S(4)} %get-tuple-element.30.table, bf16[1536,1536]{1,0:T(8,128)(2,1)S(1)} %ladder.3.left, bf16[1536,1536]{1,0:T(8,128)(2,1)S(1)} %bitcast.9), custom_call_target="tpu_custom_call" | custom-call | flops 40000000000 | bytes 1 | tf_op jit(solution)/shard_map/ladder/pallas_call | solution.py:292
  23.5 1.5 %collective-permute-done.4.arrival = bf16[64,1664]{1,0:T(8,128)(2,1)S(1)} collective-permute-done((bf16[64,1664]{1,0:T(8,128)(2,1)S(1)}, bf16[64,1664]{1,0:T(8,128)(2,1)S(1)}, u32[]{:S(2)}, u32[]{:S(2)}) %collective-permute-start.4) | collective-permute-done | bytes 213024 | tf_op jit(solution)/shard_map/ppermute | solution.py:362
  25.0 0.3 %collective-permute-start.5 = (bf16[64,1536]{1,0:T(8,128)(2,1)S(1)}, bf16[64,1536]{1,0:T(8,128)(2,1)S(1)}, u32[]{:S(2)}, u32[]{:S(2)}) collective-permute-start(bf16[64,1536]{1,0:T(8,128)(2,1)S(1)} %last_step.1.sums), channel_id=1, source_target_pairs={{0,1},{1,0},{2,3},{3,2},{4,5},{5,4},{6,7},{7,6},{8,9},{9,8},{10,11... | collective-permute-start | bytes 589832 | tf_op jit(solution)/shard_map/ppermute | solution.py:394
  25.3 1.2 %collective-permute-done.5.other_sums = bf16[64,1536]{1,0:T(8,128)(2,1)S(1)} collective-permute-done((bf16[64,1536]{1,0:T(8,128)(2,1)S(1)}, bf16[64,1536]{1,0:T(8,128)(2,1)S(1)}, u32[]{:S(2)}, u32[]{:S(2)}) %collective-permute-start.5) | collective-permute-done | bytes 196640 | tf_op jit(solution)/shard_map/ppermute | solution.py:394
  26.5 0.0 collective-permute-done.6.arrived
  26.5 1.8 %finish.1 = bf16[768,1536]{1,0:T(8,128)(2,1)} custom-call(s32[7,17]{1,0:T(8,128)S(4)} %get-tuple-element.30.table, bf16[64,1536]{1,0:T(8,128)(2,1)S(1)} %last_step.1.sums, bf16[64,1536]{1,0:T(8,128)(2,1)S(1)} %collective-permute-done.5.other_sums, bf16[2,768,768]{2,1,0:T(8,128)(2,1)S(1)} %ladder.5.near, ...), custom_call_target="tpu_custom_call" | custom-call | tf_op jit(solution)/shard_map/finish/pallas_call | solution.py:331
  (1 shorter events, 0.0 us)
Async XLA Ops:
  0.0 3.1 %collective-permute-start = (bf16[8,128,128]{2,1,0:T(8,128)(2,1)}, bf16[8,128,128]{2,1,0:T(8,128)(2,1)S(1)}, u32[]{:S(2)}, u32[]{:S(2)}) collective-permute-start(bf16[8,128,128]{2,1,0:T(8,128)(2,1)} %bitcast.10), channel_id=1, source_target_pairs={{0,1},{1,0},{2,3},{3,2},{4,5},{5,4},{6,7},{7,6},{8,9},{9,8},{10,11... | collective-permute-start | bytes 786440 | tf_op jit(solution)/shard_map/ppermute | solution.py:352
  0.5 6.7 %copy-start.1 = (s32[1,2]{1,0:T(1,128)S(1)}, s32[1,2]{1,0:T(1,128)}, u32[]{:S(2)}) copy-start(s32[1,2]{1,0:T(1,128)} %orbs.1) | copy-start | bytes 28
  0.5 8.1 %copy-start = (bf16[1,1536,1536]{2,1,0:T(8,128)(2,1)S(1)}, bf16[1,1536,1536]{2,1,0:T(8,128)(2,1)}, u32[]{:S(2)}) copy-start(bf16[1,1536,1536]{2,1,0:T(8,128)(2,1)} %param.10) | copy-start | bytes 14155780
  3.5 8.6 %collective-permute-start.2 = (bf16[64,1664]{1,0:T(8,128)(2,1)S(1)}, bf16[64,1664]{1,0:T(8,128)(2,1)S(1)}, u32[]{:S(2)}, u32[]{:S(2)}) collective-permute-start(bf16[64,1664]{1,0:T(8,128)(2,1)S(1)} %get-tuple-element.37.mine), channel_id=1, source_target_pairs={{0,8},{1,5},{2,10},{3,7},{4,12},{5,1},{6,14},{7,3},{8,0},{9,13},{1... | collective-permute-start | bytes 638984 | tf_op jit(solution)/shard_map/ppermute | solution.py:362
  7.1 4.9 %collective-permute-start.1 = (s32[1,2]{1,0:T(1,128)S(1)}, s32[1,2]{1,0:T(1,128)S(1)}, u32[]{:S(2)}, u32[]{:S(2)}) collective-permute-start(s32[1,2]{1,0:T(1,128)S(1)} %copy-done.1), channel_id=1, source_target_pairs={{0,2},{2,0},{4,6},{6,4},{8,10},{10,8},{12,14},{14,12},{1,3},{3,1},... | collective-permute-start | bytes 32 | tf_op jit(solution)/shard_map/ppermute | solution.py:367
  12.2 6.6 %collective-permute-start.3 = (bf16[64,1664]{1,0:T(8,128)(2,1)S(1)}, bf16[64,1664]{1,0:T(8,128)(2,1)S(1)}, u32[]{:S(2)}, u32[]{:S(2)}) collective-permute-start(bf16[64,1664]{1,0:T(8,128)(2,1)S(1)} %get-tuple-element.44), channel_id=1, source_target_pairs={{0,4},{1,3},{2,6},{3,1},{4,0},{5,7},{6,2},{7,5},{8,12},{9,11},{10,... | collective-permute-start | bytes 638984 | tf_op jit(solution)/shard_map/ppermute | solution.py:362
  19.0 5.9 %collective-permute-start.4 = (bf16[64,1664]{1,0:T(8,128)(2,1)S(1)}, bf16[64,1664]{1,0:T(8,128)(2,1)S(1)}, u32[]{:S(2)}, u32[]{:S(2)}) collective-permute-start(bf16[64,1664]{1,0:T(8,128)(2,1)S(1)} %get-tuple-element.50), channel_id=1, source_target_pairs={{0,2},{1,9},{2,0},{3,11},{4,6},{5,13},{6,4},{7,15},{8,10},{9,1},{1... | collective-permute-start | bytes 638984 | tf_op jit(solution)/shard_map/ppermute | solution.py:362
  20.6 5.9 %collective-permute-start.6 = (bf16[2,768,768]{2,1,0:T(8,128)(2,1)S(1)}, bf16[2,768,768]{2,1,0:T(8,128)(2,1)S(1)}, u32[]{:S(2)}, u32[]{:S(2)}) collective-permute-start(bf16[2,768,768]{2,1,0:T(8,128)(2,1)S(1)} %ladder.4), channel_id=1, source_target_pairs={{0,1},{1,0},{2,3},{3,2},{4,5},{5,4},{6,7},{7,6},{8,9},{9,8},{10,11... | collective-permute-start | bytes 7077896 | tf_op jit(solution)/shard_map/ppermute | solution.py:378
  25.0 1.5 %collective-permute-start.5 = (bf16[64,1536]{1,0:T(8,128)(2,1)S(1)}, bf16[64,1536]{1,0:T(8,128)(2,1)S(1)}, u32[]{:S(2)}, u32[]{:S(2)}) collective-permute-start(bf16[64,1536]{1,0:T(8,128)(2,1)S(1)} %last_step.1.sums), channel_id=1, source_target_pairs={{0,1},{1,0},{2,3},{3,2},{4,5},{5,4},{6,7},{7,6},{8,9},{9,8},{10,11... | collective-permute-start | bytes 589832 | tf_op jit(solution)/shard_map/ppermute | solution.py:394

commit v5 on v4

--- a/solution.py
+++ b/solution.py
@@ -7,7 +7,7 @@
 from jax.experimental.pallas import tpu as pltpu
 from jax.sharding import PartitionSpec as P
 
-LANES = 128
+LANES, LABEL = 128, 16
 SMEM = pl.BlockSpec(memory_space=pltpu.SMEM)
 VMEM = pl.BlockSpec(memory_space=pltpu.VMEM)
 HBM = pl.BlockSpec(memory_space=pltpu.HBM)
@@ -132,9 +132,12 @@
     def body(table, own, other, rows, start, out, held, total):
         total[...] = start[...]
         add_terms(total, table, rows, other, range(local, 2 * local))
-        out[:, :width] = total[block(table[FACTS, CORE], share), :].astype(out.dtype)
-        label = jnp.zeros((share, LANES), jnp.float32) + table[FACTS, ORBITAL].astype(jnp.float32)
-        out[:, width:] = label.astype(out.dtype)
+        for n in range(width // LANES):
+            out[n * share : (n + 1) * share, :] = total[
+                block(table[FACTS, CORE], share), n * LANES : (n + 1) * LANES
+            ].astype(out.dtype)
+        label = jnp.zeros((LABEL, LANES), jnp.float32) + table[FACTS, ORBITAL].astype(jnp.float32)
+        out[share * width // LANES :, :] = label.astype(out.dtype)
         held[:local] = own[...]
         held[local : 2 * local] = other[...]
         held[2 * local] = jnp.zeros((tile, tile), held.dtype)
@@ -142,7 +145,7 @@
     return pl.pallas_call(
         body,
         out_shape=[
-            jax.ShapeDtypeStruct((share, width + LANES), jnp.bfloat16),
+            jax.ShapeDtypeStruct((share * width // LANES + LABEL, LANES), jnp.bfloat16),
             jax.ShapeDtypeStruct((2 * local + 1, tile, tile), jnp.bfloat16),
         ],
         in_specs=[SMEM, VMEM, VMEM, VMEM, VMEM],
@@ -154,36 +157,35 @@
 
 
 def step(table, next_orbs, mine, arrival, *, plain):
-    share, full = arrival.shape
-    width = full - LANES
+    length = arrival.shape[0] - LABEL
 
     def body(table, next_orbs, mine, arrival, kept, out):
-        value = mine[:, :width].astype(jnp.float32)
-        extra = arrival[:, :width].astype(jnp.float32)
-        own = jnp.zeros((share, LANES), jnp.float32) + table[FACTS, ORBITAL].astype(jnp.float32)
-        out[:, width:] = own.astype(out.dtype)
+        value = mine[:length, :].astype(jnp.float32)
+        extra = arrival[:length, :].astype(jnp.float32)
+        own = jnp.zeros((LABEL, LANES), jnp.float32) + table[FACTS, ORBITAL].astype(jnp.float32)
+        out[length:, :] = own.astype(out.dtype)
 
         @pl.when(table[FACTS, CORE] == plain)
         def _():
             total = value + extra
             kept[...] = total
-            out[:, :width] = total.astype(out.dtype)
+            out[:length, :] = total.astype(out.dtype)
 
         @pl.when(table[FACTS, CORE] != plain)
         def _():
-            label = own[:, :1]
-            theirs = arrival[:, width : width + 1].astype(jnp.float32)
+            label = own[:1, :]
+            theirs = arrival[length : length + LABEL, :].astype(jnp.float32)[:1, :]
             behind = next_orbs[0:1, 1:2].astype(jnp.float32)
             kept[...] = value + jnp.where(theirs == label, extra, 0.0)
-            out[:, :width] = (
+            out[:length, :] = (
                 jnp.where(label == behind, value, 0.0) + jnp.where(theirs == behind, extra, 0.0)
             ).astype(out.dtype)
 
     return pl.pallas_call(
         body,
         out_shape=[
-            jax.ShapeDtypeStruct((share, width), jnp.float32),
-            jax.ShapeDtypeStruct((share, full), arrival.dtype),
+            jax.ShapeDtypeStruct((length, LANES), jnp.float32),
+            jax.ShapeDtypeStruct(arrival.shape, arrival.dtype),
         ],
         in_specs=[SMEM, VMEM, VMEM, VMEM],
         out_specs=[VMEM, VMEM],
@@ -193,10 +195,10 @@
 
 
 def last_step(mine, arrival):
-    width = mine.shape[1]
+    length = mine.shape[0]
 
     def body(mine, arrival, out):
-        out[...] = (mine[...] + arrival[:, :width].astype(jnp.float32)).astype(out.dtype)
+        out[...] = (mine[...] + arrival[:length, :].astype(jnp.float32)).astype(out.dtype)
 
     return pl.pallas_call(
         body,
@@ -256,44 +258,55 @@
         lax.fori_loop(0, (table[FACTS, USED] + 1) // 2, two_tiles, 0)
 
     wide = pltpu.VMEM((width, 2 * tile), jnp.float32)
-    return ladder_call(body, (width, 2 * pairs * tile), [wide], in_smem(table), held, factor, flops=10**10)
-
-
-def ladder_multiply(table, left, factor, tile, *, far, flops):
+    return ladder_call(body, [(width, 2 * pairs * tile)], [wide], in_smem(table), held, factor, flops=10**10)[0]
+
+
+def early_unit(core, steps):
+    return jnp.logical_and(core == 1, steps <= 4)
+
+
+def ladder_multiply(table, left, factor, tile, outputs, *, flops):
     half = left.shape[0] // 2
 
-    def body(table, left, factor, out):
+    def body(table, left, factor, *outs):
         core = table[FACTS, CORE]
-        rows = block(1 - core if far else core, half)
         steps = (table[FACTS, USED] + 1) // 2
         for n in range(factor.shape[0] // tile // 2 + 1):
 
             @pl.when(steps == n)
             def _():
-                def unit(k, carry):
-                    if n == 0:
-                        out[k] = jnp.zeros((half, half), out.dtype)
+                for (far, first, end, when), out in zip(outputs, outs):
+                    rows = block(1 - core if far else core, half)
+                    last = end
+                    if when is not None:
+                        chosen = early_unit(core, n) if when == "early" else jnp.logical_not(early_unit(core, n))
+                        last = jnp.where(chosen, end, first)
+
+                    def unit(k, carry):
+                        if n == 0:
+                            out[k - first] = jnp.zeros((half, half), out.dtype)
+                            return carry
+                        here = block(k, half)
+                        right = jnp.concatenate(
+                            [factor[here, block(table[NAME, w], tile)] for w in range(2 * n)], axis=1
+                        )
+                        out[k - first] = lax.dot_general(
+                            left[rows, : 2 * n * tile], right, LAST_LAST, preferred_element_type=jnp.float32
+                        ).astype(out.dtype)
                         return carry
-                    here = block(k, half)
-                    right = jnp.concatenate(
-                        [factor[here, block(table[NAME, w], tile)] for w in range(2 * n)], axis=1
-                    )
-                    out[k] = lax.dot_general(
-                        left[rows, : 2 * n * tile], right, LAST_LAST, preferred_element_type=jnp.float32
-                    ).astype(out.dtype)
-                    return carry
-
-                lax.fori_loop(0, 2, unit, 0)
-
-    return ladder_call(body, (2, half, half), [], in_smem(table), left, factor, flops=flops)
-
-
-def ladder_call(body, shape, scratch, *operands, flops):
-    return pl.pallas_call(
-        body,
-        out_shape=jax.ShapeDtypeStruct(shape, jnp.bfloat16),
+
+                    lax.fori_loop(first, last, unit, 0)
+
+    shapes = [(end - first, half, half) for far, first, end, when in outputs]
+    return ladder_call(body, shapes, [], in_smem(table), left, factor, flops=flops)
+
+
+def ladder_call(body, shapes, scratch, *operands, flops):
+    return pl.pallas_call(
+        body,
+        out_shape=[jax.ShapeDtypeStruct(shape, jnp.bfloat16) for shape in shapes],
         in_specs=[SMEM] + [VMEM] * (len(operands) - 1),
-        out_specs=VMEM,
+        out_specs=[VMEM] * len(shapes),
         scratch_shapes=scratch,
         compiler_params=params(32),
         cost_estimate=pl.CostEstimate(flops=flops, bytes_accessed=1, transcendentals=0),
@@ -301,16 +314,55 @@
     )(*operands)
 
 
-def finish(table, sums, other_sums, near, arrived, cycle_rows, *, pieces):
-    half, width = near.shape[1], 2 * near.shape[2]
+def lay_out(sums, low, core):
+    share = low.shape[0] // 2
+    for n in range(low.shape[1] // LANES):
+        side = slice(n * LANES, (n + 1) * LANES)
+        low[block(core, share), side] = sums[n * share : (n + 1) * share, :]
+        low[block(1 - core, share), side] = jnp.zeros((share, LANES), low.dtype)
+
+
+def first_terms(table, sums, near, arrived, cycle_rows, *, pieces):
+    half, width = arrived.shape[1], 2 * arrived.shape[2]
     aux = cycle_rows.shape[1]
-    share = sums.shape[0]
     rows = half // pieces
 
-    def body(table, sums, other_sums, near, arrived, factor, out, low, done, sems):
+    def body(table, sums, near_early, near_late, near_b, arrived, factor, out, low):
         core = table[FACTS, CORE]
-        low[block(core, share), :] = sums[...]
-        low[block(1 - core, share), :] = other_sums[...]
+        early = early_unit(core, (table[FACTS, USED] + 1) // 2)
+        lay_out(sums, low, core)
+        for n in range(pieces):
+            here = slice(n * rows, (n + 1) * rows)
+            term = jnp.dot(
+                factor[pl.ds(pl.multiple_of(core * half + n * rows, rows), rows), :], low[...],
+                preferred_element_type=jnp.float32,
+            )
+            near_a = jnp.where(early, near_early[0, here, :], near_late[0, here, :])
+            for k, near in enumerate([near_a, near_b[0, here, :]]):
+                side = slice(k * half, (k + 1) * half)
+                ladder = near.astype(jnp.float32) + arrived[k, here, :].astype(jnp.float32)
+                out[here, side] = ladder + term[:, side]
+
+    return pl.pallas_call(
+        body,
+        out_shape=jax.ShapeDtypeStruct((half, width), jnp.float32),
+        in_specs=[SMEM] + [VMEM] * 6,
+        out_specs=VMEM,
+        scratch_shapes=[pltpu.VMEM((aux, width), jnp.bfloat16)],
+        compiler_params=params(32),
+        cost_estimate=pl.CostEstimate(flops=10**9, bytes_accessed=1, transcendentals=0),
+        name="first_terms",
+    )(in_smem(table), sums, *near, arrived, cycle_rows)
+
+
+def finish(table, other_sums, terms, cycle_rows, *, pieces):
+    half, width = terms.shape
+    aux = cycle_rows.shape[1]
+    rows = half // pieces
+
+    def body(table, other_sums, terms, factor, out, low, done, sems):
+        core = table[FACTS, CORE]
+        lay_out(other_sums, low, 1 - core)
         stores = []
         for n in range(pieces):
             here = slice(n * rows, (n + 1) * rows)
@@ -318,10 +370,7 @@
                 factor[pl.ds(pl.multiple_of(core * half + n * rows, rows), rows), :], low[...],
                 preferred_element_type=jnp.float32,
             )
-            for k in range(2):
-                side = slice(k * half, (k + 1) * half)
-                total = near[k, here, :].astype(jnp.float32) + arrived[k, here, :].astype(jnp.float32) + term[:, side]
-                done[here, side] = total.astype(done.dtype)
+            done[here, :] = (terms[here, :] + term).astype(done.dtype)
             store = pltpu.make_async_copy(done.at[here, :], out.at[here, :], sems.at[n])
             store.start()
             stores.append(store)
@@ -331,7 +380,7 @@
     return pl.pallas_call(
         body,
         out_shape=jax.ShapeDtypeStruct((half, width), jnp.bfloat16),
-        in_specs=[SMEM] + [VMEM] * 5,
+        in_specs=[SMEM] + [VMEM] * 3,
         out_specs=HBM,
         scratch_shapes=[
             pltpu.VMEM((aux, width), jnp.bfloat16),
@@ -340,7 +389,7 @@
         ],
         compiler_params=params(32),
         name="finish",
-    )(in_smem(table), sums, other_sums, near, arrived, cycle_rows)
+    )(in_smem(table), other_sums, terms, cycle_rows)
 
 
 def shards(amp_tiles, tile_coords, tile_mask, pair_orbs, ladder_factor, cycle_factor):
@@ -370,29 +419,37 @@
         kept, message = step(table, next_orbs, message, arrival, plain=0)
         message, left = lax.optimization_barrier((message, left))
         arrival = exchange(message, 2, 1)
-        far = ladder_multiply(table, left, factor, tile, far=True, flops=10**10)
+        far, near_early = ladder_multiply(
+            table, left, factor, tile, [(True, 0, 2, None), (False, 0, 1, "early")], flops=10**10
+        )
         arrival, far = lax.optimization_barrier((arrival, far))
         kept, message = step(table, next_orbs, kept, arrival, plain=1)
         message, left, far = lax.optimization_barrier((message, left, far))
         arrival = exchange(message, 1, 4)
         arrived = lax.ppermute(far, "virt", swap)
-        near = ladder_multiply(table, left, factor, tile, far=False, flops=4 * 10**10)
-        arrival, near = lax.optimization_barrier((arrival, near))
+        near_late, near_b = ladder_multiply(
+            table, left, factor, tile, [(False, 0, 1, "late"), (False, 1, 2, None)], flops=4 * 10**10
+        )
+        arrival, near_b = lax.optimization_barrier((arrival, near_b))
         sums = last_step(kept, arrival)
     else:
         left = ladder_build(table, held, factor)
-        far = ladder_multiply(table, left, factor, tile, far=True, flops=10**10)
-        near = ladder_multiply(table, left, factor, tile, far=False, flops=10**10)
+        far, near_early = ladder_multiply(
+            table, left, factor, tile, [(True, 0, 2, None), (False, 0, 1, "early")], flops=10**10
+        )
+        near_late, near_b = ladder_multiply(
+            table, left, factor, tile, [(False, 0, 1, "late"), (False, 1, 2, None)], flops=10**10
+        )
         arrived = lax.ppermute(far, "virt", swap)
-        width = factor.shape[0]
         right = pair_orbs[0, 1]
         occupied = jnp.arange(cycle_factor.shape[0], dtype=jnp.int32) == right
-        mine = message[:, :width].astype(jnp.float32)
+        mine = message[:-LABEL].astype(jnp.float32)
         total = lax.psum(jnp.where(occupied[:, None, None], mine[None], 0.0), "pair")
         sums = lax.dynamic_index_in_dim(total, right, 0, keepdims=False).astype(jnp.bfloat16)
 
     other_sums = lax.ppermute(sums, "virt", swap)
-    return finish(table, sums, other_sums, near, arrived, cycle_rows, pieces=4)[None]
+    terms = first_terms(table, sums, [near_early, near_late, near_b], arrived, cycle_rows, pieces=4)
+    return finish(table, other_sums, terms, cycle_rows, pieces=6)[None]
 
 
 def solution(mesh):

time: 28.6 us -> 28.3 us (0.990)
  waiting for transfers between devices: 4.82 us -> 1.7 us
  Pallas kernels: 13.1 us -> 15.5 us
    pallas_call x6 -> x7, Pallas kernels: 8.65 us -> 11.1 us  [the longest x3 9.57 us: ladder_call(): pl.pallas_call(body, out_shape=[jax.ShapeDtypeStruct(shape, jnp.bfloat16)...]
    ppermute x3, waiting for transfers between devices: 3.63 us -> 1.49 us  [exchange(): return lax.ppermute(value, ('pair', 'virt'), routes)]
    ppermute x1, waiting for transfers between devices: 1.18 us -> 0.2 us  [shards(): other_sums = lax.ppermute(sums, 'virt', swap)]
  transfers between devices with their start and end apart: 7 -> 7, of which waited for: 4 -> 4; matrix products, arithmetic and copies ran while one was open for 0% -> 0% of each run, Pallas kernels for 37% -> 47%
where the time goes in v5:
time: 28.3 us; the launch traced here: 27.9 us
  Pallas kernels  15.5 us (55%)
  starting transfers between devices  10.4 us (37%)
  waiting for transfers between devices  1.7 us (6%)
    pallas_call x3, Pallas kernels, ladder_call(): pl.pallas_call(body, out_shape=[jax.ShapeDtypeStruct(shape, jnp.bfloat16)...  9.57 us
    ppermute x3, starting transfers between devices, exchange(): return lax.ppermute(value, ('pair', 'virt'), routes)  8 us
    pallas_call x1, Pallas kernels, prepare(): pl.pallas_call(body, out_shape=[pltpu.SMEM((7, places), jnp.int32), jax.S...  2.63 us
    pallas_call x1, Pallas kernels, finish(): pl.pallas_call(body, out_shape=jax.ShapeDtypeStruct((half, width), jnp.bf...  1.75 us
    ppermute x3, waiting for transfers between devices, exchange(): return lax.ppermute(value, ('pair', 'virt'), routes)  1.49 us
    ppermute x1, starting transfers between devices, shards(): lax.ppermute(pair_orbs, 'pair', [(p, p ^ 1) for p in range(pairs)])  1.49 us
    pallas_call x1, Pallas kernels, first_terms(): pl.pallas_call(body, out_shape=jax.ShapeDtypeStruct((half, width), jnp.fl...  0.86 us
  transfers between devices with their start and end apart: 7, of which 4 were waited for; matrix products, arithmetic and copies ran while one was open for 0% of the time, Pallas kernels for 47%

profile of v5, /device:TPU:0, one launch (start us, length us, event | category | flops | bytes accessed | tf_op | source)
XLA Modules:
  0.0 27.9 jit_solution(9454287097752271460)
XLA Ops:
  0.0 0.5 %collective-permute-start = (bf16[8,128,128]{2,1,0:T(8,128)(2,1)}, bf16[8,128,128]{2,1,0:T(8,128)(2,1)S(1)}, u32[]{:S(2)}, u32[]{:S(2)}) collective-permute-start(bf16[8,128,128]{2,1,0:T(8,128)(2,1)} %bitcast.10), channel_id=1, source_target_pairs={{0,1},{1,0},{2,3},{3,2},{4,5},{5,4},{6,7},{7,6},{8,9},{9,8},{10,11... | collective-permute-start | bytes 786440 | tf_op jit(solution)/shard_map/ppermute | solution.py:401
  0.5 0.0 copy-start.1
  0.5 0.0 copy-start
  0.5 2.6 %prepare.1 = (s32[7,17]{1,0:T(8,128)S(4)}, bf16[8,128,128]{2,1,0:T(8,128)(2,1)S(1)}, bf16[1536,128]{1,0:T(8,128)(2,1)S(1)}, f32[128,1536]{1,0:T(8,128)S(1)}) custom-call(s32[2,16]{1,0:T(2,128)} %bitcast.12, s32[1,16]{1,0:T(1,128)} %mask.1, s32[1,2]{1,0:T(1,128)} %orbs.1, s32[1]{0:T(128)} %bitcast.2.place, bf16[8,128,128]{2,1,0:T(8,128)(2,1)} %bitcast.11, ...), custom_call_target="tpu_custom_call" | custom-call | tf_op jit(solution)/shard_map/prepare/pallas_call | solution.py:105
  3.1 0.0 collective-permute-done.other
  3.1 0.3 %intermediate.1 = (bf16[784,128]{1,0:T(8,128)(2,1)S(1)}, bf16[17,128,128]{2,1,0:T(8,128)(2,1)S(1)}) custom-call(s32[7,17]{1,0:T(8,128)S(4)} %get-tuple-element.34.table, bf16[8,128,128]{2,1,0:T(8,128)(2,1)S(1)} %get-tuple-element.35.own, bf16[8,128,128]{2,1,0:T(8,128)(2,1)S(1)} %collective-permute-done.other, ...), custom_call_target="tpu_custom_call" | custom-call | tf_op jit(solution)/shard_map/intermediate/pallas_call | solution.py:145
  3.5 3.6 %collective-permute-start.2 = (bf16[784,128]{1,0:T(8,128)(2,1)S(1)}, bf16[784,128]{1,0:T(8,128)(2,1)S(1)}, u32[]{:S(2)}, u32[]{:S(2)}) collective-permute-start(bf16[784,128]{1,0:T(8,128)(2,1)S(1)} %get-tuple-element.41.mine), channel_id=1, source_target_pairs={{0,8},{1,5},{2,10},{3,7},{4,12},{5,1},{6,14},{7,3},{8,0},{9,13},{1... | collective-permute-start | bytes 602120 | tf_op jit(solution)/shard_map/ppermute | solution.py:411
  7.1 0.0 copy-done.1
  7.1 1.5 %collective-permute-start.1 = (s32[1,2]{1,0:T(1,128)S(1)}, s32[1,2]{1,0:T(1,128)S(1)}, u32[]{:S(2)}, u32[]{:S(2)}) collective-permute-start(s32[1,2]{1,0:T(1,128)S(1)} %copy-done.1), channel_id=1, source_target_pairs={{0,2},{2,0},{4,6},{6,4},{8,10},{10,8},{12,14},{14,12},{1,3},{3,1},... | collective-permute-start | bytes 32 | tf_op jit(solution)/shard_map/ppermute | solution.py:416
  8.6 0.0 copy-done
  8.6 2.5 %ladder.3.left = bf16[1536,1536]{1,0:T(8,128)(2,1)S(1)} custom-call(s32[7,17]{1,0:T(8,128)S(4)} %get-tuple-element.34.table, bf16[17,128,128]{2,1,0:T(8,128)(2,1)S(1)} %get-tuple-element.42.held, bf16[1536,1536]{1,0:T(8,128)(2,1)S(1)} %bitcast.7), custom_call_target="tpu_custom_call" | custom-call | flops 10000000000 | bytes 1 | tf_op jit(solution)/shard_map/ladder/pallas_call | solution.py:305
  11.1 0.7 %collective-permute-done.2.arrival = bf16[784,128]{1,0:T(8,128)(2,1)S(1)} collective-permute-done((bf16[784,128]{1,0:T(8,128)(2,1)S(1)}, bf16[784,128]{1,0:T(8,128)(2,1)S(1)}, u32[]{:S(2)}, u32[]{:S(2)}) %collective-permute-start.2) | collective-permute-done | bytes 200736 | tf_op jit(solution)/shard_map/ppermute | solution.py:411
  11.8 0.0 collective-permute-done.1.next_orbs
  11.8 0.1 step.2
  11.9 2.8 %collective-permute-start.3 = (bf16[784,128]{1,0:T(8,128)(2,1)S(1)}, bf16[784,128]{1,0:T(8,128)(2,1)S(1)}, u32[]{:S(2)}, u32[]{:S(2)}) collective-permute-start(bf16[784,128]{1,0:T(8,128)(2,1)S(1)} %get-tuple-element.48), channel_id=1, source_target_pairs={{0,4},{1,3},{2,6},{3,1},{4,0},{5,7},{6,2},{7,5},{8,12},{9,11},{10,... | collective-permute-start | bytes 602120 | tf_op jit(solution)/shard_map/ppermute | solution.py:411
  14.7 3.6 %ladder.4 = (bf16[2,768,768]{2,1,0:T(8,128)(2,1)S(1)}, bf16[1,768,768]{2,1,0:T(8,128)(2,1)S(1)}) custom-call(s32[7,17]{1,0:T(8,128)S(4)} %get-tuple-element.34.table, bf16[1536,1536]{1,0:T(8,128)(2,1)S(1)} %ladder.3.left, bf16[1536,1536]{1,0:T(8,128)(2,1)S(1)} %bitcast.8), custom_call_target="tpu_custom_call" | custom-call | flops 10000000000 | bytes 1 | tf_op jit(solution)/shard_map/ladder/pallas_call | solution.py:305
  18.3 0.1 collective-permute-done.3.arrival
  18.4 0.2 step.3
  18.6 1.6 %collective-permute-start.4 = (bf16[784,128]{1,0:T(8,128)(2,1)S(1)}, bf16[784,128]{1,0:T(8,128)(2,1)S(1)}, u32[]{:S(2)}, u32[]{:S(2)}) collective-permute-start(bf16[784,128]{1,0:T(8,128)(2,1)S(1)} %get-tuple-element.55), channel_id=1, source_target_pairs={{0,2},{1,9},{2,0},{3,11},{4,6},{5,13},{6,4},{7,15},{8,10},{9,1},{1... | collective-permute-start | bytes 602120 | tf_op jit(solution)/shard_map/ppermute | solution.py:411
  20.1 0.0 collective-permute-start.6
  20.2 3.5 %ladder.5 = (bf16[1,768,768]{2,1,0:T(8,128)(2,1)S(1)}, bf16[1,768,768]{2,1,0:T(8,128)(2,1)S(1)}) custom-call(s32[7,17]{1,0:T(8,128)S(4)} %get-tuple-element.34.table, bf16[1536,1536]{1,0:T(8,128)(2,1)S(1)} %ladder.3.left, bf16[1536,1536]{1,0:T(8,128)(2,1)S(1)} %bitcast.9), custom_call_target="tpu_custom_call" | custom-call | flops 40000000000 | bytes 1 | tf_op jit(solution)/shard_map/ladder/pallas_call | solution.py:305
  23.6 0.7 %collective-permute-done.4.arrival = bf16[784,128]{1,0:T(8,128)(2,1)S(1)} collective-permute-done((bf16[784,128]{1,0:T(8,128)(2,1)S(1)}, bf16[784,128]{1,0:T(8,128)(2,1)S(1)}, u32[]{:S(2)}, u32[]{:S(2)}) %collective-permute-start.4) | collective-permute-done | bytes 200736 | tf_op jit(solution)/shard_map/ppermute | solution.py:411
  24.4 0.5 %collective-permute-start.5 = (bf16[768,128]{1,0:T(8,128)(2,1)S(1)}, bf16[768,128]{1,0:T(8,128)(2,1)S(1)}, u32[]{:S(2)}, u32[]{:S(2)}) collective-permute-start(bf16[768,128]{1,0:T(8,128)(2,1)S(1)} %last_step.1.sums), channel_id=1, source_target_pairs={{0,1},{1,0},{2,3},{3,2},{4,5},{5,4},{6,7},{7,6},{8,9},{9,8},{10,11... | collective-permute-start | bytes 589832 | tf_op jit(solution)/shard_map/ppermute | solution.py:450
  24.9 0.0 collective-permute-done.6.arrived
  24.9 0.9 %first_terms.1.terms = f32[768,1536]{1,0:T(8,128)S(1)} custom-call(s32[7,17]{1,0:T(8,128)S(4)} %get-tuple-element.34.table, bf16[768,128]{1,0:T(8,128)(2,1)S(1)} %last_step.1.sums, bf16[1,768,768]{2,1,0:T(8,128)(2,1)S(1)} %get-tuple-element.59.near_early, bf16[1,768,768]{2,1,0:T(8,128)(2,1)S(1)} %get-tuple-element.60.near_late, ...), custom_call_target="tpu_custom_call" | custom-call | flops 1000000000 | bytes 1 | tf_op jit(solution)/shard_map/first_terms/pallas_call | solution.py:346
  25.7 0.2 collective-permute-done.5.other_sums
  25.9 1.7 %finish.1 = bf16[768,1536]{1,0:T(8,128)(2,1)} custom-call(s32[7,17]{1,0:T(8,128)S(4)} %get-tuple-element.34.table, bf16[768,128]{1,0:T(8,128)(2,1)S(1)} %collective-permute-done.5.other_sums, f32[768,1536]{1,0:T(8,128)S(1)} %first_terms.1.terms, bf16[1536,128]{1,0:T(8,128)(2,1)S(1)} %get-tuple-element.36.rows.factor), custom_call_target="tpu_custom_call" | custom-call | tf_op jit(solution)/shard_map/finish/pallas_call | solution.py:380
  (1 shorter events, 0.0 us)
Async XLA Ops:
  0.0 3.1 %collective-permute-start = (bf16[8,128,128]{2,1,0:T(8,128)(2,1)}, bf16[8,128,128]{2,1,0:T(8,128)(2,1)S(1)}, u32[]{:S(2)}, u32[]{:S(2)}) collective-permute-start(bf16[8,128,128]{2,1,0:T(8,128)(2,1)} %bitcast.10), channel_id=1, source_target_pairs={{0,1},{1,0},{2,3},{3,2},{4,5},{5,4},{6,7},{7,6},{8,9},{9,8},{10,11... | collective-permute-start | bytes 786440 | tf_op jit(solution)/shard_map/ppermute | solution.py:401
  0.5 6.7 %copy-start.1 = (s32[1,2]{1,0:T(1,128)S(1)}, s32[1,2]{1,0:T(1,128)}, u32[]{:S(2)}) copy-start(s32[1,2]{1,0:T(1,128)} %orbs.1) | copy-start | bytes 28
  0.5 8.2 %copy-start = (bf16[1,1536,1536]{2,1,0:T(8,128)(2,1)S(1)}, bf16[1,1536,1536]{2,1,0:T(8,128)(2,1)}, u32[]{:S(2)}) copy-start(bf16[1,1536,1536]{2,1,0:T(8,128)(2,1)} %param.10) | copy-start | bytes 14155780
  3.5 8.3 %collective-permute-start.2 = (bf16[784,128]{1,0:T(8,128)(2,1)S(1)}, bf16[784,128]{1,0:T(8,128)(2,1)S(1)}, u32[]{:S(2)}, u32[]{:S(2)}) collective-permute-start(bf16[784,128]{1,0:T(8,128)(2,1)S(1)} %get-tuple-element.41.mine), channel_id=1, source_target_pairs={{0,8},{1,5},{2,10},{3,7},{4,12},{5,1},{6,14},{7,3},{8,0},{9,13},{1... | collective-permute-start | bytes 602120 | tf_op jit(solution)/shard_map/ppermute | solution.py:411
  7.1 4.7 %collective-permute-start.1 = (s32[1,2]{1,0:T(1,128)S(1)}, s32[1,2]{1,0:T(1,128)S(1)}, u32[]{:S(2)}, u32[]{:S(2)}) collective-permute-start(s32[1,2]{1,0:T(1,128)S(1)} %copy-done.1), channel_id=1, source_target_pairs={{0,2},{2,0},{4,6},{6,4},{8,10},{10,8},{12,14},{14,12},{1,3},{3,1},... | collective-permute-start | bytes 32 | tf_op jit(solution)/shard_map/ppermute | solution.py:416
  11.9 6.5 %collective-permute-start.3 = (bf16[784,128]{1,0:T(8,128)(2,1)S(1)}, bf16[784,128]{1,0:T(8,128)(2,1)S(1)}, u32[]{:S(2)}, u32[]{:S(2)}) collective-permute-start(bf16[784,128]{1,0:T(8,128)(2,1)S(1)} %get-tuple-element.48), channel_id=1, source_target_pairs={{0,4},{1,3},{2,6},{3,1},{4,0},{5,7},{6,2},{7,5},{8,12},{9,11},{10,... | collective-permute-start | bytes 602120 | tf_op jit(solution)/shard_map/ppermute | solution.py:411
  18.6 5.8 %collective-permute-start.4 = (bf16[784,128]{1,0:T(8,128)(2,1)S(1)}, bf16[784,128]{1,0:T(8,128)(2,1)S(1)}, u32[]{:S(2)}, u32[]{:S(2)}) collective-permute-start(bf16[784,128]{1,0:T(8,128)(2,1)S(1)} %get-tuple-element.55), channel_id=1, source_target_pairs={{0,2},{1,9},{2,0},{3,11},{4,6},{5,13},{6,4},{7,15},{8,10},{9,1},{1... | collective-permute-start | bytes 602120 | tf_op jit(solution)/shard_map/ppermute | solution.py:411
  20.1 4.7 %collective-permute-start.6 = (bf16[2,768,768]{2,1,0:T(8,128)(2,1)S(1)}, bf16[2,768,768]{2,1,0:T(8,128)(2,1)S(1)}, u32[]{:S(2)}, u32[]{:S(2)}) collective-permute-start(bf16[2,768,768]{2,1,0:T(8,128)(2,1)S(1)} %get-tuple-element.62), channel_id=1, source_target_pairs={{0,1},{1,0},{2,3},{3,2},{4,5},{5,4},{6,7},{7,6},{8,9},{9,8},{10,11... | collective-permute-start | bytes 7077896 | tf_op jit(solution)/shard_map/ppermute | solution.py:429
  24.4 1.5 %collective-permute-start.5 = (bf16[768,128]{1,0:T(8,128)(2,1)S(1)}, bf16[768,128]{1,0:T(8,128)(2,1)S(1)}, u32[]{:S(2)}, u32[]{:S(2)}) collective-permute-start(bf16[768,128]{1,0:T(8,128)(2,1)S(1)} %last_step.1.sums), channel_id=1, source_target_pairs={{0,1},{1,0},{2,3},{3,2},{4,5},{5,4},{6,7},{7,6},{8,9},{9,8},{10,11... | collective-permute-start | bytes 589832 | tf_op jit(solution)/shard_map/ppermute | solution.py:450

commit v6 on v4

--- a/solution.py
+++ b/solution.py
@@ -7,7 +7,8 @@
 from jax.experimental.pallas import tpu as pltpu
 from jax.sharding import PartitionSpec as P
 
-LANES = 128
+LANES, LABEL = 128, 16
+ORDERS = (4, 2, 1), (2, 1, 4)
 SMEM = pl.BlockSpec(memory_space=pltpu.SMEM)
 VMEM = pl.BlockSpec(memory_space=pltpu.VMEM)
 HBM = pl.BlockSpec(memory_space=pltpu.HBM)
@@ -127,14 +128,17 @@
 def intermediate(table, own, other, rows, start, *, cores):
     local, tile = own.shape[0], own.shape[1]
     aux, width = start.shape
-    share = aux // cores
+    blocks = width // LANES // cores
 
     def body(table, own, other, rows, start, out, held, total):
         total[...] = start[...]
         add_terms(total, table, rows, other, range(local, 2 * local))
-        out[:, :width] = total[block(table[FACTS, CORE], share), :].astype(out.dtype)
-        label = jnp.zeros((share, LANES), jnp.float32) + table[FACTS, ORBITAL].astype(jnp.float32)
-        out[:, width:] = label.astype(out.dtype)
+        for n in range(blocks):
+            out[n * aux : (n + 1) * aux, :] = total[
+                :, block(table[FACTS, CORE] * blocks + n, LANES)
+            ].astype(out.dtype)
+        label = jnp.zeros((LABEL, LANES), jnp.float32) + table[FACTS, ORBITAL].astype(jnp.float32)
+        out[blocks * aux :, :] = label.astype(out.dtype)
         held[:local] = own[...]
         held[local : 2 * local] = other[...]
         held[2 * local] = jnp.zeros((tile, tile), held.dtype)
@@ -142,7 +146,7 @@
     return pl.pallas_call(
         body,
         out_shape=[
-            jax.ShapeDtypeStruct((share, width + LANES), jnp.bfloat16),
+            jax.ShapeDtypeStruct((blocks * aux + LABEL, LANES), jnp.bfloat16),
             jax.ShapeDtypeStruct((2 * local + 1, tile, tile), jnp.bfloat16),
         ],
         in_specs=[SMEM, VMEM, VMEM, VMEM, VMEM],
@@ -154,36 +158,35 @@
 
 
 def step(table, next_orbs, mine, arrival, *, plain):
-    share, full = arrival.shape
-    width = full - LANES
+    length = arrival.shape[0] - LABEL
 
     def body(table, next_orbs, mine, arrival, kept, out):
-        value = mine[:, :width].astype(jnp.float32)
-        extra = arrival[:, :width].astype(jnp.float32)
-        own = jnp.zeros((share, LANES), jnp.float32) + table[FACTS, ORBITAL].astype(jnp.float32)
-        out[:, width:] = own.astype(out.dtype)
+        value = mine[:length, :].astype(jnp.float32)
+        extra = arrival[:length, :].astype(jnp.float32)
+        own = jnp.zeros((LABEL, LANES), jnp.float32) + table[FACTS, ORBITAL].astype(jnp.float32)
+        out[length:, :] = own.astype(out.dtype)
 
         @pl.when(table[FACTS, CORE] == plain)
         def _():
             total = value + extra
             kept[...] = total
-            out[:, :width] = total.astype(out.dtype)
+            out[:length, :] = total.astype(out.dtype)
 
         @pl.when(table[FACTS, CORE] != plain)
         def _():
-            label = own[:, :1]
-            theirs = arrival[:, width : width + 1].astype(jnp.float32)
+            label = own[:1, :]
+            theirs = arrival[length : length + LABEL, :].astype(jnp.float32)[:1, :]
             behind = next_orbs[0:1, 1:2].astype(jnp.float32)
             kept[...] = value + jnp.where(theirs == label, extra, 0.0)
-            out[:, :width] = (
+            out[:length, :] = (
                 jnp.where(label == behind, value, 0.0) + jnp.where(theirs == behind, extra, 0.0)
             ).astype(out.dtype)
 
     return pl.pallas_call(
         body,
         out_shape=[
-            jax.ShapeDtypeStruct((share, width), jnp.float32),
-            jax.ShapeDtypeStruct((share, full), arrival.dtype),
+            jax.ShapeDtypeStruct((length, LANES), jnp.float32),
+            jax.ShapeDtypeStruct(arrival.shape, arrival.dtype),
         ],
         in_specs=[SMEM, VMEM, VMEM, VMEM],
         out_specs=[VMEM, VMEM],
@@ -193,10 +196,10 @@
 
 
 def last_step(mine, arrival):
-    width = mine.shape[1]
+    length = mine.shape[0]
 
     def body(mine, arrival, out):
-        out[...] = (mine[...] + arrival[:, :width].astype(jnp.float32)).astype(out.dtype)
+        out[...] = (mine[...] + arrival[:length, :].astype(jnp.float32)).astype(out.dtype)
 
     return pl.pallas_call(
         body,
@@ -301,16 +304,18 @@
     )(*operands)
 
 
-def finish(table, sums, other_sums, near, arrived, cycle_rows, *, pieces):
-    half, width = near.shape[1], 2 * near.shape[2]
+def finish(table, sums, near, arrived, cycle_rows, whole, *, pieces):
+    half = arrived.shape[1]
     aux = cycle_rows.shape[1]
-    share = sums.shape[0]
     rows = half // pieces
-
-    def body(table, sums, other_sums, near, arrived, factor, out, low, done, sems):
+    first = whole is None
+
+    def body(table, sums, near, arrived, factor, *refs):
+        out, low, done, sems = refs[-4:]
         core = table[FACTS, CORE]
-        low[block(core, share), :] = sums[...]
-        low[block(1 - core, share), :] = other_sums[...]
+        side = core if first else 1 - core
+        for n in range(half // LANES):
+            low[:, n * LANES : (n + 1) * LANES] = sums[n * aux : (n + 1) * aux, :]
         stores = []
         for n in range(pieces):
             here = slice(n * rows, (n + 1) * rows)
@@ -318,29 +323,33 @@
                 factor[pl.ds(pl.multiple_of(core * half + n * rows, rows), rows), :], low[...],
                 preferred_element_type=jnp.float32,
             )
-            for k in range(2):
-                side = slice(k * half, (k + 1) * half)
-                total = near[k, here, :].astype(jnp.float32) + arrived[k, here, :].astype(jnp.float32) + term[:, side]
-                done[here, side] = total.astype(done.dtype)
-            store = pltpu.make_async_copy(done.at[here, :], out.at[here, :], sems.at[n])
+            ladder = near[side, here, :].astype(jnp.float32) + arrived[side, here, :].astype(jnp.float32)
+            total = ladder + term
+            done[here, :] = total.astype(done.dtype)
+            store = pltpu.make_async_copy(
+                done.at[here, :], out.at[here, block(side, half)], sems.at[n]
+            )
             store.start()
             stores.append(store)
         for store in stores:
             store.wait()
 
-    return pl.pallas_call(
-        body,
-        out_shape=jax.ShapeDtypeStruct((half, width), jnp.bfloat16),
-        in_specs=[SMEM] + [VMEM] * 5,
+    operands = [in_smem(table), sums, near, arrived, cycle_rows]
+    return pl.pallas_call(
+        body,
+        out_shape=jax.ShapeDtypeStruct((half, 2 * half), jnp.bfloat16),
+        in_specs=[SMEM] + [VMEM] * 4 + [HBM] * (not first),
         out_specs=HBM,
         scratch_shapes=[
-            pltpu.VMEM((aux, width), jnp.bfloat16),
-            pltpu.VMEM((half, width), jnp.bfloat16),
+            pltpu.VMEM((aux, half), jnp.bfloat16),
+            pltpu.VMEM((half, half), jnp.bfloat16),
             pltpu.SemaphoreType.DMA((pieces,)),
         ],
-        compiler_params=params(32),
-        name="finish",
-    )(in_smem(table), sums, other_sums, near, arrived, cycle_rows)
+        input_output_aliases={} if first else {len(operands): 0},
+        compiler_params=params(16),
+        cost_estimate=pl.CostEstimate(flops=10**9, bytes_accessed=1, transcendentals=0),
+        name="finish_own" if first else "finish_other",
+    )(*operands, *([] if first else [whole]))
 
 
 def shards(amp_tiles, tile_coords, tile_mask, pair_orbs, ladder_factor, cycle_factor):
@@ -356,25 +365,24 @@
     factor = ladder_factor[0]
     tile = held.shape[1]
 
-    def exchange(value, first_core, second_core):
-        partners = (first_core, second_core)
+    def exchange(value, *partners):
         routes = [(p * 2 + c, (p ^ partners[c]) * 2 + c) for p in range(pairs) for c in range(2)]
         return lax.ppermute(value, ("pair", "virt"), routes)
 
     if square:
-        arrival = exchange(message, 4, 2)
+        arrival = exchange(message, ORDERS[0][0], ORDERS[1][0])
         message, pair_orbs, held, factor = lax.optimization_barrier((message, pair_orbs, held, factor))
-        next_orbs = lax.ppermute(pair_orbs, "pair", [(p, p ^ 1) for p in range(pairs)])
+        next_orbs = exchange(pair_orbs, ORDERS[0][2], ORDERS[1][1])
         left = ladder_build(table, held, factor)
         arrival, left = lax.optimization_barrier((arrival, left))
         kept, message = step(table, next_orbs, message, arrival, plain=0)
         message, left = lax.optimization_barrier((message, left))
-        arrival = exchange(message, 2, 1)
+        arrival = exchange(message, ORDERS[0][1], ORDERS[1][1])
         far = ladder_multiply(table, left, factor, tile, far=True, flops=10**10)
         arrival, far = lax.optimization_barrier((arrival, far))
         kept, message = step(table, next_orbs, kept, arrival, plain=1)
         message, left, far = lax.optimization_barrier((message, left, far))
-        arrival = exchange(message, 1, 4)
+        arrival = exchange(message, ORDERS[0][2], ORDERS[1][2])
         arrived = lax.ppermute(far, "virt", swap)
         near = ladder_multiply(table, left, factor, tile, far=False, flops=4 * 10**10)
         arrival, near = lax.optimization_barrier((arrival, near))
@@ -384,15 +392,15 @@
         far = ladder_multiply(table, left, factor, tile, far=True, flops=10**10)
         near = ladder_multiply(table, left, factor, tile, far=False, flops=10**10)
         arrived = lax.ppermute(far, "virt", swap)
-        width = factor.shape[0]
         right = pair_orbs[0, 1]
         occupied = jnp.arange(cycle_factor.shape[0], dtype=jnp.int32) == right
-        mine = message[:, :width].astype(jnp.float32)
+        mine = message[:-LABEL].astype(jnp.float32)
         total = lax.psum(jnp.where(occupied[:, None, None], mine[None], 0.0), "pair")
         sums = lax.dynamic_index_in_dim(total, right, 0, keepdims=False).astype(jnp.bfloat16)
 
     other_sums = lax.ppermute(sums, "virt", swap)
-    return finish(table, sums, other_sums, near, arrived, cycle_rows, pieces=4)[None]
+    own_side = finish(table, sums, near, arrived, cycle_rows, None, pieces=4)
+    return finish(table, other_sums, near, arrived, cycle_rows, own_side, pieces=4)[None]
 
 
 def solution(mesh):

time: 28.6 us -> 27.8 us (0.972)
  waiting for transfers between devices: 4.82 us -> 1.57 us
  Pallas kernels: 13.1 us -> 15.6 us
    ppermute x3 -> x4, waiting for transfers between devices: 3.63 us -> 1.47 us  [exchange(): return lax.ppermute(value, ('pair', 'virt'), routes)]
    pallas_call x3, Pallas kernels: 7.97 us -> 9.61 us  [ladder_call(): pl.pallas_call(body, out_shape=jax.ShapeDtypeStruct(shape, jnp.bfloat16),...]
    ppermute x1 -> x0, starting transfers between devices: 1.49 us -> none  [shards(): lax.ppermute(pair_orbs, 'pair', [(p, p ^ 1) for p in range(pairs)])]
    ppermute x3 -> x4, starting transfers between devices: 7.99 us -> 9.48 us  [exchange(): return lax.ppermute(value, ('pair', 'virt'), routes)]
    ppermute x1, waiting for transfers between devices: 1.18 us -> 0.01 us  [shards(): other_sums = lax.ppermute(sums, 'virt', swap)]
    pallas_call x4 -> x5, Pallas kernels: 2.45 us -> 3.3 us  [the longest x2 2.63 us: finish(): pl.pallas_call(body, out_shape=jax.ShapeDtypeStruct((half, 2 * half), jnp...]
  transfers between devices with their start and end apart: 7 -> 7, of which waited for: 4 -> 4; matrix products, arithmetic and copies ran while one was open for 0% -> 0% of each run, Pallas kernels for 37% -> 49%
where the time goes in v6:
time: 27.8 us; the launch traced here: 27.5 us
  Pallas kernels  15.6 us (56%)
  starting transfers between devices  10.1 us (36%)
  waiting for transfers between devices  1.57 us (6%)
    pallas_call x3, Pallas kernels, ladder_call(): pl.pallas_call(body, out_shape=jax.ShapeDtypeStruct(shape, jnp.bfloat16),...  9.61 us
    ppermute x4, starting transfers between devices, exchange(): return lax.ppermute(value, ('pair', 'virt'), routes)  9.48 us
    pallas_call x1, Pallas kernels, prepare(): pl.pallas_call(body, out_shape=[pltpu.SMEM((7, places), jnp.int32), jax.S...  2.63 us
    pallas_call x2, Pallas kernels, finish(): pl.pallas_call(body, out_shape=jax.ShapeDtypeStruct((half, 2 * half), jnp...  2.63 us
    ppermute x4, waiting for transfers between devices, exchange(): return lax.ppermute(value, ('pair', 'virt'), routes)  1.47 us
  transfers between devices with their start and end apart: 7, of which 4 were waited for; matrix products, arithmetic and copies ran while one was open for 0% of the time, Pallas kernels for 49%

profile of v6, /device:TPU:0, one launch (start us, length us, event | category | flops | bytes accessed | tf_op | source)
XLA Modules:
  0.0 27.5 jit_solution(2635525884122487267)
XLA Ops:
  0.0 0.5 %collective-permute-start = (bf16[8,128,128]{2,1,0:T(8,128)(2,1)}, bf16[8,128,128]{2,1,0:T(8,128)(2,1)S(1)}, u32[]{:S(2)}, u32[]{:S(2)}) collective-permute-start(bf16[8,128,128]{2,1,0:T(8,128)(2,1)} %bitcast.10), channel_id=1, source_target_pairs={{0,1},{1,0},{2,3},{3,2},{4,5},{5,4},{6,7},{7,6},{8,9},{9,8},{10,11... | collective-permute-start | bytes 786440 | tf_op jit(solution)/shard_map/ppermute | solution.py:361
  0.5 0.0 copy-start.1
  0.5 0.0 copy-start
  0.5 2.6 %prepare.1 = (s32[7,17]{1,0:T(8,128)S(4)}, bf16[8,128,128]{2,1,0:T(8,128)(2,1)S(1)}, bf16[1536,128]{1,0:T(8,128)(2,1)S(1)}, f32[128,1536]{1,0:T(8,128)S(1)}) custom-call(s32[2,16]{1,0:T(2,128)} %bitcast.12, s32[1,16]{1,0:T(1,128)} %mask.1, s32[1,2]{1,0:T(1,128)} %orbs.1, s32[1]{0:T(128)} %bitcast.2.place, bf16[8,128,128]{2,1,0:T(8,128)(2,1)} %bitcast.11, ...), custom_call_target="tpu_custom_call" | custom-call | tf_op jit(solution)/shard_map/prepare/pallas_call | solution.py:106
  3.1 0.0 collective-permute-done.other
  3.1 0.4 %intermediate.1 = (bf16[784,128]{1,0:T(8,128)(2,1)S(1)}, bf16[17,128,128]{2,1,0:T(8,128)(2,1)S(1)}) custom-call(s32[7,17]{1,0:T(8,128)S(4)} %get-tuple-element.30.table, bf16[8,128,128]{2,1,0:T(8,128)(2,1)S(1)} %get-tuple-element.31.own, bf16[8,128,128]{2,1,0:T(8,128)(2,1)S(1)} %collective-permute-done.other, ...), custom_call_target="tpu_custom_call" | custom-call | tf_op jit(solution)/shard_map/intermediate/pallas_call | solution.py:146
  3.5 3.7 %collective-permute-start.2 = (bf16[784,128]{1,0:T(8,128)(2,1)S(1)}, bf16[784,128]{1,0:T(8,128)(2,1)S(1)}, u32[]{:S(2)}, u32[]{:S(2)}) collective-permute-start(bf16[784,128]{1,0:T(8,128)(2,1)S(1)} %get-tuple-element.37.mine), channel_id=1, source_target_pairs={{0,8},{1,5},{2,10},{3,7},{4,12},{5,1},{6,14},{7,3},{8,0},{9,13},{1... | collective-permute-start | bytes 602120 | tf_op jit(solution)/shard_map/ppermute | solution.py:370
  7.1 0.0 copy-done.1
  7.1 1.5 %collective-permute-start.1 = (s32[1,2]{1,0:T(1,128)S(1)}, s32[1,2]{1,0:T(1,128)S(1)}, u32[]{:S(2)}, u32[]{:S(2)}) collective-permute-start(s32[1,2]{1,0:T(1,128)S(1)} %copy-done.1), channel_id=1, source_target_pairs={{0,2},{1,3},{2,0},{3,1},{4,6},{5,7},{6,4},{7,5},{8,10},{9,11},{10,... | collective-permute-start | bytes 32 | tf_op jit(solution)/shard_map/ppermute | solution.py:370
  8.6 0.0 copy-done
  8.6 2.7 %ladder.3.left = bf16[1536,1536]{1,0:T(8,128)(2,1)S(1)} custom-call(s32[7,17]{1,0:T(8,128)S(4)} %get-tuple-element.30.table, bf16[17,128,128]{2,1,0:T(8,128)(2,1)S(1)} %get-tuple-element.38.held, bf16[1536,1536]{1,0:T(8,128)(2,1)S(1)} %bitcast.7), custom_call_target="tpu_custom_call" | custom-call | flops 10000000000 | bytes 1 | tf_op jit(solution)/shard_map/ladder/pallas_call | solution.py:295
  11.3 0.5 %collective-permute-done.2.arrival = bf16[784,128]{1,0:T(8,128)(2,1)S(1)} collective-permute-done((bf16[784,128]{1,0:T(8,128)(2,1)S(1)}, bf16[784,128]{1,0:T(8,128)(2,1)S(1)}, u32[]{:S(2)}, u32[]{:S(2)}) %collective-permute-start.2) | collective-permute-done | bytes 200736 | tf_op jit(solution)/shard_map/ppermute | solution.py:370
  11.8 0.0 collective-permute-done.1.next_orbs
  11.8 0.1 step.2
  11.9 2.8 %collective-permute-start.3 = (bf16[784,128]{1,0:T(8,128)(2,1)S(1)}, bf16[784,128]{1,0:T(8,128)(2,1)S(1)}, u32[]{:S(2)}, u32[]{:S(2)}) collective-permute-start(bf16[784,128]{1,0:T(8,128)(2,1)S(1)} %get-tuple-element.44), channel_id=1, source_target_pairs={{0,4},{1,3},{2,6},{3,1},{4,0},{5,7},{6,2},{7,5},{8,12},{9,11},{10,... | collective-permute-start | bytes 602120 | tf_op jit(solution)/shard_map/ppermute | solution.py:370
  14.7 3.5 %ladder.4 = bf16[2,768,768]{2,1,0:T(8,128)(2,1)S(1)} custom-call(s32[7,17]{1,0:T(8,128)S(4)} %get-tuple-element.30.table, bf16[1536,1536]{1,0:T(8,128)(2,1)S(1)} %ladder.3.left, bf16[1536,1536]{1,0:T(8,128)(2,1)S(1)} %bitcast.8), custom_call_target="tpu_custom_call" | custom-call | flops 10000000000 | bytes 1 | tf_op jit(solution)/shard_map/ladder/pallas_call | solution.py:295
  18.2 0.2 collective-permute-done.3.arrival
  18.4 0.2 step.3
  18.6 1.6 %collective-permute-start.4 = (bf16[784,128]{1,0:T(8,128)(2,1)S(1)}, bf16[784,128]{1,0:T(8,128)(2,1)S(1)}, u32[]{:S(2)}, u32[]{:S(2)}) collective-permute-start(bf16[784,128]{1,0:T(8,128)(2,1)S(1)} %get-tuple-element.50), channel_id=1, source_target_pairs={{0,2},{1,9},{2,0},{3,11},{4,6},{5,13},{6,4},{7,15},{8,10},{9,1},{1... | collective-permute-start | bytes 602120 | tf_op jit(solution)/shard_map/ppermute | solution.py:370
  20.2 0.0 collective-permute-start.6
  20.2 3.5 %ladder.5.near = bf16[2,768,768]{2,1,0:T(8,128)(2,1)S(1)} custom-call(s32[7,17]{1,0:T(8,128)S(4)} %get-tuple-element.30.table, bf16[1536,1536]{1,0:T(8,128)(2,1)S(1)} %ladder.3.left, bf16[1536,1536]{1,0:T(8,128)(2,1)S(1)} %bitcast.9), custom_call_target="tpu_custom_call" | custom-call | flops 40000000000 | bytes 1 | tf_op jit(solution)/shard_map/ladder/pallas_call | solution.py:295
  23.6 0.8 %collective-permute-done.4.arrival = bf16[784,128]{1,0:T(8,128)(2,1)S(1)} collective-permute-done((bf16[784,128]{1,0:T(8,128)(2,1)S(1)}, bf16[784,128]{1,0:T(8,128)(2,1)S(1)}, u32[]{:S(2)}, u32[]{:S(2)}) %collective-permute-start.4) | collective-permute-done | bytes 200736 | tf_op jit(solution)/shard_map/ppermute | solution.py:370
  24.4 0.2 collective-permute-start.5
  24.6 0.1 collective-permute-done.6.arrived
  24.7 1.3 %finish_own.1.refs_0_ = bf16[768,1536]{1,0:T(8,128)(2,1)} custom-call(s32[7,17]{1,0:T(8,128)S(4)} %get-tuple-element.30.table, bf16[768,128]{1,0:T(8,128)(2,1)S(1)} %last_step.1.sums, bf16[2,768,768]{2,1,0:T(8,128)(2,1)S(1)} %ladder.5.near, bf16[2,768,768]{2,1,0:T(8,128)(2,1)S(1)} %collective-permute-done.6.arrived, ...), custom_call_target="tpu_custom_call" | custom-call | flops 1000000000 | bytes 1 | tf_op jit(solution)/shard_map/finish_own/pallas_call | solution.py:338
  26.0 0.0 collective-permute-done.5.sums
  26.0 1.3 %finish_other.1 = bf16[768,1536]{1,0:T(8,128)(2,1)} custom-call(s32[7,17]{1,0:T(8,128)S(4)} %get-tuple-element.30.table, bf16[768,128]{1,0:T(8,128)(2,1)S(1)} %collective-permute-done.5.sums, bf16[2,768,768]{2,1,0:T(8,128)(2,1)S(1)} %ladder.5.near, bf16[2,768,768]{2,1,0:T(8,128)(2,1)S(1)} %collective-permute-done.6.arrived, ...), custom_call_target="tpu_custom_call", output_to_operand_aliasing={{}: (5, {})} | custom-call | flops 1000000000 | bytes 1 | tf_op jit(solution)/shard_map/finish_other/pallas_call | solution.py:338
  (1 shorter events, 0.0 us)
Async XLA Ops:
  0.0 3.1 %collective-permute-start = (bf16[8,128,128]{2,1,0:T(8,128)(2,1)}, bf16[8,128,128]{2,1,0:T(8,128)(2,1)S(1)}, u32[]{:S(2)}, u32[]{:S(2)}) collective-permute-start(bf16[8,128,128]{2,1,0:T(8,128)(2,1)} %bitcast.10), channel_id=1, source_target_pairs={{0,1},{1,0},{2,3},{3,2},{4,5},{5,4},{6,7},{7,6},{8,9},{9,8},{10,11... | collective-permute-start | bytes 786440 | tf_op jit(solution)/shard_map/ppermute | solution.py:361
  0.5 6.7 %copy-start.1 = (s32[1,2]{1,0:T(1,128)S(1)}, s32[1,2]{1,0:T(1,128)}, u32[]{:S(2)}) copy-start(s32[1,2]{1,0:T(1,128)} %orbs.1) | copy-start | bytes 28
  0.5 8.2 %copy-start = (bf16[1,1536,1536]{2,1,0:T(8,128)(2,1)S(1)}, bf16[1,1536,1536]{2,1,0:T(8,128)(2,1)}, u32[]{:S(2)}) copy-start(bf16[1,1536,1536]{2,1,0:T(8,128)(2,1)} %param.10) | copy-start | bytes 14155780
  3.5 8.3 %collective-permute-start.2 = (bf16[784,128]{1,0:T(8,128)(2,1)S(1)}, bf16[784,128]{1,0:T(8,128)(2,1)S(1)}, u32[]{:S(2)}, u32[]{:S(2)}) collective-permute-start(bf16[784,128]{1,0:T(8,128)(2,1)S(1)} %get-tuple-element.37.mine), channel_id=1, source_target_pairs={{0,8},{1,5},{2,10},{3,7},{4,12},{5,1},{6,14},{7,3},{8,0},{9,13},{1... | collective-permute-start | bytes 602120 | tf_op jit(solution)/shard_map/ppermute | solution.py:370
  7.1 4.7 %collective-permute-start.1 = (s32[1,2]{1,0:T(1,128)S(1)}, s32[1,2]{1,0:T(1,128)S(1)}, u32[]{:S(2)}, u32[]{:S(2)}) collective-permute-start(s32[1,2]{1,0:T(1,128)S(1)} %copy-done.1), channel_id=1, source_target_pairs={{0,2},{1,3},{2,0},{3,1},{4,6},{5,7},{6,4},{7,5},{8,10},{9,11},{10,... | collective-permute-start | bytes 32 | tf_op jit(solution)/shard_map/ppermute | solution.py:370
  11.9 6.5 %collective-permute-start.3 = (bf16[784,128]{1,0:T(8,128)(2,1)S(1)}, bf16[784,128]{1,0:T(8,128)(2,1)S(1)}, u32[]{:S(2)}, u32[]{:S(2)}) collective-permute-start(bf16[784,128]{1,0:T(8,128)(2,1)S(1)} %get-tuple-element.44), channel_id=1, source_target_pairs={{0,4},{1,3},{2,6},{3,1},{4,0},{5,7},{6,2},{7,5},{8,12},{9,11},{10,... | collective-permute-start | bytes 602120 | tf_op jit(solution)/shard_map/ppermute | solution.py:370
  18.6 5.8 %collective-permute-start.4 = (bf16[784,128]{1,0:T(8,128)(2,1)S(1)}, bf16[784,128]{1,0:T(8,128)(2,1)S(1)}, u32[]{:S(2)}, u32[]{:S(2)}) collective-permute-start(bf16[784,128]{1,0:T(8,128)(2,1)S(1)} %get-tuple-element.50), channel_id=1, source_target_pairs={{0,2},{1,9},{2,0},{3,11},{4,6},{5,13},{6,4},{7,15},{8,10},{9,1},{1... | collective-permute-start | bytes 602120 | tf_op jit(solution)/shard_map/ppermute | solution.py:370
  20.2 4.5 %collective-permute-start.6 = (bf16[2,768,768]{2,1,0:T(8,128)(2,1)S(1)}, bf16[2,768,768]{2,1,0:T(8,128)(2,1)S(1)}, u32[]{:S(2)}, u32[]{:S(2)}) collective-permute-start(bf16[2,768,768]{2,1,0:T(8,128)(2,1)S(1)} %ladder.4), channel_id=1, source_target_pairs={{0,1},{1,0},{2,3},{3,2},{4,5},{5,4},{6,7},{7,6},{8,9},{9,8},{10,11... | collective-permute-start | bytes 7077896 | tf_op jit(solution)/shard_map/ppermute | solution.py:386
  24.4 1.6 %collective-permute-start.5 = (bf16[768,128]{1,0:T(8,128)(2,1)S(1)}, bf16[768,128]{1,0:T(8,128)(2,1)S(1)}, u32[]{:S(2)}, u32[]{:S(2)}) collective-permute-start(bf16[768,128]{1,0:T(8,128)(2,1)S(1)} %last_step.1.sums), channel_id=1, source_target_pairs={{0,1},{1,0},{2,3},{3,2},{4,5},{5,4},{6,7},{7,6},{8,9},{9,8},{10,11... | collective-permute-start | bytes 589832 | tf_op jit(solution)/shard_map/ppermute | solution.py:401

commit v7 on v6

--- a/solution.py
+++ b/solution.py
@@ -46,11 +46,11 @@
         total[:, block(table[ROW, s], size)] += term * table[KEPT, s].astype(jnp.float32)
 
 
-def prepare(coords, mask, orbs, place, own, cycle_factor):
+def prepare(coords, mask, orbs, place, own, cycle_factor, *, cores):
     slots = coords.shape[1]
     local, tile = own.shape[0], own.shape[1]
     width, aux = cycle_factor.shape[1:]
-    tiles = width // tile
+    tiles, tiles_here = width // tile, width // tile // cores
     places = max(slots + 1, tiles + 3)
 
     def body(coords, mask, orbs, place, own, factor, table, held, rows, total, s_coords, s_mask, s_orbs, count, sems):
@@ -76,8 +76,9 @@
             g = lax.rem(s + core * local, slots)
             d, kept = s_coords[1, g], s_mask[0, g]
             table[COLUMN, s] = s_coords[0, g]
-            table[ROW, s] = d
-            table[KEPT, s] = kept
+            inside = d // tiles_here == core
+            table[ROW, s] = jnp.where(inside, d - core * tiles_here, 0)
+            table[KEPT, s] = jnp.where(inside, kept, 0)
             table[SORTED, s] = slots
             count[d] += (kept != 0).astype(jnp.int32)
         table[COLUMN, slots] = 0
@@ -94,9 +95,9 @@
             table[NAME, used + n] = 0
             table[BEGIN, used + n] = begin
         for s in range(slots):
-            d = table[ROW, s]
+            g = lax.rem(s + core * local, slots)
+            d, kept = s_coords[1, g], s_mask[0, g] != 0
             at = count[d]
-            kept = table[KEPT, s] != 0
             table[SORTED, jnp.where(kept, at, slots)] = s
             count[d] = at + kept.astype(jnp.int32)
         loads[3].wait()
@@ -109,7 +110,7 @@
             pltpu.SMEM((7, places), jnp.int32),
             jax.ShapeDtypeStruct(own.shape, own.dtype),
             jax.ShapeDtypeStruct((width, aux), jnp.bfloat16),
-            jax.ShapeDtypeStruct((aux, width), jnp.float32),
+            jax.ShapeDtypeStruct((aux, width // cores), jnp.float32),
         ],
         in_specs=[HBM, HBM, HBM, SMEM, HBM, HBM],
         out_specs=[SMEM, VMEM, VMEM, VMEM],
@@ -125,18 +126,16 @@
     )(in_hbm(coords), in_hbm(mask), in_hbm(orbs), place, in_hbm(own), in_hbm(cycle_factor))
 
 
-def intermediate(table, own, other, rows, start, *, cores):
+def intermediate(table, own, other, rows, start):
     local, tile = own.shape[0], own.shape[1]
     aux, width = start.shape
-    blocks = width // LANES // cores
+    blocks = width // LANES
 
     def body(table, own, other, rows, start, out, held, total):
         total[...] = start[...]
         add_terms(total, table, rows, other, range(local, 2 * local))
         for n in range(blocks):
-            out[n * aux : (n + 1) * aux, :] = total[
-                :, block(table[FACTS, CORE] * blocks + n, LANES)
-            ].astype(out.dtype)
+            out[n * aux : (n + 1) * aux, :] = total[:, n * LANES : (n + 1) * LANES].astype(out.dtype)
         label = jnp.zeros((LABEL, LANES), jnp.float32) + table[FACTS, ORBITAL].astype(jnp.float32)
         out[blocks * aux :, :] = label.astype(out.dtype)
         held[:local] = own[...]
@@ -214,19 +213,59 @@
 def ladder_build(table, held, factor):
     empty, tile = held.shape[0] - 1, held.shape[1]
     width = factor.shape[0]
-    pairs = -(-(width // tile) // 2)
-
-    def body(table, held, factor, left, wide):
+    tiles = width // tile
+    pairs = -(-tiles // 2)
+
+    def body(table, held, source, left, factor, wide, state, sems):
+        def load(c):
+            here = block(c, tile)
+            return pltpu.make_async_copy(source.at[:, here], factor.at[:, here], sems.at[c])
+
+        def start(c):
+            @pl.when(state[c] == 0)
+            def _():
+                load(c).start()
+                state[c] = 1
+
+        def wait(c):
+            @pl.when(state[c] == 1)
+            def _():
+                load(c).wait()
+                state[c] = 2
+
+        for c in range(tiles):
+            state[c] = 0
+        used = table[FACTS, USED]
+        kept = table[BEGIN, used]
+
+        def start_slot(k, carry):
+            start(table[COLUMN, table[SORTED, k]])
+            return carry
+
+        def start_rest(c, carry):
+            start(c)
+            return carry
+
+        lax.fori_loop(0, kept, start_slot, 0)
+        lax.fori_loop(0, tiles, start_rest, 0)
+
         def two_tiles(m, carry):
             first, second, end = [table[BEGIN, 2 * m + k] for k in range(3)]
             here = block(m, 2 * tile)
 
+            def wait_slot(k, carry):
+                wait(table[COLUMN, table[SORTED, k]])
+                return carry
+
+            lax.fori_loop(first, end, wait_slot, 0)
+
             def product(at, count):
                 columns, weights = [], []
                 for k in range(count):
-                    s = jnp.where(at + k < end, table[SORTED, jnp.minimum(at + k, empty)], empty)
+                    there = at + k < end
+                    s = table[SORTED, jnp.where(there, at + k, first)]
                     columns.append(factor[:, block(table[COLUMN, s], tile)])
-                    value, none = held[s], jnp.zeros((tile, tile), held.dtype)
+                    value, none = held[jnp.where(there, s, empty)], jnp.zeros((tile, tile), held.dtype)
                     early = at + k < second
                     weights.append(
                         jnp.concatenate([jnp.where(early, value, none), jnp.where(early, none, value)], axis=1)
@@ -256,10 +295,31 @@
 
             return carry
 
-        lax.fori_loop(0, (table[FACTS, USED] + 1) // 2, two_tiles, 0)
-
-    wide = pltpu.VMEM((width, 2 * tile), jnp.float32)
-    return ladder_call(body, (width, 2 * pairs * tile), [wide], in_smem(table), held, factor, flops=10**10)
+        lax.fori_loop(0, (used + 1) // 2, two_tiles, 0)
+
+        def wait_rest(c, carry):
+            wait(c)
+            return carry
+
+        lax.fori_loop(0, tiles, wait_rest, 0)
+
+    return pl.pallas_call(
+        body,
+        out_shape=[
+            jax.ShapeDtypeStruct((width, 2 * pairs * tile), jnp.bfloat16),
+            jax.ShapeDtypeStruct(factor.shape, factor.dtype),
+        ],
+        in_specs=[SMEM, VMEM, HBM],
+        out_specs=[VMEM, VMEM],
+        scratch_shapes=[
+            pltpu.VMEM((width, 2 * tile), jnp.float32),
+            pltpu.SMEM((tiles,), jnp.int32),
+            pltpu.SemaphoreType.DMA((tiles,)),
+        ],
+        compiler_params=params(32),
+        cost_estimate=pl.CostEstimate(flops=10**10, bytes_accessed=1, transcendentals=0),
+        name="ladder_build",
+    )(in_smem(table), held, in_hbm(factor))
 
 
 def ladder_multiply(table, left, factor, tile, *, far, flops):
@@ -360,8 +420,8 @@
     swap = [(0, 1), (1, 0)]
     other = lax.ppermute(own, "virt", swap)
     square = pairs == 8
-    table, own, cycle_rows, start = prepare(tile_coords[0].T, tile_mask, pair_orbs, place, own, cycle_factor)
-    message, held = intermediate(table, own, other, cycle_rows, start, cores=cores)
+    table, own, cycle_rows, start = prepare(tile_coords[0].T, tile_mask, pair_orbs, place, own, cycle_factor, cores=cores)
+    message, held = intermediate(table, own, other, cycle_rows, start)
     factor = ladder_factor[0]
     tile = held.shape[1]
 
@@ -373,7 +433,7 @@
         arrival = exchange(message, ORDERS[0][0], ORDERS[1][0])
         message, pair_orbs, held, factor = lax.optimization_barrier((message, pair_orbs, held, factor))
         next_orbs = exchange(pair_orbs, ORDERS[0][2], ORDERS[1][1])
-        left = ladder_build(table, held, factor)
+        left, factor = ladder_build(table, held, factor)
         arrival, left = lax.optimization_barrier((arrival, left))
         kept, message = step(table, next_orbs, message, arrival, plain=0)
         message, left = lax.optimization_barrier((message, left))
@@ -388,7 +448,7 @@
         arrival, near = lax.optimization_barrier((arrival, near))
         sums = last_step(kept, arrival)
     else:
-        left = ladder_build(table, held, factor)
+        left, factor = ladder_build(table, held, factor)
         far = ladder_multiply(table, left, factor, tile, far=True, flops=10**10)
         near = ladder_multiply(table, left, factor, tile, far=False, flops=10**10)
         arrived = lax.ppermute(far, "virt", swap)

time: 27.8 us -> 27.2 us (0.978)
  Pallas kernels: 15.6 us -> 13.7 us
  waiting for transfers between devices: 1.57 us -> 3.22 us
    pallas_call x3 -> x2, Pallas kernels: 9.61 us -> 4.68 us  [ladder_call(): pl.pallas_call(body, out_shape=jax.ShapeDtypeStruct(shape, jnp.bfloat16),...]
    pallas_call x0 -> x1, Pallas kernels: none -> 3.59 us  [ladder_build(): pl.pallas_call(body, out_shape=[jax.ShapeDtypeStruct((width, 2 * pairs *...]
    ppermute x4, waiting for transfers between devices: 1.47 us -> 3.22 us  [exchange(): return lax.ppermute(value, ('pair', 'virt'), routes)]
    pallas_call x1, Pallas kernels: 2.63 us -> 2.14 us  [prepare(): pl.pallas_call(body, out_shape=[pltpu.SMEM((7, places), jnp.int32), jax.S...]
    ppermute x4, starting transfers between devices: 9.48 us -> 9.05 us  [exchange(): return lax.ppermute(value, ('pair', 'virt'), routes)]
  transfers between devices with their start and end apart: 7 -> 7, of which waited for: 4 -> 2; matrix products, arithmetic and copies ran while one was open for 0% -> 0% of each run, Pallas kernels for 49% -> 43%
where the time goes in v7:
time: 27.2 us; the launch traced here: 27.1 us
  Pallas kernels  13.7 us (50%)
  starting transfers between devices  9.96 us (37%)
  waiting for transfers between devices  3.22 us (12%)
    ppermute x4, starting transfers between devices, exchange(): return lax.ppermute(value, ('pair', 'virt'), routes)  9.05 us
    pallas_call x2, Pallas kernels, ladder_call(): pl.pallas_call(body, out_shape=jax.ShapeDtypeStruct(shape, jnp.bfloat16),...  4.68 us
    pallas_call x1, Pallas kernels, ladder_build(): pl.pallas_call(body, out_shape=[jax.ShapeDtypeStruct((width, 2 * pairs *...  3.59 us
    ppermute x4, waiting for transfers between devices, exchange(): return lax.ppermute(value, ('pair', 'virt'), routes)  3.22 us
    pallas_call x2, Pallas kernels, finish(): pl.pallas_call(body, out_shape=jax.ShapeDtypeStruct((half, 2 * half), jnp...  2.63 us
    pallas_call x1, Pallas kernels, prepare(): pl.pallas_call(body, out_shape=[pltpu.SMEM((7, places), jnp.int32), jax.S...  2.14 us
  transfers between devices with their start and end apart: 7, of which 2 were waited for; matrix products, arithmetic and copies ran while one was open for 0% of the time, Pallas kernels for 43%

profile of v7, /device:TPU:0, one launch (start us, length us, event | category | flops | bytes accessed | tf_op | source)
XLA Modules:
  0.0 27.1 jit_solution(5074631256855715472)
XLA Ops:
  0.0 0.5 %collective-permute-start = (bf16[8,128,128]{2,1,0:T(8,128)(2,1)}, bf16[8,128,128]{2,1,0:T(8,128)(2,1)S(1)}, u32[]{:S(2)}, u32[]{:S(2)}) collective-permute-start(bf16[8,128,128]{2,1,0:T(8,128)(2,1)} %bitcast.7), channel_id=1, source_target_pairs={{0,1},{1,0},{2,3},{3,2},{4,5},{5,4},{6,7},{7,6},{8,9},{9,8},{10,11... | collective-permute-start | bytes 786440 | tf_op jit(solution)/shard_map/ppermute | solution.py:421
  0.5 0.0 copy-start
  0.5 2.1 %prepare.1 = (s32[7,17]{1,0:T(8,128)S(4)}, bf16[8,128,128]{2,1,0:T(8,128)(2,1)S(1)}, bf16[1536,128]{1,0:T(8,128)(2,1)S(1)}, f32[128,768]{1,0:T(8,128)S(1)}) custom-call(s32[2,16]{1,0:T(2,128)} %bitcast.9, s32[1,16]{1,0:T(1,128)} %mask.1, s32[1,2]{1,0:T(1,128)} %orbs.1, s32[1]{0:T(128)} %bitcast.2.place, bf16[8,128,128]{2,1,0:T(8,128)(2,1)} %bitcast.8, ...), custom_call_target="tpu_custom_call" | custom-call | tf_op jit(solution)/shard_map/prepare/pallas_call | solution.py:107
  2.6 0.0 collective-permute-done.other
  2.6 0.3 %intermediate.1 = (bf16[784,128]{1,0:T(8,128)(2,1)S(1)}, bf16[17,128,128]{2,1,0:T(8,128)(2,1)S(1)}) custom-call(s32[7,17]{1,0:T(8,128)S(4)} %get-tuple-element.32.table, bf16[8,128,128]{2,1,0:T(8,128)(2,1)S(1)} %get-tuple-element.33.own, bf16[8,128,128]{2,1,0:T(8,128)(2,1)S(1)} %collective-permute-done.other, ...), custom_call_target="tpu_custom_call" | custom-call | tf_op jit(solution)/shard_map/intermediate/pallas_call | solution.py:145
  2.9 3.7 %collective-permute-start.2 = (bf16[784,128]{1,0:T(8,128)(2,1)S(1)}, bf16[784,128]{1,0:T(8,128)(2,1)S(1)}, u32[]{:S(2)}, u32[]{:S(2)}) collective-permute-start(bf16[784,128]{1,0:T(8,128)(2,1)S(1)} %get-tuple-element.39.mine), channel_id=1, source_target_pairs={{0,8},{1,5},{2,10},{3,7},{4,12},{5,1},{6,14},{7,3},{8,0},{9,13},{1... | collective-permute-start | bytes 602120 | tf_op jit(solution)/shard_map/ppermute | solution.py:430
  6.6 0.0 copy-done
  6.6 1.5 %collective-permute-start.1 = (s32[1,2]{1,0:T(1,128)S(1)}, s32[1,2]{1,0:T(1,128)S(1)}, u32[]{:S(2)}, u32[]{:S(2)}) collective-permute-start(s32[1,2]{1,0:T(1,128)S(1)} %copy-done), channel_id=1, source_target_pairs={{0,2},{1,3},{2,0},{3,1},{4,6},{5,7},{6,4},{7,5},{8,10},{9,11},{10,... | collective-permute-start | bytes 32 | tf_op jit(solution)/shard_map/ppermute | solution.py:430
  8.1 3.6 %ladder_build.1 = (bf16[1536,1536]{1,0:T(8,128)(2,1)S(1)}, bf16[1536,1536]{1,0:T(8,128)(2,1)S(1)}) custom-call(s32[7,17]{1,0:T(8,128)S(4)} %get-tuple-element.32.table, bf16[17,128,128]{2,1,0:T(8,128)(2,1)S(1)} %get-tuple-element.40.held, bf16[1536,1536]{1,0:T(8,128)(2,1)} %bitcast.10), custom_call_target="tpu_custom_call" | custom-call | flops 10000000000 | bytes 1 | tf_op jit(solution)/shard_map/ladder_build/pallas_call | solution.py:306
  11.7 0.0 collective-permute-done.2.arrival
  11.7 0.0 collective-permute-done.1.next_orbs
  11.7 0.1 step.2
  11.8 2.4 %collective-permute-start.3 = (bf16[784,128]{1,0:T(8,128)(2,1)S(1)}, bf16[784,128]{1,0:T(8,128)(2,1)S(1)}, u32[]{:S(2)}, u32[]{:S(2)}) collective-permute-start(bf16[784,128]{1,0:T(8,128)(2,1)S(1)} %get-tuple-element.47), channel_id=1, source_target_pairs={{0,4},{1,3},{2,6},{3,1},{4,0},{5,7},{6,2},{7,5},{8,12},{9,11},{10,... | collective-permute-start | bytes 602120 | tf_op jit(solution)/shard_map/ppermute | solution.py:430
  14.2 2.2 %ladder.2 = bf16[2,768,768]{2,1,0:T(8,128)(2,1)S(1)} custom-call(s32[7,17]{1,0:T(8,128)S(4)} %get-tuple-element.32.table, bf16[1536,1536]{1,0:T(8,128)(2,1)S(1)} %get-tuple-element.55.left, bf16[1536,1536]{1,0:T(8,128)(2,1)S(1)} %get-tuple-element.49.factor), custom_call_target="tpu_custom_call" | custom-call | flops 10000000000 | bytes 1 | tf_op jit(solution)/shard_map/ladder/pallas_call | solution.py:355
  16.4 1.4 %collective-permute-done.3.arrival = bf16[784,128]{1,0:T(8,128)(2,1)S(1)} collective-permute-done((bf16[784,128]{1,0:T(8,128)(2,1)S(1)}, bf16[784,128]{1,0:T(8,128)(2,1)S(1)}, u32[]{:S(2)}, u32[]{:S(2)}) %collective-permute-start.3) | collective-permute-done | bytes 200736 | tf_op jit(solution)/shard_map/ppermute | solution.py:430
  17.9 0.2 step.3
  18.1 1.6 %collective-permute-start.4 = (bf16[784,128]{1,0:T(8,128)(2,1)S(1)}, bf16[784,128]{1,0:T(8,128)(2,1)S(1)}, u32[]{:S(2)}, u32[]{:S(2)}) collective-permute-start(bf16[784,128]{1,0:T(8,128)(2,1)S(1)} %get-tuple-element.54), channel_id=1, source_target_pairs={{0,2},{1,9},{2,0},{3,11},{4,6},{5,13},{6,4},{7,15},{8,10},{9,1},{1... | collective-permute-start | bytes 602120 | tf_op jit(solution)/shard_map/ppermute | solution.py:430
  19.6 0.0 collective-permute-start.6
  19.6 2.4 %ladder.3.near = bf16[2,768,768]{2,1,0:T(8,128)(2,1)S(1)} custom-call(s32[7,17]{1,0:T(8,128)S(4)} %get-tuple-element.32.table, bf16[1536,1536]{1,0:T(8,128)(2,1)S(1)} %get-tuple-element.55.left, bf16[1536,1536]{1,0:T(8,128)(2,1)S(1)} %get-tuple-element.49.factor), custom_call_target="tpu_custom_call" | custom-call | flops 40000000000 | bytes 1 | tf_op jit(solution)/shard_map/ladder/pallas_call | solution.py:355
  22.1 1.8 %collective-permute-done.4.arrival = bf16[784,128]{1,0:T(8,128)(2,1)S(1)} collective-permute-done((bf16[784,128]{1,0:T(8,128)(2,1)S(1)}, bf16[784,128]{1,0:T(8,128)(2,1)S(1)}, u32[]{:S(2)}, u32[]{:S(2)}) %collective-permute-start.4) | collective-permute-done | bytes 200736 | tf_op jit(solution)/shard_map/ppermute | solution.py:430
  23.9 0.5 %collective-permute-start.5 = (bf16[768,128]{1,0:T(8,128)(2,1)S(1)}, bf16[768,128]{1,0:T(8,128)(2,1)S(1)}, u32[]{:S(2)}, u32[]{:S(2)}) collective-permute-start(bf16[768,128]{1,0:T(8,128)(2,1)S(1)} %last_step.1.sums), channel_id=1, source_target_pairs={{0,1},{1,0},{2,3},{3,2},{4,5},{5,4},{6,7},{7,6},{8,9},{9,8},{10,11... | collective-permute-start | bytes 589832 | tf_op jit(solution)/shard_map/ppermute | solution.py:461
  24.3 0.0 collective-permute-done.6.arrived
  24.3 1.3 %finish_own.1.refs_0_ = bf16[768,1536]{1,0:T(8,128)(2,1)} custom-call(s32[7,17]{1,0:T(8,128)S(4)} %get-tuple-element.32.table, bf16[768,128]{1,0:T(8,128)(2,1)S(1)} %last_step.1.sums, bf16[2,768,768]{2,1,0:T(8,128)(2,1)S(1)} %ladder.3.near, bf16[2,768,768]{2,1,0:T(8,128)(2,1)S(1)} %collective-permute-done.6.arrived, ...), custom_call_target="tpu_custom_call" | custom-call | flops 1000000000 | bytes 1 | tf_op jit(solution)/shard_map/finish_own/pallas_call | solution.py:398
  25.6 0.0 collective-permute-done.5.sums
  25.7 1.3 %finish_other.1 = bf16[768,1536]{1,0:T(8,128)(2,1)} custom-call(s32[7,17]{1,0:T(8,128)S(4)} %get-tuple-element.32.table, bf16[768,128]{1,0:T(8,128)(2,1)S(1)} %collective-permute-done.5.sums, bf16[2,768,768]{2,1,0:T(8,128)(2,1)S(1)} %ladder.3.near, bf16[2,768,768]{2,1,0:T(8,128)(2,1)S(1)} %collective-permute-done.6.arrived, ...), custom_call_target="tpu_custom_call", output_to_operand_aliasing={{}: (5, {})} | custom-call | flops 1000000000 | bytes 1 | tf_op jit(solution)/shard_map/finish_other/pallas_call | solution.py:398
  (1 shorter events, 0.0 us)
Async XLA Ops:
  0.0 2.6 %collective-permute-start = (bf16[8,128,128]{2,1,0:T(8,128)(2,1)}, bf16[8,128,128]{2,1,0:T(8,128)(2,1)S(1)}, u32[]{:S(2)}, u32[]{:S(2)}) collective-permute-start(bf16[8,128,128]{2,1,0:T(8,128)(2,1)} %bitcast.7), channel_id=1, source_target_pairs={{0,1},{1,0},{2,3},{3,2},{4,5},{5,4},{6,7},{7,6},{8,9},{9,8},{10,11... | collective-permute-start | bytes 786440 | tf_op jit(solution)/shard_map/ppermute | solution.py:421
  0.5 6.1 %copy-start = (s32[1,2]{1,0:T(1,128)S(1)}, s32[1,2]{1,0:T(1,128)}, u32[]{:S(2)}) copy-start(s32[1,2]{1,0:T(1,128)} %orbs.1) | copy-start | bytes 28
  2.9 8.7 %collective-permute-start.2 = (bf16[784,128]{1,0:T(8,128)(2,1)S(1)}, bf16[784,128]{1,0:T(8,128)(2,1)S(1)}, u32[]{:S(2)}, u32[]{:S(2)}) collective-permute-start(bf16[784,128]{1,0:T(8,128)(2,1)S(1)} %get-tuple-element.39.mine), channel_id=1, source_target_pairs={{0,8},{1,5},{2,10},{3,7},{4,12},{5,1},{6,14},{7,3},{8,0},{9,13},{1... | collective-permute-start | bytes 602120 | tf_op jit(solution)/shard_map/ppermute | solution.py:430
  6.6 5.1 %collective-permute-start.1 = (s32[1,2]{1,0:T(1,128)S(1)}, s32[1,2]{1,0:T(1,128)S(1)}, u32[]{:S(2)}, u32[]{:S(2)}) collective-permute-start(s32[1,2]{1,0:T(1,128)S(1)} %copy-done), channel_id=1, source_target_pairs={{0,2},{1,3},{2,0},{3,1},{4,6},{5,7},{6,4},{7,5},{8,10},{9,11},{10,... | collective-permute-start | bytes 32 | tf_op jit(solution)/shard_map/ppermute | solution.py:430
  11.8 6.0 %collective-permute-start.3 = (bf16[784,128]{1,0:T(8,128)(2,1)S(1)}, bf16[784,128]{1,0:T(8,128)(2,1)S(1)}, u32[]{:S(2)}, u32[]{:S(2)}) collective-permute-start(bf16[784,128]{1,0:T(8,128)(2,1)S(1)} %get-tuple-element.47), channel_id=1, source_target_pairs={{0,4},{1,3},{2,6},{3,1},{4,0},{5,7},{6,2},{7,5},{8,12},{9,11},{10,... | collective-permute-start | bytes 602120 | tf_op jit(solution)/shard_map/ppermute | solution.py:430
  18.1 5.8 %collective-permute-start.4 = (bf16[784,128]{1,0:T(8,128)(2,1)S(1)}, bf16[784,128]{1,0:T(8,128)(2,1)S(1)}, u32[]{:S(2)}, u32[]{:S(2)}) collective-permute-start(bf16[784,128]{1,0:T(8,128)(2,1)S(1)} %get-tuple-element.54), channel_id=1, source_target_pairs={{0,2},{1,9},{2,0},{3,11},{4,6},{5,13},{6,4},{7,15},{8,10},{9,1},{1... | collective-permute-start | bytes 602120 | tf_op jit(solution)/shard_map/ppermute | solution.py:430
  19.6 4.7 %collective-permute-start.6 = (bf16[2,768,768]{2,1,0:T(8,128)(2,1)S(1)}, bf16[2,768,768]{2,1,0:T(8,128)(2,1)S(1)}, u32[]{:S(2)}, u32[]{:S(2)}) collective-permute-start(bf16[2,768,768]{2,1,0:T(8,128)(2,1)S(1)} %ladder.2), channel_id=1, source_target_pairs={{0,1},{1,0},{2,3},{3,2},{4,5},{5,4},{6,7},{7,6},{8,9},{9,8},{10,11... | collective-permute-start | bytes 7077896 | tf_op jit(solution)/shard_map/ppermute | solution.py:446
  23.9 1.8 %collective-permute-start.5 = (bf16[768,128]{1,0:T(8,128)(2,1)S(1)}, bf16[768,128]{1,0:T(8,128)(2,1)S(1)}, u32[]{:S(2)}, u32[]{:S(2)}) collective-permute-start(bf16[768,128]{1,0:T(8,128)(2,1)S(1)} %last_step.1.sums), channel_id=1, source_target_pairs={{0,1},{1,0},{2,3},{3,2},{4,5},{5,4},{6,7},{7,6},{8,9},{9,8},{10,11... | collective-permute-start | bytes 589832 | tf_op jit(solution)/shard_map/ppermute | solution.py:461

commit v8 on v7

--- a/solution.py
+++ b/solution.py
@@ -53,25 +53,24 @@
     tiles, tiles_here = width // tile, width // tile // cores
     places = max(slots + 1, tiles + 3)
 
-    def body(coords, mask, orbs, place, own, factor, table, held, rows, total, s_coords, s_mask, s_orbs, count, sems):
+    def body(coords, mask, orbs, place, own, factor, table, held, rows, total, s_coords, s_mask, count, sems):
         loads = [
             pltpu.make_async_copy(source, target, sems.at[n])
-            for n, (source, target) in enumerate([(orbs, s_orbs), (coords, s_coords), (mask, s_mask), (own, held)])
+            for n, (source, target) in enumerate([(coords, s_coords), (mask, s_mask), (own, held)])
         ]
         for load in loads:
             load.start()
         core = place[0]
         total[...] = jnp.zeros_like(total)
-        loads[0].wait()
-        load_rows = pltpu.make_async_copy(factor.at[s_orbs[0, 0]], rows, sems.at[4])
+        load_rows = pltpu.make_async_copy(factor.at[orbs[0, 0]], rows, sems.at[4])
         load_rows.start()
         table[FACTS, CORE] = core
-        table[FACTS, ORBITAL] = s_orbs[0, 1]
+        table[FACTS, ORBITAL] = orbs[0, 1]
 
         for n in range(tiles):
             count[n] = 0
+        loads[0].wait()
         loads[1].wait()
-        loads[2].wait()
         for s in range(slots):
             g = lax.rem(s + core * local, slots)
             d, kept = s_coords[1, g], s_mask[0, g]
@@ -100,7 +99,7 @@
             at = count[d]
             table[SORTED, jnp.where(kept, at, slots)] = s
             count[d] = at + kept.astype(jnp.int32)
-        loads[3].wait()
+        loads[2].wait()
         load_rows.wait()
         add_terms(total, table, rows, held, range(local))
 
@@ -112,18 +111,17 @@
             jax.ShapeDtypeStruct((width, aux), jnp.bfloat16),
             jax.ShapeDtypeStruct((aux, width // cores), jnp.float32),
         ],
-        in_specs=[HBM, HBM, HBM, SMEM, HBM, HBM],
+        in_specs=[HBM, HBM, SMEM, SMEM, HBM, HBM],
         out_specs=[SMEM, VMEM, VMEM, VMEM],
         scratch_shapes=[
             pltpu.SMEM(coords.shape, jnp.int32),
             pltpu.SMEM(mask.shape, jnp.int32),
-            pltpu.SMEM(orbs.shape, jnp.int32),
             pltpu.SMEM((tiles,), jnp.int32),
             pltpu.SemaphoreType.DMA((5,)),
         ],
         compiler_params=params(16),
         name="prepare",
-    )(in_hbm(coords), in_hbm(mask), in_hbm(orbs), place, in_hbm(own), in_hbm(cycle_factor))
+    )(in_hbm(coords), in_hbm(mask), in_smem(orbs), place, in_hbm(own), in_hbm(cycle_factor))
 
 
 def intermediate(table, own, other, rows, start):

time: 27.2 us -> 27.1 us (level)
  Pallas kernels: 13.7 us -> 16.2 us
  waiting for transfers between devices: 3.22 us -> 1.24 us
  starting transfers between devices: 9.96 us -> 9.17 us
    pallas_call x2, Pallas kernels: 4.68 us -> 6.92 us  [ladder_call(): pl.pallas_call(body, out_shape=jax.ShapeDtypeStruct(shape, jnp.bfloat16),...]
    ppermute x4, waiting for transfers between devices: 3.22 us -> 1.23 us  [exchange(): return lax.ppermute(value, ('pair', 'virt'), routes)]
    ppermute x4, starting transfers between devices: 9.05 us -> 8.54 us  [exchange(): return lax.ppermute(value, ('pair', 'virt'), routes)]
    pallas_call x1, Pallas kernels: 3.59 us -> 3.98 us  [ladder_build(): pl.pallas_call(body, out_shape=[jax.ShapeDtypeStruct((width, 2 * pairs *...]
    ppermute x1, starting transfers between devices: 0.45 us -> 0.18 us  [shards(): other_sums = lax.ppermute(sums, 'virt', swap)]
  transfers between devices with their start and end apart: 7 -> 7, of which waited for: 2 -> 2; matrix products, arithmetic and copies ran while one was open for 0% -> 0% of each run, Pallas kernels for 43% -> 53%
where the time goes in v8:
time: 27.1 us; the launch traced here: 26.9 us
  Pallas kernels  16.2 us (60%)
  starting transfers between devices  9.17 us (34%)
  waiting for transfers between devices  1.24 us (5%)
    ppermute x4, starting transfers between devices, exchange(): return lax.ppermute(value, ('pair', 'virt'), routes)  8.54 us
    pallas_call x2, Pallas kernels, ladder_call(): pl.pallas_call(body, out_shape=jax.ShapeDtypeStruct(shape, jnp.bfloat16),...  6.92 us
    pallas_call x1, Pallas kernels, ladder_build(): pl.pallas_call(body, out_shape=[jax.ShapeDtypeStruct((width, 2 * pairs *...  3.98 us
    pallas_call x2, Pallas kernels, finish(): pl.pallas_call(body, out_shape=jax.ShapeDtypeStruct((half, 2 * half), jnp...  2.63 us
    pallas_call x1, Pallas kernels, prepare(): pl.pallas_call(body, out_shape=[pltpu.SMEM((7, places), jnp.int32), jax.S...  2.07 us
    ppermute x4, waiting for transfers between devices, exchange(): return lax.ppermute(value, ('pair', 'virt'), routes)  1.23 us
  transfers between devices with their start and end apart: 7, of which 2 were waited for; matrix products, arithmetic and copies ran while one was open for 0% of the time, Pallas kernels for 53%

profile of v8, /device:TPU:0, one launch (start us, length us, event | category | flops | bytes accessed | tf_op | source)
XLA Modules:
  0.0 26.9 jit_solution(4763433702508505238)
XLA Ops:
  0.0 0.5 %collective-permute-start = (bf16[8,128,128]{2,1,0:T(8,128)(2,1)}, bf16[8,128,128]{2,1,0:T(8,128)(2,1)S(1)}, u32[]{:S(2)}, u32[]{:S(2)}) collective-permute-start(bf16[8,128,128]{2,1,0:T(8,128)(2,1)} %bitcast.7), channel_id=1, source_target_pairs={{0,1},{1,0},{2,3},{3,2},{4,5},{5,4},{6,7},{7,6},{8,9},{9,8},{10,11... | collective-permute-start | bytes 786440 | tf_op jit(solution)/shard_map/ppermute | solution.py:419
  0.5 2.1 %prepare.1 = (s32[7,17]{1,0:T(8,128)S(4)}, bf16[8,128,128]{2,1,0:T(8,128)(2,1)S(1)}, bf16[1536,128]{1,0:T(8,128)(2,1)S(1)}, f32[128,768]{1,0:T(8,128)S(1)}) custom-call(s32[2,16]{1,0:T(2,128)} %bitcast.9, s32[1,16]{1,0:T(1,128)} %mask.1, s32[1,2]{1,0:T(1,128)} %orbs.1, s32[1]{0:T(128)} %bitcast.2.place, bf16[8,128,128]{2,1,0:T(8,128)(2,1)} %bitcast.8, ...), custom_call_target="tpu_custom_call" | custom-call | tf_op jit(solution)/shard_map/prepare/pallas_call | solution.py:106
  2.5 0.0 collective-permute-done.other
  2.5 0.3 %intermediate.1 = (bf16[784,128]{1,0:T(8,128)(2,1)S(1)}, bf16[17,128,128]{2,1,0:T(8,128)(2,1)S(1)}) custom-call(s32[7,17]{1,0:T(8,128)S(4)} %get-tuple-element.32.table, bf16[8,128,128]{2,1,0:T(8,128)(2,1)S(1)} %get-tuple-element.33.own, bf16[8,128,128]{2,1,0:T(8,128)(2,1)S(1)} %collective-permute-done.other, ...), custom_call_target="tpu_custom_call" | custom-call | tf_op jit(solution)/shard_map/intermediate/pallas_call | solution.py:143
  2.9 3.7 %collective-permute-start.2 = (bf16[784,128]{1,0:T(8,128)(2,1)S(1)}, bf16[784,128]{1,0:T(8,128)(2,1)S(1)}, u32[]{:S(2)}, u32[]{:S(2)}) collective-permute-start(bf16[784,128]{1,0:T(8,128)(2,1)S(1)} %get-tuple-element.39.mine), channel_id=1, source_target_pairs={{0,8},{1,5},{2,10},{3,7},{4,12},{5,1},{6,14},{7,3},{8,0},{9,13},{1... | collective-permute-start | bytes 602120 | tf_op jit(solution)/shard_map/ppermute | solution.py:428
  6.5 1.5 %collective-permute-start.1 = (s32[1,2]{1,0:T(1,128)}, s32[1,2]{1,0:T(1,128)S(1)}, u32[]{:S(2)}, u32[]{:S(2)}) collective-permute-start(s32[1,2]{1,0:T(1,128)} %orbs.1), channel_id=1, source_target_pairs={{0,2},{1,3},{2,0},{3,1},{4,6},{5,7},{6,4},{7,5},{8,10},{9,11},{10,... | collective-permute-start | bytes 32 | tf_op jit(solution)/shard_map/ppermute | solution.py:428
  8.0 4.0 %ladder_build.1 = (bf16[1536,1536]{1,0:T(8,128)(2,1)S(1)}, bf16[1536,1536]{1,0:T(8,128)(2,1)S(1)}) custom-call(s32[7,17]{1,0:T(8,128)S(4)} %get-tuple-element.32.table, bf16[17,128,128]{2,1,0:T(8,128)(2,1)S(1)} %get-tuple-element.40.held, bf16[1536,1536]{1,0:T(8,128)(2,1)} %bitcast.10), custom_call_target="tpu_custom_call" | custom-call | flops 10000000000 | bytes 1 | tf_op jit(solution)/shard_map/ladder_build/pallas_call | solution.py:304
  12.0 0.0 collective-permute-done.2.arrival
  12.0 0.0 collective-permute-done.1.next_orbs
  12.0 0.1 step.2
  12.1 2.0 %collective-permute-start.3 = (bf16[784,128]{1,0:T(8,128)(2,1)S(1)}, bf16[784,128]{1,0:T(8,128)(2,1)S(1)}, u32[]{:S(2)}, u32[]{:S(2)}) collective-permute-start(bf16[784,128]{1,0:T(8,128)(2,1)S(1)} %get-tuple-element.47), channel_id=1, source_target_pairs={{0,4},{1,3},{2,6},{3,1},{4,0},{5,7},{6,2},{7,5},{8,12},{9,11},{10,... | collective-permute-start | bytes 602120 | tf_op jit(solution)/shard_map/ppermute | solution.py:428
  14.1 3.5 %ladder.2 = bf16[2,768,768]{2,1,0:T(8,128)(2,1)S(1)} custom-call(s32[7,17]{1,0:T(8,128)S(4)} %get-tuple-element.32.table, bf16[1536,1536]{1,0:T(8,128)(2,1)S(1)} %get-tuple-element.55.left, bf16[1536,1536]{1,0:T(8,128)(2,1)S(1)} %get-tuple-element.49.factor), custom_call_target="tpu_custom_call" | custom-call | flops 10000000000 | bytes 1 | tf_op jit(solution)/shard_map/ladder/pallas_call | solution.py:353
  17.6 0.3 %collective-permute-done.3.arrival = bf16[784,128]{1,0:T(8,128)(2,1)S(1)} collective-permute-done((bf16[784,128]{1,0:T(8,128)(2,1)S(1)}, bf16[784,128]{1,0:T(8,128)(2,1)S(1)}, u32[]{:S(2)}, u32[]{:S(2)}) %collective-permute-start.3) | collective-permute-done | bytes 200736 | tf_op jit(solution)/shard_map/ppermute | solution.py:428
  17.9 0.2 step.3
  18.1 1.4 %collective-permute-start.4 = (bf16[784,128]{1,0:T(8,128)(2,1)S(1)}, bf16[784,128]{1,0:T(8,128)(2,1)S(1)}, u32[]{:S(2)}, u32[]{:S(2)}) collective-permute-start(bf16[784,128]{1,0:T(8,128)(2,1)S(1)} %get-tuple-element.54), channel_id=1, source_target_pairs={{0,2},{1,9},{2,0},{3,11},{4,6},{5,13},{6,4},{7,15},{8,10},{9,1},{1... | collective-permute-start | bytes 602120 | tf_op jit(solution)/shard_map/ppermute | solution.py:428
  19.5 0.0 collective-permute-start.6
  19.5 3.5 %ladder.3.near = bf16[2,768,768]{2,1,0:T(8,128)(2,1)S(1)} custom-call(s32[7,17]{1,0:T(8,128)S(4)} %get-tuple-element.32.table, bf16[1536,1536]{1,0:T(8,128)(2,1)S(1)} %get-tuple-element.55.left, bf16[1536,1536]{1,0:T(8,128)(2,1)S(1)} %get-tuple-element.49.factor), custom_call_target="tpu_custom_call" | custom-call | flops 40000000000 | bytes 1 | tf_op jit(solution)/shard_map/ladder/pallas_call | solution.py:353
  23.0 0.9 %collective-permute-done.4.arrival = bf16[784,128]{1,0:T(8,128)(2,1)S(1)} collective-permute-done((bf16[784,128]{1,0:T(8,128)(2,1)S(1)}, bf16[784,128]{1,0:T(8,128)(2,1)S(1)}, u32[]{:S(2)}, u32[]{:S(2)}) %collective-permute-start.4) | collective-permute-done | bytes 200736 | tf_op jit(solution)/shard_map/ppermute | solution.py:428
  23.9 0.2 collective-permute-start.5
  24.1 0.0 collective-permute-done.6.arrived
  24.1 1.3 %finish_own.1.refs_0_ = bf16[768,1536]{1,0:T(8,128)(2,1)} custom-call(s32[7,17]{1,0:T(8,128)S(4)} %get-tuple-element.32.table, bf16[768,128]{1,0:T(8,128)(2,1)S(1)} %last_step.1.sums, bf16[2,768,768]{2,1,0:T(8,128)(2,1)S(1)} %ladder.3.near, bf16[2,768,768]{2,1,0:T(8,128)(2,1)S(1)} %collective-permute-done.6.arrived, ...), custom_call_target="tpu_custom_call" | custom-call | flops 1000000000 | bytes 1 | tf_op jit(solution)/shard_map/finish_own/pallas_call | solution.py:396
  25.4 0.0 collective-permute-done.5.sums
  25.4 1.3 %finish_other.1 = bf16[768,1536]{1,0:T(8,128)(2,1)} custom-call(s32[7,17]{1,0:T(8,128)S(4)} %get-tuple-element.32.table, bf16[768,128]{1,0:T(8,128)(2,1)S(1)} %collective-permute-done.5.sums, bf16[2,768,768]{2,1,0:T(8,128)(2,1)S(1)} %ladder.3.near, bf16[2,768,768]{2,1,0:T(8,128)(2,1)S(1)} %collective-permute-done.6.arrived, ...), custom_call_target="tpu_custom_call", output_to_operand_aliasing={{}: (5, {})} | custom-call | flops 1000000000 | bytes 1 | tf_op jit(solution)/shard_map/finish_other/pallas_call | solution.py:396
  (1 shorter events, 0.0 us)
Async XLA Ops:
  0.0 2.5 %collective-permute-start = (bf16[8,128,128]{2,1,0:T(8,128)(2,1)}, bf16[8,128,128]{2,1,0:T(8,128)(2,1)S(1)}, u32[]{:S(2)}, u32[]{:S(2)}) collective-permute-start(bf16[8,128,128]{2,1,0:T(8,128)(2,1)} %bitcast.7), channel_id=1, source_target_pairs={{0,1},{1,0},{2,3},{3,2},{4,5},{5,4},{6,7},{7,6},{8,9},{9,8},{10,11... | collective-permute-start | bytes 786440 | tf_op jit(solution)/shard_map/ppermute | solution.py:419
  2.9 9.1 %collective-permute-start.2 = (bf16[784,128]{1,0:T(8,128)(2,1)S(1)}, bf16[784,128]{1,0:T(8,128)(2,1)S(1)}, u32[]{:S(2)}, u32[]{:S(2)}) collective-permute-start(bf16[784,128]{1,0:T(8,128)(2,1)S(1)} %get-tuple-element.39.mine), channel_id=1, source_target_pairs={{0,8},{1,5},{2,10},{3,7},{4,12},{5,1},{6,14},{7,3},{8,0},{9,13},{1... | collective-permute-start | bytes 602120 | tf_op jit(solution)/shard_map/ppermute | solution.py:428
  6.5 5.5 %collective-permute-start.1 = (s32[1,2]{1,0:T(1,128)}, s32[1,2]{1,0:T(1,128)S(1)}, u32[]{:S(2)}, u32[]{:S(2)}) collective-permute-start(s32[1,2]{1,0:T(1,128)} %orbs.1), channel_id=1, source_target_pairs={{0,2},{1,3},{2,0},{3,1},{4,6},{5,7},{6,4},{7,5},{8,10},{9,11},{10,... | collective-permute-start | bytes 32 | tf_op jit(solution)/shard_map/ppermute | solution.py:428
  12.1 5.8 %collective-permute-start.3 = (bf16[784,128]{1,0:T(8,128)(2,1)S(1)}, bf16[784,128]{1,0:T(8,128)(2,1)S(1)}, u32[]{:S(2)}, u32[]{:S(2)}) collective-permute-start(bf16[784,128]{1,0:T(8,128)(2,1)S(1)} %get-tuple-element.47), channel_id=1, source_target_pairs={{0,4},{1,3},{2,6},{3,1},{4,0},{5,7},{6,2},{7,5},{8,12},{9,11},{10,... | collective-permute-start | bytes 602120 | tf_op jit(solution)/shard_map/ppermute | solution.py:428
  18.1 5.8 %collective-permute-start.4 = (bf16[784,128]{1,0:T(8,128)(2,1)S(1)}, bf16[784,128]{1,0:T(8,128)(2,1)S(1)}, u32[]{:S(2)}, u32[]{:S(2)}) collective-permute-start(bf16[784,128]{1,0:T(8,128)(2,1)S(1)} %get-tuple-element.54), channel_id=1, source_target_pairs={{0,2},{1,9},{2,0},{3,11},{4,6},{5,13},{6,4},{7,15},{8,10},{9,1},{1... | collective-permute-start | bytes 602120 | tf_op jit(solution)/shard_map/ppermute | solution.py:428
  19.5 4.6 %collective-permute-start.6 = (bf16[2,768,768]{2,1,0:T(8,128)(2,1)S(1)}, bf16[2,768,768]{2,1,0:T(8,128)(2,1)S(1)}, u32[]{:S(2)}, u32[]{:S(2)}) collective-permute-start(bf16[2,768,768]{2,1,0:T(8,128)(2,1)S(1)} %ladder.2), channel_id=1, source_target_pairs={{0,1},{1,0},{2,3},{3,2},{4,5},{5,4},{6,7},{7,6},{8,9},{9,8},{10,11... | collective-permute-start | bytes 7077896 | tf_op jit(solution)/shard_map/ppermute | solution.py:444
  23.9 1.5 %collective-permute-start.5 = (bf16[768,128]{1,0:T(8,128)(2,1)S(1)}, bf16[768,128]{1,0:T(8,128)(2,1)S(1)}, u32[]{:S(2)}, u32[]{:S(2)}) collective-permute-start(bf16[768,128]{1,0:T(8,128)(2,1)S(1)} %last_step.1.sums), channel_id=1, source_target_pairs={{0,1},{1,0},{2,3},{3,2},{4,5},{5,4},{6,7},{7,6},{8,9},{9,8},{10,11... | collective-permute-start | bytes 589832 | tf_op jit(solution)/shard_map/ppermute | solution.py:459

commit v9 on v7

--- a/solution.py
+++ b/solution.py
@@ -127,29 +127,23 @@
 
 
 def intermediate(table, own, other, rows, start):
-    local, tile = own.shape[0], own.shape[1]
+    local = own.shape[0]
     aux, width = start.shape
     blocks = width // LANES
 
-    def body(table, own, other, rows, start, out, held, total):
+    def body(table, own, other, rows, start, out, total):
         total[...] = start[...]
         add_terms(total, table, rows, other, range(local, 2 * local))
         for n in range(blocks):
             out[n * aux : (n + 1) * aux, :] = total[:, n * LANES : (n + 1) * LANES].astype(out.dtype)
         label = jnp.zeros((LABEL, LANES), jnp.float32) + table[FACTS, ORBITAL].astype(jnp.float32)
         out[blocks * aux :, :] = label.astype(out.dtype)
-        held[:local] = own[...]
-        held[local : 2 * local] = other[...]
-        held[2 * local] = jnp.zeros((tile, tile), held.dtype)
-
-    return pl.pallas_call(
-        body,
-        out_shape=[
-            jax.ShapeDtypeStruct((blocks * aux + LABEL, LANES), jnp.bfloat16),
-            jax.ShapeDtypeStruct((2 * local + 1, tile, tile), jnp.bfloat16),
-        ],
+
+    return pl.pallas_call(
+        body,
+        out_shape=jax.ShapeDtypeStruct((blocks * aux + LABEL, LANES), jnp.bfloat16),
         in_specs=[SMEM, VMEM, VMEM, VMEM, VMEM],
-        out_specs=[VMEM, VMEM],
+        out_specs=VMEM,
         scratch_shapes=[pltpu.VMEM((aux, width), jnp.float32)],
         compiler_params=params(16),
         name="intermediate",
@@ -210,13 +204,14 @@
     )(mine, arrival)
 
 
-def ladder_build(table, held, factor):
-    empty, tile = held.shape[0] - 1, held.shape[1]
+def ladder_build(table, own, other, factor):
+    local, tile = own.shape[0], own.shape[1]
+    empty = 2 * local
     width = factor.shape[0]
     tiles = width // tile
     pairs = -(-tiles // 2)
 
-    def body(table, held, source, left, factor, wide, state, sems):
+    def body(table, own, other, source, left, factor, held, wide, state, sems):
         def load(c):
             here = block(c, tile)
             return pltpu.make_async_copy(source.at[:, here], factor.at[:, here], sems.at[c])
@@ -248,6 +243,9 @@
 
         lax.fori_loop(0, kept, start_slot, 0)
         lax.fori_loop(0, tiles, start_rest, 0)
+        held[:local] = own[...]
+        held[local:empty] = other[...]
+        held[empty] = jnp.zeros((tile, tile), held.dtype)
 
         def two_tiles(m, carry):
             first, second, end = [table[BEGIN, 2 * m + k] for k in range(3)]
@@ -309,9 +307,10 @@
             jax.ShapeDtypeStruct((width, 2 * pairs * tile), jnp.bfloat16),
             jax.ShapeDtypeStruct(factor.shape, factor.dtype),
         ],
-        in_specs=[SMEM, VMEM, HBM],
+        in_specs=[SMEM, VMEM, VMEM, HBM],
         out_specs=[VMEM, VMEM],
         scratch_shapes=[
+            pltpu.VMEM((empty + 1, tile, tile), own.dtype),
             pltpu.VMEM((width, 2 * tile), jnp.float32),
             pltpu.SMEM((tiles,), jnp.int32),
             pltpu.SemaphoreType.DMA((tiles,)),
@@ -319,7 +318,7 @@
         compiler_params=params(32),
         cost_estimate=pl.CostEstimate(flops=10**10, bytes_accessed=1, transcendentals=0),
         name="ladder_build",
-    )(in_smem(table), held, in_hbm(factor))
+    )(in_smem(table), own, other, in_hbm(factor))
 
 
 def ladder_multiply(table, left, factor, tile, *, far, flops):
@@ -421,9 +420,9 @@
     other = lax.ppermute(own, "virt", swap)
     square = pairs == 8
     table, own, cycle_rows, start = prepare(tile_coords[0].T, tile_mask, pair_orbs, place, own, cycle_factor, cores=cores)
-    message, held = intermediate(table, own, other, cycle_rows, start)
+    message = intermediate(table, own, other, cycle_rows, start)
     factor = ladder_factor[0]
-    tile = held.shape[1]
+    tile = own.shape[1]
 
     def exchange(value, *partners):
         routes = [(p * 2 + c, (p ^ partners[c]) * 2 + c) for p in range(pairs) for c in range(2)]
@@ -431,9 +430,9 @@
 
     if square:
         arrival = exchange(message, ORDERS[0][0], ORDERS[1][0])
-        message, pair_orbs, held, factor = lax.optimization_barrier((message, pair_orbs, held, factor))
+        message, pair_orbs, own, other, factor = lax.optimization_barrier((message, pair_orbs, own, other, factor))
         next_orbs = exchange(pair_orbs, ORDERS[0][2], ORDERS[1][1])
-        left, factor = ladder_build(table, held, factor)
+        left, factor = ladder_build(table, own, other, factor)
         arrival, left = lax.optimization_barrier((arrival, left))
         kept, message = step(table, next_orbs, message, arrival, plain=0)
         message, left = lax.optimization_barrier((message, left))
@@ -448,7 +447,7 @@
         arrival, near = lax.optimization_barrier((arrival, near))
         sums = last_step(kept, arrival)
     else:
-        left, factor = ladder_build(table, held, factor)
+        left, factor = ladder_build(table, own, other, factor)
         far = ladder_multiply(table, left, factor, tile, far=True, flops=10**10)
         near = ladder_multiply(table, left, factor, tile, far=False, flops=10**10)
         arrived = lax.ppermute(far, "virt", swap)

time: 27.2 us -> 27.3 us (level)
  waiting for transfers between devices: 3.22 us -> 2.24 us
  Pallas kernels: 13.7 us -> 14.6 us
    pallas_call x2, Pallas kernels: 4.68 us -> 5.72 us  [ladder_call(): pl.pallas_call(body, out_shape=jax.ShapeDtypeStruct(shape, jnp.bfloat16),...]
    ppermute x4, waiting for transfers between devices: 3.22 us -> 2.23 us  [exchange(): return lax.ppermute(value, ('pair', 'virt'), routes)]
  transfers between devices with their start and end apart: 7 -> 7, of which waited for: 2 -> 2; matrix products, arithmetic and copies ran while one was open for 0% -> 0% of each run, Pallas kernels for 43% -> 47%
where the time goes in v9:
time: 27.3 us; the launch traced here: 27 us
  Pallas kernels  14.6 us (53%)
  starting transfers between devices  9.85 us (36%)
  waiting for transfers between devices  2.24 us (8%)
    ppermute x4, starting transfers between devices, exchange(): return lax.ppermute(value, ('pair', 'virt'), routes)  9.13 us
    pallas_call x2, Pallas kernels, ladder_call(): pl.pallas_call(body, out_shape=jax.ShapeDtypeStruct(shape, jnp.bfloat16),...  5.72 us
    pallas_call x1, Pallas kernels, ladder_build(): pl.pallas_call(body, out_shape=[jax.ShapeDtypeStruct((width, 2 * pairs *...  3.52 us
    pallas_call x2, Pallas kernels, finish(): pl.pallas_call(body, out_shape=jax.ShapeDtypeStruct((half, 2 * half), jnp...  2.63 us
    ppermute x4, waiting for transfers between devices, exchange(): return lax.ppermute(value, ('pair', 'virt'), routes)  2.23 us
    pallas_call x1, Pallas kernels, prepare(): pl.pallas_call(body, out_shape=[pltpu.SMEM((7, places), jnp.int32), jax.S...  2.13 us
  transfers between devices with their start and end apart: 7, of which 2 were waited for; matrix products, arithmetic and copies ran while one was open for 0% of the time, Pallas kernels for 47%

profile of v9, /device:TPU:0, one launch (start us, length us, event | category | flops | bytes accessed | tf_op | source)
XLA Modules:
  0.0 27.0 jit_solution(3053817174375577520)
XLA Ops:
  0.0 0.5 %collective-permute-start = (bf16[8,128,128]{2,1,0:T(8,128)(2,1)}, bf16[8,128,128]{2,1,0:T(8,128)(2,1)S(1)}, u32[]{:S(2)}, u32[]{:S(2)}) collective-permute-start(bf16[8,128,128]{2,1,0:T(8,128)(2,1)} %bitcast.7), channel_id=1, source_target_pairs={{0,1},{1,0},{2,3},{3,2},{4,5},{5,4},{6,7},{7,6},{8,9},{9,8},{10,11... | collective-permute-start | bytes 786440 | tf_op jit(solution)/shard_map/ppermute | solution.py:420
  0.5 0.0 copy-start
  0.5 2.1 %prepare.1 = (s32[7,17]{1,0:T(8,128)S(4)}, bf16[8,128,128]{2,1,0:T(8,128)(2,1)S(1)}, bf16[1536,128]{1,0:T(8,128)(2,1)S(1)}, f32[128,768]{1,0:T(8,128)S(1)}) custom-call(s32[2,16]{1,0:T(2,128)} %bitcast.9, s32[1,16]{1,0:T(1,128)} %mask.1, s32[1,2]{1,0:T(1,128)} %orbs.1, s32[1]{0:T(128)} %bitcast.2.place, bf16[8,128,128]{2,1,0:T(8,128)(2,1)} %bitcast.8, ...), custom_call_target="tpu_custom_call" | custom-call | tf_op jit(solution)/shard_map/prepare/pallas_call | solution.py:107
  2.6 0.0 collective-permute-done.other
  2.6 0.3 %intermediate.1.mine = bf16[784,128]{1,0:T(8,128)(2,1)S(1)} custom-call(s32[7,17]{1,0:T(8,128)S(4)} %get-tuple-element.31.table, bf16[8,128,128]{2,1,0:T(8,128)(2,1)S(1)} %get-tuple-element.37.own, bf16[8,128,128]{2,1,0:T(8,128)(2,1)S(1)} %collective-permute-done.other, bf16[1536,128]{1,0:T(8,128)(2,1)S(1)} %get-tuple-element.33.rows.factor, ...), custom_call_target="tpu_custom_call" | custom-call | tf_op jit(solution)/shard_map/intermediate/pallas_call | solution.py:142
  2.9 3.7 %collective-permute-start.2 = (bf16[784,128]{1,0:T(8,128)(2,1)S(1)}, bf16[784,128]{1,0:T(8,128)(2,1)S(1)}, u32[]{:S(2)}, u32[]{:S(2)}) collective-permute-start(bf16[784,128]{1,0:T(8,128)(2,1)S(1)} %intermediate.1.mine), channel_id=1, source_target_pairs={{0,8},{1,5},{2,10},{3,7},{4,12},{5,1},{6,14},{7,3},{8,0},{9,13},{1... | collective-permute-start | bytes 602120 | tf_op jit(solution)/shard_map/ppermute | solution.py:429
  6.6 0.0 copy-done
  6.6 1.5 %collective-permute-start.1 = (s32[1,2]{1,0:T(1,128)S(1)}, s32[1,2]{1,0:T(1,128)S(1)}, u32[]{:S(2)}, u32[]{:S(2)}) collective-permute-start(s32[1,2]{1,0:T(1,128)S(1)} %copy-done), channel_id=1, source_target_pairs={{0,2},{1,3},{2,0},{3,1},{4,6},{5,7},{6,4},{7,5},{8,10},{9,11},{10,... | collective-permute-start | bytes 32 | tf_op jit(solution)/shard_map/ppermute | solution.py:429
  8.1 3.5 %ladder_build.1 = (bf16[1536,1536]{1,0:T(8,128)(2,1)S(1)}, bf16[1536,1536]{1,0:T(8,128)(2,1)S(1)}) custom-call(s32[7,17]{1,0:T(8,128)S(4)} %get-tuple-element.31.table, bf16[8,128,128]{2,1,0:T(8,128)(2,1)S(1)} %get-tuple-element.37.own, bf16[8,128,128]{2,1,0:T(8,128)(2,1)S(1)} %collective-permute-done.other, bf16[1536,1536]{1,0:T(8,128)(2,1)} %bitcast.10), custom_call_target="tpu_custom_call" | custom-call | flops 10000000000 | bytes 1 | tf_op jit(solution)/shard_map/ladder_build/pallas_call | solution.py:304
  11.6 0.0 collective-permute-done.2.arrival
  11.6 0.0 collective-permute-done.1.next_orbs
  11.6 0.1 step.2
  11.7 2.5 %collective-permute-start.3 = (bf16[784,128]{1,0:T(8,128)(2,1)S(1)}, bf16[784,128]{1,0:T(8,128)(2,1)S(1)}, u32[]{:S(2)}, u32[]{:S(2)}) collective-permute-start(bf16[784,128]{1,0:T(8,128)(2,1)S(1)} %get-tuple-element.45), channel_id=1, source_target_pairs={{0,4},{1,3},{2,6},{3,1},{4,0},{5,7},{6,2},{7,5},{8,12},{9,11},{10,... | collective-permute-start | bytes 602120 | tf_op jit(solution)/shard_map/ppermute | solution.py:429
  14.2 2.9 %ladder.2 = bf16[2,768,768]{2,1,0:T(8,128)(2,1)S(1)} custom-call(s32[7,17]{1,0:T(8,128)S(4)} %get-tuple-element.31.table, bf16[1536,1536]{1,0:T(8,128)(2,1)S(1)} %get-tuple-element.53.left, bf16[1536,1536]{1,0:T(8,128)(2,1)S(1)} %get-tuple-element.47.factor), custom_call_target="tpu_custom_call" | custom-call | flops 10000000000 | bytes 1 | tf_op jit(solution)/shard_map/ladder/pallas_call | solution.py:354
  17.1 0.8 %collective-permute-done.3.arrival = bf16[784,128]{1,0:T(8,128)(2,1)S(1)} collective-permute-done((bf16[784,128]{1,0:T(8,128)(2,1)S(1)}, bf16[784,128]{1,0:T(8,128)(2,1)S(1)}, u32[]{:S(2)}, u32[]{:S(2)}) %collective-permute-start.3) | collective-permute-done | bytes 200736 | tf_op jit(solution)/shard_map/ppermute | solution.py:429
  17.9 0.2 step.3
  18.1 1.5 %collective-permute-start.4 = (bf16[784,128]{1,0:T(8,128)(2,1)S(1)}, bf16[784,128]{1,0:T(8,128)(2,1)S(1)}, u32[]{:S(2)}, u32[]{:S(2)}) collective-permute-start(bf16[784,128]{1,0:T(8,128)(2,1)S(1)} %get-tuple-element.52), channel_id=1, source_target_pairs={{0,2},{1,9},{2,0},{3,11},{4,6},{5,13},{6,4},{7,15},{8,10},{9,1},{1... | collective-permute-start | bytes 602120 | tf_op jit(solution)/shard_map/ppermute | solution.py:429
  19.6 0.0 collective-permute-start.6
  19.6 2.9 %ladder.3.near = bf16[2,768,768]{2,1,0:T(8,128)(2,1)S(1)} custom-call(s32[7,17]{1,0:T(8,128)S(4)} %get-tuple-element.31.table, bf16[1536,1536]{1,0:T(8,128)(2,1)S(1)} %get-tuple-element.53.left, bf16[1536,1536]{1,0:T(8,128)(2,1)S(1)} %get-tuple-element.47.factor), custom_call_target="tpu_custom_call" | custom-call | flops 40000000000 | bytes 1 | tf_op jit(solution)/shard_map/ladder/pallas_call | solution.py:354
  22.5 1.4 %collective-permute-done.4.arrival = bf16[784,128]{1,0:T(8,128)(2,1)S(1)} collective-permute-done((bf16[784,128]{1,0:T(8,128)(2,1)S(1)}, bf16[784,128]{1,0:T(8,128)(2,1)S(1)}, u32[]{:S(2)}, u32[]{:S(2)}) %collective-permute-start.4) | collective-permute-done | bytes 200736 | tf_op jit(solution)/shard_map/ppermute | solution.py:429
  23.9 0.3 %collective-permute-start.5 = (bf16[768,128]{1,0:T(8,128)(2,1)S(1)}, bf16[768,128]{1,0:T(8,128)(2,1)S(1)}, u32[]{:S(2)}, u32[]{:S(2)}) collective-permute-start(bf16[768,128]{1,0:T(8,128)(2,1)S(1)} %last_step.1.sums), channel_id=1, source_target_pairs={{0,1},{1,0},{2,3},{3,2},{4,5},{5,4},{6,7},{7,6},{8,9},{9,8},{10,11... | collective-permute-start | bytes 589832 | tf_op jit(solution)/shard_map/ppermute | solution.py:460
  24.2 0.0 collective-permute-done.6.arrived
  24.2 1.3 %finish_own.1.refs_0_ = bf16[768,1536]{1,0:T(8,128)(2,1)} custom-call(s32[7,17]{1,0:T(8,128)S(4)} %get-tuple-element.31.table, bf16[768,128]{1,0:T(8,128)(2,1)S(1)} %last_step.1.sums, bf16[2,768,768]{2,1,0:T(8,128)(2,1)S(1)} %ladder.3.near, bf16[2,768,768]{2,1,0:T(8,128)(2,1)S(1)} %collective-permute-done.6.arrived, ...), custom_call_target="tpu_custom_call" | custom-call | flops 1000000000 | bytes 1 | tf_op jit(solution)/shard_map/finish_own/pallas_call | solution.py:397
  25.5 0.0 collective-permute-done.5.sums
  25.5 1.3 %finish_other.1 = bf16[768,1536]{1,0:T(8,128)(2,1)} custom-call(s32[7,17]{1,0:T(8,128)S(4)} %get-tuple-element.31.table, bf16[768,128]{1,0:T(8,128)(2,1)S(1)} %collective-permute-done.5.sums, bf16[2,768,768]{2,1,0:T(8,128)(2,1)S(1)} %ladder.3.near, bf16[2,768,768]{2,1,0:T(8,128)(2,1)S(1)} %collective-permute-done.6.arrived, ...), custom_call_target="tpu_custom_call", output_to_operand_aliasing={{}: (5, {})} | custom-call | flops 1000000000 | bytes 1 | tf_op jit(solution)/shard_map/finish_other/pallas_call | solution.py:397
  (1 shorter events, 0.0 us)
Async XLA Ops:
  0.0 2.6 %collective-permute-start = (bf16[8,128,128]{2,1,0:T(8,128)(2,1)}, bf16[8,128,128]{2,1,0:T(8,128)(2,1)S(1)}, u32[]{:S(2)}, u32[]{:S(2)}) collective-permute-start(bf16[8,128,128]{2,1,0:T(8,128)(2,1)} %bitcast.7), channel_id=1, source_target_pairs={{0,1},{1,0},{2,3},{3,2},{4,5},{5,4},{6,7},{7,6},{8,9},{9,8},{10,11... | collective-permute-start | bytes 786440 | tf_op jit(solution)/shard_map/ppermute | solution.py:420
  0.5 6.1 %copy-start = (s32[1,2]{1,0:T(1,128)S(1)}, s32[1,2]{1,0:T(1,128)}, u32[]{:S(2)}) copy-start(s32[1,2]{1,0:T(1,128)} %orbs.1) | copy-start | bytes 28
  2.9 8.7 %collective-permute-start.2 = (bf16[784,128]{1,0:T(8,128)(2,1)S(1)}, bf16[784,128]{1,0:T(8,128)(2,1)S(1)}, u32[]{:S(2)}, u32[]{:S(2)}) collective-permute-start(bf16[784,128]{1,0:T(8,128)(2,1)S(1)} %intermediate.1.mine), channel_id=1, source_target_pairs={{0,8},{1,5},{2,10},{3,7},{4,12},{5,1},{6,14},{7,3},{8,0},{9,13},{1... | collective-permute-start | bytes 602120 | tf_op jit(solution)/shard_map/ppermute | solution.py:429
  6.6 5.0 %collective-permute-start.1 = (s32[1,2]{1,0:T(1,128)S(1)}, s32[1,2]{1,0:T(1,128)S(1)}, u32[]{:S(2)}, u32[]{:S(2)}) collective-permute-start(s32[1,2]{1,0:T(1,128)S(1)} %copy-done), channel_id=1, source_target_pairs={{0,2},{1,3},{2,0},{3,1},{4,6},{5,7},{6,4},{7,5},{8,10},{9,11},{10,... | collective-permute-start | bytes 32 | tf_op jit(solution)/shard_map/ppermute | solution.py:429
  11.7 6.2 %collective-permute-start.3 = (bf16[784,128]{1,0:T(8,128)(2,1)S(1)}, bf16[784,128]{1,0:T(8,128)(2,1)S(1)}, u32[]{:S(2)}, u32[]{:S(2)}) collective-permute-start(bf16[784,128]{1,0:T(8,128)(2,1)S(1)} %get-tuple-element.45), channel_id=1, source_target_pairs={{0,4},{1,3},{2,6},{3,1},{4,0},{5,7},{6,2},{7,5},{8,12},{9,11},{10,... | collective-permute-start | bytes 602120 | tf_op jit(solution)/shard_map/ppermute | solution.py:429
  18.1 5.8 %collective-permute-start.4 = (bf16[784,128]{1,0:T(8,128)(2,1)S(1)}, bf16[784,128]{1,0:T(8,128)(2,1)S(1)}, u32[]{:S(2)}, u32[]{:S(2)}) collective-permute-start(bf16[784,128]{1,0:T(8,128)(2,1)S(1)} %get-tuple-element.52), channel_id=1, source_target_pairs={{0,2},{1,9},{2,0},{3,11},{4,6},{5,13},{6,4},{7,15},{8,10},{9,1},{1... | collective-permute-start | bytes 602120 | tf_op jit(solution)/shard_map/ppermute | solution.py:429
  19.6 4.6 %collective-permute-start.6 = (bf16[2,768,768]{2,1,0:T(8,128)(2,1)S(1)}, bf16[2,768,768]{2,1,0:T(8,128)(2,1)S(1)}, u32[]{:S(2)}, u32[]{:S(2)}) collective-permute-start(bf16[2,768,768]{2,1,0:T(8,128)(2,1)S(1)} %ladder.2), channel_id=1, source_target_pairs={{0,1},{1,0},{2,3},{3,2},{4,5},{5,4},{6,7},{7,6},{8,9},{9,8},{10,11... | collective-permute-start | bytes 7077896 | tf_op jit(solution)/shard_map/ppermute | solution.py:445
  23.9 1.6 %collective-permute-start.5 = (bf16[768,128]{1,0:T(8,128)(2,1)S(1)}, bf16[768,128]{1,0:T(8,128)(2,1)S(1)}, u32[]{:S(2)}, u32[]{:S(2)}) collective-permute-start(bf16[768,128]{1,0:T(8,128)(2,1)S(1)} %last_step.1.sums), channel_id=1, source_target_pairs={{0,1},{1,0},{2,3},{3,2},{4,5},{5,4},{6,7},{7,6},{8,9},{9,8},{10,11... | collective-permute-start | bytes 589832 | tf_op jit(solution)/shard_map/ppermute | solution.py:460

commit v10 on v7

--- a/solution.py
+++ b/solution.py
@@ -346,7 +346,7 @@
                     ).astype(out.dtype)
                     return carry
 
-                lax.fori_loop(0, 2, unit, 0)
+                lax.fori_loop(0, 2, unit, 0, unroll=True)
 
     return ladder_call(body, (2, half, half), [], in_smem(table), left, factor, flops=flops)
 

time: 27.2 us -> 27.2 us (level)
  Pallas kernels: 13.7 us -> 15.1 us
  starting transfers between devices: 9.96 us -> 9.03 us
  waiting for transfers between devices: 3.22 us -> 2.61 us
    pallas_call x2, Pallas kernels: 4.68 us -> 5.68 us  [ladder_call(): pl.pallas_call(body, out_shape=jax.ShapeDtypeStruct(shape, jnp.bfloat16),...]
    ppermute x4, waiting for transfers between devices: 3.22 us -> 2.5 us  [exchange(): return lax.ppermute(value, ('pair', 'virt'), routes)]
    ppermute x4, starting transfers between devices: 9.05 us -> 8.5 us  [exchange(): return lax.ppermute(value, ('pair', 'virt'), routes)]
    pallas_call x1, Pallas kernels: 3.59 us -> 3.99 us  [ladder_build(): pl.pallas_call(body, out_shape=[jax.ShapeDtypeStruct((width, 2 * pairs *...]
    ppermute x1, starting transfers between devices: 0.45 us -> 0.07 us  [shards(): other_sums = lax.ppermute(sums, 'virt', swap)]
  transfers between devices with their start and end apart: 7 -> 7, of which waited for: 2 -> 4; matrix products, arithmetic and copies ran while one was open for 0% -> 0% of each run, Pallas kernels for 43% -> 49%
where the time goes in v10:
time: 27.2 us; the launch traced here: 27 us
  Pallas kernels  15.1 us (56%)
  starting transfers between devices  9.03 us (33%)
  waiting for transfers between devices  2.61 us (10%)
  between operations  0.28 us (1%)
    ppermute x4, starting transfers between devices, exchange(): return lax.ppermute(value, ('pair', 'virt'), routes)  8.5 us
    pallas_call x2, Pallas kernels, ladder_call(): pl.pallas_call(body, out_shape=jax.ShapeDtypeStruct(shape, jnp.bfloat16),...  5.68 us
    pallas_call x1, Pallas kernels, ladder_build(): pl.pallas_call(body, out_shape=[jax.ShapeDtypeStruct((width, 2 * pairs *...  3.99 us
    pallas_call x2, Pallas kernels, finish(): pl.pallas_call(body, out_shape=jax.ShapeDtypeStruct((half, 2 * half), jnp...  2.62 us
    ppermute x4, waiting for transfers between devices, exchange(): return lax.ppermute(value, ('pair', 'virt'), routes)  2.5 us
    pallas_call x1, Pallas kernels, prepare(): pl.pallas_call(body, out_shape=[pltpu.SMEM((7, places), jnp.int32), jax.S...  2.14 us
  transfers between devices with their start and end apart: 7, of which 4 were waited for; matrix products, arithmetic and copies ran while one was open for 0% of the time, Pallas kernels for 49%

profile of v10, /device:TPU:0, one launch (start us, length us, event | category | flops | bytes accessed | tf_op | source)
XLA Modules:
  0.0 27.0 jit_solution(11417489202425907147)
XLA Ops:
  0.0 0.5 %collective-permute-start = (bf16[8,128,128]{2,1,0:T(8,128)(2,1)}, bf16[8,128,128]{2,1,0:T(8,128)(2,1)S(1)}, u32[]{:S(2)}, u32[]{:S(2)}) collective-permute-start(bf16[8,128,128]{2,1,0:T(8,128)(2,1)} %bitcast.7), channel_id=1, source_target_pairs={{0,1},{1,0},{2,3},{3,2},{4,5},{5,4},{6,7},{7,6},{8,9},{9,8},{10,11... | collective-permute-start | bytes 786440 | tf_op jit(solution)/shard_map/ppermute | solution.py:421
  0.5 0.0 copy-start
  0.5 2.1 %prepare.1 = (s32[7,17]{1,0:T(8,128)S(4)}, bf16[8,128,128]{2,1,0:T(8,128)(2,1)S(1)}, bf16[1536,128]{1,0:T(8,128)(2,1)S(1)}, f32[128,768]{1,0:T(8,128)S(1)}) custom-call(s32[2,16]{1,0:T(2,128)} %bitcast.9, s32[1,16]{1,0:T(1,128)} %mask.1, s32[1,2]{1,0:T(1,128)} %orbs.1, s32[1]{0:T(128)} %bitcast.2.place, bf16[8,128,128]{2,1,0:T(8,128)(2,1)} %bitcast.8, ...), custom_call_target="tpu_custom_call" | custom-call | tf_op jit(solution)/shard_map/prepare/pallas_call | solution.py:107
  2.6 0.0 collective-permute-done.other
  2.6 0.3 %intermediate.1 = (bf16[784,128]{1,0:T(8,128)(2,1)S(1)}, bf16[17,128,128]{2,1,0:T(8,128)(2,1)S(1)}) custom-call(s32[7,17]{1,0:T(8,128)S(4)} %get-tuple-element.32.table, bf16[8,128,128]{2,1,0:T(8,128)(2,1)S(1)} %get-tuple-element.33.own, bf16[8,128,128]{2,1,0:T(8,128)(2,1)S(1)} %collective-permute-done.other, ...), custom_call_target="tpu_custom_call" | custom-call | tf_op jit(solution)/shard_map/intermediate/pallas_call | solution.py:145
  2.9 3.7 %collective-permute-start.2 = (bf16[784,128]{1,0:T(8,128)(2,1)S(1)}, bf16[784,128]{1,0:T(8,128)(2,1)S(1)}, u32[]{:S(2)}, u32[]{:S(2)}) collective-permute-start(bf16[784,128]{1,0:T(8,128)(2,1)S(1)} %get-tuple-element.39.mine), channel_id=1, source_target_pairs={{0,8},{1,5},{2,10},{3,7},{4,12},{5,1},{6,14},{7,3},{8,0},{9,13},{1... | collective-permute-start | bytes 602120 | tf_op jit(solution)/shard_map/ppermute | solution.py:430
  6.6 0.0 copy-done
  6.6 1.5 %collective-permute-start.1 = (s32[1,2]{1,0:T(1,128)S(1)}, s32[1,2]{1,0:T(1,128)S(1)}, u32[]{:S(2)}, u32[]{:S(2)}) collective-permute-start(s32[1,2]{1,0:T(1,128)S(1)} %copy-done), channel_id=1, source_target_pairs={{0,2},{1,3},{2,0},{3,1},{4,6},{5,7},{6,4},{7,5},{8,10},{9,11},{10,... | collective-permute-start | bytes 32 | tf_op jit(solution)/shard_map/ppermute | solution.py:430
  8.1 4.0 %ladder_build.1 = (bf16[1536,1536]{1,0:T(8,128)(2,1)S(1)}, bf16[1536,1536]{1,0:T(8,128)(2,1)S(1)}) custom-call(s32[7,17]{1,0:T(8,128)S(4)} %get-tuple-element.32.table, bf16[17,128,128]{2,1,0:T(8,128)(2,1)S(1)} %get-tuple-element.40.held, bf16[1536,1536]{1,0:T(8,128)(2,1)} %bitcast.10), custom_call_target="tpu_custom_call" | custom-call | flops 10000000000 | bytes 1 | tf_op jit(solution)/shard_map/ladder_build/pallas_call | solution.py:306
  12.1 0.0 collective-permute-done.2.arrival
  12.1 0.0 collective-permute-done.1.next_orbs
  12.1 0.1 step.2
  12.2 1.9 %collective-permute-start.3 = (bf16[784,128]{1,0:T(8,128)(2,1)S(1)}, bf16[784,128]{1,0:T(8,128)(2,1)S(1)}, u32[]{:S(2)}, u32[]{:S(2)}) collective-permute-start(bf16[784,128]{1,0:T(8,128)(2,1)S(1)} %get-tuple-element.47), channel_id=1, source_target_pairs={{0,4},{1,3},{2,6},{3,1},{4,0},{5,7},{6,2},{7,5},{8,12},{9,11},{10,... | collective-permute-start | bytes 602120 | tf_op jit(solution)/shard_map/ppermute | solution.py:430
  14.2 2.8 %ladder.2 = bf16[2,768,768]{2,1,0:T(8,128)(2,1)S(1)} custom-call(s32[7,17]{1,0:T(8,128)S(4)} %get-tuple-element.32.table, bf16[1536,1536]{1,0:T(8,128)(2,1)S(1)} %get-tuple-element.55.left, bf16[1536,1536]{1,0:T(8,128)(2,1)S(1)} %get-tuple-element.49.factor), custom_call_target="tpu_custom_call" | custom-call | flops 10000000000 | bytes 1 | tf_op jit(solution)/shard_map/ladder/pallas_call | solution.py:355
  17.0 1.0 %collective-permute-done.3.arrival = bf16[784,128]{1,0:T(8,128)(2,1)S(1)} collective-permute-done((bf16[784,128]{1,0:T(8,128)(2,1)S(1)}, bf16[784,128]{1,0:T(8,128)(2,1)S(1)}, u32[]{:S(2)}, u32[]{:S(2)}) %collective-permute-start.3) | collective-permute-done | bytes 200736 | tf_op jit(solution)/shard_map/ppermute | solution.py:430
  18.0 0.2 step.3
  18.2 1.4 %collective-permute-start.4 = (bf16[784,128]{1,0:T(8,128)(2,1)S(1)}, bf16[784,128]{1,0:T(8,128)(2,1)S(1)}, u32[]{:S(2)}, u32[]{:S(2)}) collective-permute-start(bf16[784,128]{1,0:T(8,128)(2,1)S(1)} %get-tuple-element.54), channel_id=1, source_target_pairs={{0,2},{1,9},{2,0},{3,11},{4,6},{5,13},{6,4},{7,15},{8,10},{9,1},{1... | collective-permute-start | bytes 602120 | tf_op jit(solution)/shard_map/ppermute | solution.py:430
  19.6 0.0 collective-permute-start.6
  19.6 2.9 %ladder.3.near = bf16[2,768,768]{2,1,0:T(8,128)(2,1)S(1)} custom-call(s32[7,17]{1,0:T(8,128)S(4)} %get-tuple-element.32.table, bf16[1536,1536]{1,0:T(8,128)(2,1)S(1)} %get-tuple-element.55.left, bf16[1536,1536]{1,0:T(8,128)(2,1)S(1)} %get-tuple-element.49.factor), custom_call_target="tpu_custom_call" | custom-call | flops 40000000000 | bytes 1 | tf_op jit(solution)/shard_map/ladder/pallas_call | solution.py:355
  22.5 1.5 %collective-permute-done.4.arrival = bf16[784,128]{1,0:T(8,128)(2,1)S(1)} collective-permute-done((bf16[784,128]{1,0:T(8,128)(2,1)S(1)}, bf16[784,128]{1,0:T(8,128)(2,1)S(1)}, u32[]{:S(2)}, u32[]{:S(2)}) %collective-permute-start.4) | collective-permute-done | bytes 200736 | tf_op jit(solution)/shard_map/ppermute | solution.py:430
  24.0 0.1 collective-permute-start.5
  24.1 0.1 collective-permute-done.6.arrived
  24.1 1.3 %finish_own.1.refs_0_ = bf16[768,1536]{1,0:T(8,128)(2,1)} custom-call(s32[7,17]{1,0:T(8,128)S(4)} %get-tuple-element.32.table, bf16[768,128]{1,0:T(8,128)(2,1)S(1)} %last_step.1.sums, bf16[2,768,768]{2,1,0:T(8,128)(2,1)S(1)} %ladder.3.near, bf16[2,768,768]{2,1,0:T(8,128)(2,1)S(1)} %collective-permute-done.6.arrived, ...), custom_call_target="tpu_custom_call" | custom-call | flops 1000000000 | bytes 1 | tf_op jit(solution)/shard_map/finish_own/pallas_call | solution.py:398
  25.5 0.1 collective-permute-done.5.sums
  25.5 1.3 %finish_other.1 = bf16[768,1536]{1,0:T(8,128)(2,1)} custom-call(s32[7,17]{1,0:T(8,128)S(4)} %get-tuple-element.32.table, bf16[768,128]{1,0:T(8,128)(2,1)S(1)} %collective-permute-done.5.sums, bf16[2,768,768]{2,1,0:T(8,128)(2,1)S(1)} %ladder.3.near, bf16[2,768,768]{2,1,0:T(8,128)(2,1)S(1)} %collective-permute-done.6.arrived, ...), custom_call_target="tpu_custom_call", output_to_operand_aliasing={{}: (5, {})} | custom-call | flops 1000000000 | bytes 1 | tf_op jit(solution)/shard_map/finish_other/pallas_call | solution.py:398
  (1 shorter events, 0.0 us)
Async XLA Ops:
  0.0 2.6 %collective-permute-start = (bf16[8,128,128]{2,1,0:T(8,128)(2,1)}, bf16[8,128,128]{2,1,0:T(8,128)(2,1)S(1)}, u32[]{:S(2)}, u32[]{:S(2)}) collective-permute-start(bf16[8,128,128]{2,1,0:T(8,128)(2,1)} %bitcast.7), channel_id=1, source_target_pairs={{0,1},{1,0},{2,3},{3,2},{4,5},{5,4},{6,7},{7,6},{8,9},{9,8},{10,11... | collective-permute-start | bytes 786440 | tf_op jit(solution)/shard_map/ppermute | solution.py:421
  0.5 6.1 %copy-start = (s32[1,2]{1,0:T(1,128)S(1)}, s32[1,2]{1,0:T(1,128)}, u32[]{:S(2)}) copy-start(s32[1,2]{1,0:T(1,128)} %orbs.1) | copy-start | bytes 28
  2.9 9.2 %collective-permute-start.2 = (bf16[784,128]{1,0:T(8,128)(2,1)S(1)}, bf16[784,128]{1,0:T(8,128)(2,1)S(1)}, u32[]{:S(2)}, u32[]{:S(2)}) collective-permute-start(bf16[784,128]{1,0:T(8,128)(2,1)S(1)} %get-tuple-element.39.mine), channel_id=1, source_target_pairs={{0,8},{1,5},{2,10},{3,7},{4,12},{5,1},{6,14},{7,3},{8,0},{9,13},{1... | collective-permute-start | bytes 602120 | tf_op jit(solution)/shard_map/ppermute | solution.py:430
  6.6 5.5 %collective-permute-start.1 = (s32[1,2]{1,0:T(1,128)S(1)}, s32[1,2]{1,0:T(1,128)S(1)}, u32[]{:S(2)}, u32[]{:S(2)}) collective-permute-start(s32[1,2]{1,0:T(1,128)S(1)} %copy-done), channel_id=1, source_target_pairs={{0,2},{1,3},{2,0},{3,1},{4,6},{5,7},{6,4},{7,5},{8,10},{9,11},{10,... | collective-permute-start | bytes 32 | tf_op jit(solution)/shard_map/ppermute | solution.py:430
  12.2 5.8 %collective-permute-start.3 = (bf16[784,128]{1,0:T(8,128)(2,1)S(1)}, bf16[784,128]{1,0:T(8,128)(2,1)S(1)}, u32[]{:S(2)}, u32[]{:S(2)}) collective-permute-start(bf16[784,128]{1,0:T(8,128)(2,1)S(1)} %get-tuple-element.47), channel_id=1, source_target_pairs={{0,4},{1,3},{2,6},{3,1},{4,0},{5,7},{6,2},{7,5},{8,12},{9,11},{10,... | collective-permute-start | bytes 602120 | tf_op jit(solution)/shard_map/ppermute | solution.py:430
  18.2 5.8 %collective-permute-start.4 = (bf16[784,128]{1,0:T(8,128)(2,1)S(1)}, bf16[784,128]{1,0:T(8,128)(2,1)S(1)}, u32[]{:S(2)}, u32[]{:S(2)}) collective-permute-start(bf16[784,128]{1,0:T(8,128)(2,1)S(1)} %get-tuple-element.54), channel_id=1, source_target_pairs={{0,2},{1,9},{2,0},{3,11},{4,6},{5,13},{6,4},{7,15},{8,10},{9,1},{1... | collective-permute-start | bytes 602120 | tf_op jit(solution)/shard_map/ppermute | solution.py:430
  19.6 4.5 %collective-permute-start.6 = (bf16[2,768,768]{2,1,0:T(8,128)(2,1)S(1)}, bf16[2,768,768]{2,1,0:T(8,128)(2,1)S(1)}, u32[]{:S(2)}, u32[]{:S(2)}) collective-permute-start(bf16[2,768,768]{2,1,0:T(8,128)(2,1)S(1)} %ladder.2), channel_id=1, source_target_pairs={{0,1},{1,0},{2,3},{3,2},{4,5},{5,4},{6,7},{7,6},{8,9},{9,8},{10,11... | collective-permute-start | bytes 7077896 | tf_op jit(solution)/shard_map/ppermute | solution.py:446
  24.0 1.5 %collective-permute-start.5 = (bf16[768,128]{1,0:T(8,128)(2,1)S(1)}, bf16[768,128]{1,0:T(8,128)(2,1)S(1)}, u32[]{:S(2)}, u32[]{:S(2)}) collective-permute-start(bf16[768,128]{1,0:T(8,128)(2,1)S(1)} %last_step.1.sums), channel_id=1, source_target_pairs={{0,1},{1,0},{2,3},{3,2},{4,5},{5,4},{6,7},{7,6},{8,9},{9,8},{10,11... | collective-permute-start | bytes 589832 | tf_op jit(solution)/shard_map/ppermute | solution.py:461
